TPU v7x, 32 devices: a whole 2x2x4 slice. The times are simulated.
32 devices in a mesh: dp: 4 (over z), tensor: 4 (over y, core), ctx: 2 (over x).
Axes of the slice: x: 2, y: 2, z: 4, core: 2. Of those that a mesh axis runs over, the one named last changes fastest.
Arguments:
- tokens: bfloat16 [2048, 2048], P('dp', ('tensor', 'ctx')), may hold values from -6 to 6
- targets: bfloat16 [2048, 2048], P('dp', ('tensor', 'ctx')), may hold values from -6 to 6
- ln_gain: bfloat16 [2048], P(('tensor', 'ctx')), may hold values from 0.5 to 1.5
- up_weight: bfloat16 [2048, 2, 4, 1024], P('dp', None, 'ctx', 'tensor'), may hold values from -0.125 to 0.125
- conv_weight: bfloat16 [4, 4, 1024], P(None, 'ctx', 'tensor'), may hold values from -3 to 3
- conv_bias: bfloat16 [4, 1024], P('ctx', 'tensor'), may hold values from -3 to 3
- qkv_weight: bfloat16 [3, 4, 4, 1024], P(None, None, 'ctx', 'tensor'), may hold values from -3 to 3
- gate_weight: bfloat16 [2, 4, 3, 4, 1024], P(None, None, None, 'ctx', 'tensor'), may hold values from -0.0546875 to 0.0546875
- gate_bias: bfloat16 [2, 4], replicated, may hold values from -3 to 5, as said below
- group_gain: bfloat16 [4, 1024], P('ctx', 'tensor'), may hold values from 0.099609375 to 1.8984375
- skip_gain: bfloat16 [4, 1024], P('ctx', 'tensor'), may hold values from 0.099609375 to 1.8984375
- down_weight: bfloat16 [4, 1024, 2048], P('ctx', 'tensor', 'dp'), may hold values from -0.1875 to 0.1875
- lengths: int32 [4, 3], replicated, may hold values from 64 to 256, as said below
- permutation: int32 [2048], replicated, may hold values from 0 to 2047, as said below
- valid: int32 [2048], P('dp'), may hold values from 0 to 1, as said below
Outputs:
- output: bfloat16 [2048, 2048], P('dp', ('tensor', 'ctx'))
- loss: float32 [], replicated
- grad_input: bfloat16 [2048, 2048], P('dp', ('tensor', 'ctx'))
- grad_ln_gain: float32 [2048], P(('tensor', 'ctx'))
- grad_up_weight: float32 [2048, 2, 4, 1024], P('dp', None, 'ctx', 'tensor')
- grad_conv_weight: float32 [4, 4, 1024], P(None, 'ctx', 'tensor')
- grad_conv_bias: float32 [4, 1024], P('ctx', 'tensor')
- grad_qkv_weight: float32 [3, 4, 4, 1024], P(None, None, 'ctx', 'tensor')
- grad_gate_weight: float32 [2, 4, 3, 4, 1024], P(None, None, None, 'ctx', 'tensor')
- grad_gate_bias: float32 [2, 4], replicated
- grad_group_gain: float32 [4, 1024], P('ctx', 'tensor')
- grad_skip_gain: float32 [4, 1024], P('ctx', 'tensor')
- grad_down_weight: float32 [4, 1024, 2048], P('ctx', 'tensor', 'dp')
Inputs may be any that keep to these rules, and one draw needn't show every extreme that they name: `lengths`: in each pack one sequence has exactly 256 tokens and the others between one eighth and one quarter of 512. A permutation of the 2048 slots; the 512 tokens that one index of dp holds in the loader's order go to every pack, exactly 128 to each. `valid`: A 0 or 1 for each token. `gate_bias`: input gate biases (first index 0) lie from -3 to 0, forget gate biases from 1 to 5.
All inputs are finite; a program needn't handle non-finite values.
Results may differ from a plain program's by a relative error of at most 0.014.
The roundings to bfloat16 on the way count: a program that leaves them out, or rounds other values in their place, can miss the bound.
Values may be sent and summed in bfloat16 or wider, within the bound.
A program may use at most 192 MiB of HBM per device.

v0:
```python
import jax
import jax.numpy as jnp
from jax import lax
from jax.sharding import PartitionSpec as P

SPAN = 256


NEG_FILL = -1e30
EPSILON = 1e-05
HIGHEST = lax.Precision.HIGHEST


def low(v):
    rounded = v.astype(jnp.bfloat16).astype(jnp.float32)
    return v + lax.stop_gradient(rounded - v)


def convolve(branch, conv_taps, conv_shift, segment):
    result = conv_shift[None] + conv_taps[0][None] * branch
    for offset in range(1, conv_taps.shape[0]):
        shifted = jnp.concatenate(
            [jnp.zeros((offset,) + branch.shape[1:], jnp.float32), branch[:-offset]], axis=0
        )
        shifted_ids = jnp.concatenate(
            [jnp.full((offset,), -1, jnp.int32), segment[:-offset]], axis=0
        )
        result = result + jnp.where(
            (shifted_ids == segment)[:, None, None], conv_taps[offset][None] * shifted, 0.0
        )
    return result


def blockwise(values_in, block_map):
    row_count, head_count, channels = values_in.shape
    block_width = block_map.shape[0]
    split_values = values_in.reshape(row_count, head_count, channels // block_width, block_width)
    split_map = block_map.reshape(block_width, head_count, channels // block_width, block_width)
    return jnp.einsum("thbi,ihbj->thbj", split_values, split_map, precision=HIGHEST).reshape(
        row_count, head_count, channels
    )


def front(up_values, conv_taps, conv_shift, mix_maps, segment):
    branch = up_values[:, 0]
    gate_branch = up_values[:, 1]
    convolved = convolve(branch, conv_taps, conv_shift, segment)
    activated = convolved * jax.nn.sigmoid(convolved)
    queries = low(blockwise(activated, mix_maps[0]))
    keys_out = low(blockwise(activated, mix_maps[1]))
    values_out = low(blockwise(branch, mix_maps[2]))
    return (jnp.stack([queries, keys_out, values_out], axis=1), activated, gate_branch)


def cell_block(running, block):
    memory, normalizer, stabilizer, last_id = running
    queries, keys_in, values_in, in_gate, log_forget, segment = block
    length = queries.shape[0]
    score_scale = queries.shape[2] ** (-0.5)
    rising = jnp.cumsum(log_forget, axis=0).T
    gate_in = in_gate.T
    position = jnp.arange(length)
    allowed = (segment[:, None] == segment[None, :]) & (position[:, None] >= position[None, :])
    logits = jnp.where(
        allowed[None], rising[:, :, None] - rising[:, None, :] + gate_in[:, None, :], NEG_FILL
    )
    carried = jnp.where((segment == last_id)[None, :], rising + stabilizer[:, None], NEG_FILL)
    row_top = jnp.maximum(jnp.max(logits, axis=2), carried)
    scores = jnp.einsum("thd,shd->hts", queries, keys_in, precision=HIGHEST)
    weights = scores * score_scale * jnp.exp(logits - row_top[:, :, None])
    decay_in = jnp.exp(carried - row_top)
    through = jnp.einsum("thd,hdv->htv", queries, memory, precision=HIGHEST)
    inner_sum = jnp.einsum("hts,shv->htv", weights, values_in, precision=HIGHEST)
    numerator = inner_sum + score_scale * decay_in[:, :, None] * through
    denominator = jnp.sum(weights, axis=2) + score_scale * decay_in * jnp.einsum(
        "thd,hd->ht", queries, normalizer, precision=HIGHEST
    )
    divisor = jnp.maximum(jnp.abs(denominator), jnp.exp(-row_top))
    hidden = numerator / divisor[:, :, None]
    end_id = segment[length - 1]
    block_total = rising[:, length - 1]
    kept_log = jnp.where(last_id == end_id, block_total + stabilizer, NEG_FILL)
    added_log = jnp.where(
        (segment == end_id)[None, :], block_total[:, None] - rising + gate_in, NEG_FILL
    )
    new_stab = jnp.maximum(kept_log, jnp.max(added_log, axis=1))
    kept_weight = jnp.exp(kept_log - new_stab)
    added_weight = jnp.exp(added_log - new_stab[:, None])
    weighted_keys = keys_in * added_weight.T[:, :, None]
    memory = kept_weight[:, None, None] * memory + jnp.einsum(
        "shd,shv->hdv", weighted_keys, values_in, precision=HIGHEST
    )
    normalizer = kept_weight[:, None] * normalizer + jnp.einsum(
        "shd,hs->hd", keys_in, added_weight, precision=HIGHEST
    )
    return ((memory, normalizer, new_stab, end_id), jnp.transpose(hidden, (1, 0, 2)))


def run_cell(queries, keys_in, values_in, in_gate, log_forget, segment):
    row_count, head_count, key_depth = queries.shape
    value_depth = values_in.shape[2]
    block_count = row_count // SPAN
    blocks = (
        queries.reshape(block_count, SPAN, head_count, key_depth),
        keys_in.reshape(block_count, SPAN, head_count, key_depth),
        values_in.reshape(block_count, SPAN, head_count, value_depth),
        in_gate.reshape(block_count, SPAN, head_count),
        log_forget.reshape(block_count, SPAN, head_count),
        segment.reshape(block_count, SPAN),
    )
    initial = (
        jnp.zeros((head_count, key_depth, value_depth), jnp.float32),
        jnp.zeros((head_count, key_depth), jnp.float32),
        jnp.full((head_count,), NEG_FILL, jnp.float32),
        jnp.int32(-1),
    )
    final_state, hidden = lax.scan(jax.checkpoint(cell_block), initial, blocks)
    return hidden.reshape(row_count, head_count, value_depth)


def regroup(values_in, take_rows, put_rows):
    return lax.all_to_all(values_in[take_rows], "dp", split_axis=0, concat_axis=0, tiled=True)[
        put_rows
    ]


def row_sums(values_in):
    return lax.psum(values_in, ("tensor", "ctx"))


def spread_rows(values_in):
    return lax.all_gather(values_in, ("tensor", "ctx"), axis=1, tiled=True)


def fold_columns(values_in):
    return lax.psum_scatter(values_in, ("tensor", "ctx"), scatter_dimension=1, tiled=True)


def fetch_weights(up_shard, down_shard):
    return (
        lax.all_gather(up_shard, "dp", axis=0, tiled=True),
        lax.all_gather(down_shard, "dp", axis=2, tiled=True),
    )


def shards(
    tokens,
    targets,
    ln_gain,
    up_weight,
    conv_weight,
    conv_bias,
    qkv_weight,
    gate_weight,
    gate_bias,
    group_gain,
    skip_gain,
    down_weight,
    lengths,
    permutation,
    valid,
):
    group_rows = tokens.shape[0]
    dp_count = lax.axis_size("dp")
    spread_count = lax.axis_size("tensor") * lax.axis_size("ctx")
    model_width = tokens.shape[1] * spread_count
    dp_index = lax.axis_index("dp")
    ctx_index = lax.axis_index("ctx")
    local_heads = up_weight.shape[2]
    all_heads = gate_weight.shape[1]
    head_width = up_weight.shape[3] * lax.axis_size("tensor")
    all_rows = group_rows * dp_count
    bucket_rows = group_rows // dp_count
    inverse = (
        jnp.zeros((all_rows,), jnp.int32).at[permutation].set(jnp.arange(all_rows, dtype=jnp.int32))
    )
    arrival = inverse.reshape(dp_count, group_rows)
    from_here = arrival // group_rows == dp_index
    ranking = jnp.cumsum(from_here.astype(jnp.int32), axis=1) - 1
    bucket_slot = jnp.where(
        from_here,
        jnp.arange(dp_count, dtype=jnp.int32)[:, None] * bucket_rows + ranking,
        group_rows,
    )
    send_rows = (
        jnp.zeros((group_rows,), jnp.int32)
        .at[bucket_slot.reshape(-1)]
        .set((arrival - dp_index * group_rows).reshape(-1), mode="drop")
    )
    own_sources = lax.dynamic_slice_in_dim(inverse, dp_index * group_rows, group_rows) // group_rows
    source_hits = (own_sources[:, None] == jnp.arange(dp_count, dtype=jnp.int32)[None, :]).astype(
        jnp.int32
    )
    arrival_rank = jnp.sum((jnp.cumsum(source_hits, axis=0) - 1) * source_hits, axis=1)
    recv_rows = own_sources * bucket_rows + arrival_rank
    back_rows = (
        jnp.zeros((group_rows,), jnp.int32)
        .at[recv_rows]
        .set(jnp.arange(group_rows, dtype=jnp.int32))
    )
    home_rows = (
        jnp.zeros((group_rows,), jnp.int32)
        .at[send_rows]
        .set(jnp.arange(group_rows, dtype=jnp.int32))
    )
    ends_all = jnp.cumsum(lengths, axis=1)
    places = jnp.arange(group_rows, dtype=jnp.int32)
    segment_all = jnp.sum((places[None, :, None] >= ends_all[:, None, :]).astype(jnp.int32), axis=2)
    segment = lax.dynamic_index_in_dim(segment_all, dp_index, 0, keepdims=False)
    open_slots = (segment_all < lengths.shape[1]).reshape(-1)
    local_perm = lax.dynamic_slice_in_dim(permutation, dp_index * group_rows, group_rows)
    keep = valid.astype(jnp.float32) * open_slots[local_perm].astype(jnp.float32)
    work_tokens = regroup(tokens, send_rows, recv_rows)
    x_float = work_tokens.astype(jnp.float32)
    moments = row_sums(
        jnp.stack([jnp.sum(x_float, axis=1), jnp.sum(x_float * x_float, axis=1)], axis=1)
    )
    row_mean = moments[:, 0:1] / model_width
    row_rstd = lax.rsqrt(moments[:, 1:2] / model_width - row_mean * row_mean + EPSILON)
    x_hat = (x_float - row_mean) * row_rstd
    ln_float = ln_gain.astype(jnp.float32)
    normed = (x_hat * ln_float[None]).astype(jnp.bfloat16)
    up_full, down_full = fetch_weights(up_weight, down_weight)
    up_matrix = up_full.reshape(model_width, -1)
    down_matrix = down_full.reshape(-1, model_width)
    normed_full = spread_rows(normed)
    up_values = jnp.dot(normed_full, up_matrix, preferred_element_type=jnp.float32).astype(
        jnp.bfloat16
    )
    up_values = up_values.reshape(group_rows, 2, local_heads, up_weight.shape[3])

    def front_here(up_in, conv_in, shift_in, mix_in):
        return front(up_in, conv_in, shift_in, mix_in, segment)

    (projected, activated, gate_branch), front_pull = jax.vjp(
        front_here,
        up_values.astype(jnp.float32),
        conv_weight.astype(jnp.float32),
        conv_bias.astype(jnp.float32),
        qkv_weight.astype(jnp.float32),
    )
    projected_low = projected.astype(jnp.bfloat16)
    gate_part = jnp.einsum(
        "tshd,goshd->tgo", projected_low, gate_weight, preferred_element_type=jnp.float32
    )
    gate_pre = row_sums(gate_part) + gate_bias.astype(jnp.float32)[None]
    own_pre = lax.dynamic_slice_in_dim(gate_pre, ctx_index * local_heads, local_heads, 2)
    query_full, key_full = (
        lax.all_gather(projected_low[:, 0], "tensor", axis=2, tiled=True),
        lax.all_gather(projected_low[:, 1], "tensor", axis=2, tiled=True),
    )

    def cell_here(queries, keys_in, values_in, in_gate, forget_pre):
        return run_cell(
            queries, keys_in, values_in, in_gate, jax.nn.log_sigmoid(forget_pre), segment
        )

    hidden, cell_pull = jax.vjp(
        cell_here,
        query_full.astype(jnp.float32),
        key_full.astype(jnp.float32),
        projected[:, 2],
        own_pre[:, 0],
        own_pre[:, 1],
    )
    local_moments = jnp.stack([jnp.sum(hidden, axis=2), jnp.sum(hidden * hidden, axis=2)], axis=2)
    empty_moments = jnp.zeros((group_rows, all_heads, 2), jnp.float32)
    placed = lax.dynamic_update_slice_in_dim(
        empty_moments, local_moments, ctx_index * local_heads, 1
    )
    head_moments = lax.dynamic_slice_in_dim(
        row_sums(placed), ctx_index * local_heads, local_heads, 1
    )

    def finish(hidden_in, moments_in, gain_in, skip_in, act_in, branch_in):
        head_mean = moments_in[:, :, 0:1] / head_width
        head_rstd = lax.rsqrt(moments_in[:, :, 1:2] / head_width - head_mean * head_mean + EPSILON)
        normal_h = (hidden_in - head_mean) * head_rstd * gain_in[None]
        return low((normal_h + skip_in[None] * act_in) * (branch_in * jax.nn.sigmoid(branch_in)))

    gated, finish_pull = jax.vjp(
        finish,
        hidden,
        head_moments,
        group_gain.astype(jnp.float32),
        skip_gain.astype(jnp.float32),
        activated,
        gate_branch,
    )
    gated_low = gated.astype(jnp.bfloat16).reshape(group_rows, -1)
    down_part = jnp.dot(gated_low, down_matrix, preferred_element_type=jnp.float32)
    output_work = (x_float + fold_columns(down_part)).astype(jnp.bfloat16)
    output = regroup(output_work, back_rows, home_rows)
    difference = output.astype(jnp.float32) - targets.astype(jnp.float32)
    loss_sum, valid_count = lax.psum(
        (
            jnp.sum(keep * 0.5 * jnp.sum(difference * difference, axis=1)),
            jnp.sum(keep) / spread_count,
        ),
        ("dp", "tensor", "ctx"),
    )
    loss = loss_sum / valid_count
    seed_rows = (all_rows / valid_count * keep[:, None] * difference).astype(jnp.bfloat16)
    grad_work = regroup(seed_rows, send_rows, recv_rows)
    grad_full = spread_rows(grad_work)
    up_full, down_full = fetch_weights(up_weight, down_weight)
    up_matrix = up_full.reshape(model_width, -1)
    down_matrix = down_full.reshape(-1, model_width)
    grad_gated = jnp.einsum("td,cd->tc", grad_full, down_matrix, preferred_element_type=jnp.float32)
    grad_down = jnp.einsum("tc,td->cd", gated_low, grad_full, preferred_element_type=jnp.float32)
    grad_down = grad_down.reshape(down_weight.shape[0], down_weight.shape[1], model_width)
    grad_hidden, grad_moments, grad_group, grad_skip, grad_act, grad_branch = finish_pull(
        grad_gated.reshape(gated.shape)
    )
    moment_grads = row_sums(
        lax.dynamic_update_slice_in_dim(empty_moments, grad_moments, ctx_index * local_heads, 1)
    )
    own_moment_grads = lax.dynamic_slice_in_dim(
        moment_grads, ctx_index * local_heads, local_heads, 1
    )
    grad_hidden = (
        grad_hidden + own_moment_grads[:, :, 0:1] + 2.0 * hidden * own_moment_grads[:, :, 1:2]
    )
    grad_query, grad_key, grad_value, grad_in_gate, grad_forget = cell_pull(grad_hidden)
    local_query, local_key = (
        lax.psum_scatter(grad_query, "tensor", scatter_dimension=2, tiled=True),
        lax.psum_scatter(grad_key, "tensor", scatter_dimension=2, tiled=True),
    )
    empty_pre = jnp.zeros((group_rows, 2, all_heads), jnp.float32)
    pre_grads = row_sums(
        lax.dynamic_update_slice_in_dim(
            empty_pre, jnp.stack([grad_in_gate, grad_forget], axis=1), ctx_index * local_heads, 2
        )
    )
    grad_gate_bias = jnp.sum(pre_grads, axis=0)
    grad_projected = jnp.einsum(
        "tgo,goshd->tshd", pre_grads, gate_weight.astype(jnp.float32), precision=HIGHEST
    )
    grad_projected = grad_projected + jnp.stack([local_query, local_key, grad_value], axis=1)
    grad_gate_weight = jnp.einsum("tshd,tgo->goshd", projected, pre_grads, precision=HIGHEST)
    grad_up_in, grad_conv_w, grad_conv_b, grad_mix = front_pull(
        (grad_projected, grad_act, grad_branch)
    )
    grad_up_low = grad_up_in.astype(jnp.bfloat16).reshape(group_rows, -1)
    grad_up = jnp.einsum(
        "td,tc->dc", normed_full, grad_up_low, preferred_element_type=jnp.float32
    ).reshape(up_full.shape)
    grad_normed = fold_columns(
        jnp.einsum("tc,dc->td", grad_up_low, up_matrix, preferred_element_type=jnp.float32)
    )
    grad_scaled = grad_normed * ln_float[None]
    grad_ln_part = jnp.sum(grad_normed * x_hat, axis=0)
    line_sums = row_sums(
        jnp.stack([jnp.sum(grad_scaled, axis=1), jnp.sum(grad_scaled * x_hat, axis=1)], axis=1)
    )
    grad_x = row_rstd * (
        grad_scaled - line_sums[:, 0:1] / model_width - x_hat * line_sums[:, 1:2] / model_width
    )
    grad_tokens = regroup(
        (grad_work.astype(jnp.float32) + grad_x).astype(jnp.bfloat16), back_rows, home_rows
    )
    up_owned, down_owned = (
        lax.psum_scatter(grad_up, "dp", scatter_dimension=0, tiled=True),
        lax.psum_scatter(grad_down, "dp", scatter_dimension=2, tiled=True),
    )
    summed = lax.psum(
        (
            grad_ln_part,
            grad_conv_w,
            grad_conv_b,
            grad_mix,
            grad_gate_weight,
            grad_gate_bias,
            grad_group,
            grad_skip,
        ),
        "dp",
    )
    return (
        output,
        loss,
        grad_tokens,
        summed[0],
        up_owned,
        summed[1],
        summed[2],
        summed[3],
        summed[4],
        summed[5],
        summed[6],
        summed[7],
        down_owned,
    )


def solution(mesh):
    return jax.shard_map(
        shards,
        mesh=mesh,
        in_specs=(
            P("dp", ("tensor", "ctx")),
            P("dp", ("tensor", "ctx")),
            P(("tensor", "ctx")),
            P("dp", None, "ctx", "tensor"),
            P(None, "ctx", "tensor"),
            P("ctx", "tensor"),
            P(None, None, "ctx", "tensor"),
            P(None, None, None, "ctx", "tensor"),
            P(),
            P("ctx", "tensor"),
            P("ctx", "tensor"),
            P("ctx", "tensor", "dp"),
            P(),
            P(),
            P("dp"),
        ),
        out_specs=(
            P("dp", ("tensor", "ctx")),
            P(),
            P("dp", ("tensor", "ctx")),
            P(("tensor", "ctx")),
            P("dp", None, "ctx", "tensor"),
            P(None, "ctx", "tensor"),
            P("ctx", "tensor"),
            P(None, None, "ctx", "tensor"),
            P(None, None, None, "ctx", "tensor"),
            P(),
            P("ctx", "tensor"),
            P("ctx", "tensor"),
            P("ctx", "tensor", "dp"),
        ),
        check_vma=False,
    )
```

profile of v0, /device:TPU:0, one launch (start us, length us, event | category | flops | bytes accessed | tf_op | source)
XLA Modules:
  0.0 1320.3 jit_solution(15423559793588336140)
XLA Ops:
  9.8 8.0 scatter_custom_fusion
  19.6 8.0 scatter_custom_fusion.1
  30.9 6.5 all-to-all-start
  39.4 13.4 %all-to-all-done = bf16[4,128,256]{2,1,0:T(8,128)(2,1)S(1)} async-done(((bf16[4,128,256]{2,1,0:T(8,128)(2,1)}), bf16[4,128,256]{2,1,0:T(8,128)(2,1)S(1)}, u32[]{:S(2)}, u32[]{:S(2)}) %all-to-all-start) | async-done | bytes 262176 | tf_op jit(solution)/shard_map/all_to_all | solution.py:122
  55.1 16.0 %psum.112 = f32[512,2]{0,1:T(2,128)S(1)} all-reduce(f32[512,2]{0,1:T(2,128)S(1)} %pad_maximum_fusion.1), channel_id=1, replica_groups=mesh['dp'=4,'tensor'=4,'ctx'=2] {'tensor','ctx'}, use_global_device_ids=true, to_apply=%region_9.10 | all-reduce | flops 1024 | bytes 8192 | tf_op jit(solution)/shard_map/psum | solution.py:128
  76.9 22.2 %all-gather.12.cloned.1.call-done = bf16[2048,2,2,256]{3,0,2,1:T(8,128)(2,1)} async-done(((bf16[512,2,2,256]{3,0,2,1:T(8,128)(2,1)}), bf16[2048,2,2,256]{3,0,2,1:T(8,128)(2,1)}) %all-gather.12.cloned.1.call-update) | async-done | bytes 4194320 | tf_op jit(solution)/shard_map/all_gather | solution.py:141
  99.2 6.4 copy.395
  105.6 22.8 %all-gather.10.cloned.1.call-done = bf16[512,2048]{1,0:T(8,128)(2,1)} async-done(((bf16[512,256]{1,0:T(8,128)(2,1)}), bf16[512,2048]{1,0:T(8,128)(2,1)}) %all-gather.10.cloned.1.call-update) | async-done | bytes 2097168 | tf_op jit(solution)/shard_map/all_gather | solution.py:132
  128.4 5.2 convolution_convert_fusion
  174.3 24.2 %psum.113 = f32[512,2,4]{0,2,1:T(4,128)S(1)} all-reduce(f32[512,2,4]{0,2,1:T(4,128)S(1)} %fusion.173), channel_id=1, replica_groups=mesh['dp'=4,'tensor'=4,'ctx'=2] {'tensor','ctx'}, use_global_device_ids=true, to_apply=%region_12.13 | all-reduce | flops 4096 | bytes 32768 | tf_op jit(solution)/shard_map/psum | solution.py:128
  202.7 10.6 all-gather.18.cloned.1.call-done
  217.3 48.0 %while.58 = (s32[]{:T(128)}, f32[2,1024,256]{2,1,0:T(8,128)S(1)}, f32[2,1024]{1,0:T(2,128)S(1)}, f32[2]{0:T(128)S(1)}, s32[]{:T(128)}, /*index=5*/f32[2,256,2,25...) while((s32[]{:T(128)}, f32[2,1024,256]{2,1,0:T(8,128)S(1)}, ...), condition=%wide.region_19.20_spmd.clone, body=%wide.region_13.19_spmd.clone.sunk | while | flops 5252334592 | bytes 102587848 | solution.py:117
  269.4 23.9 %psum.114 = f32[512,4,2]{0,1,2:T(4,128)S(1)} all-reduce(f32[512,4,2]{0,1,2:T(4,128)S(1)} %maximum_dynamic-update-slice_fusion), channel_id=1, replica_groups=mesh['dp'=4,'tensor'=4,'ctx'=2] {'tensor','ctx'}, use_global_device_ids=true, to_apply=%region_22.23 | all-reduce | flops 4096 | bytes 32768 | tf_op jit(solution)/shard_map/psum | solution.py:128
  296.4 4.9 convolution_bitcast_fusion.1
  306.6 46.1 %reduce-scatter.7.cloned.1.call-done = f32[512,256]{1,0:T(8,128)} async-done(((f32[512,2048]{1,0:T(8,128)}), f32[512,256]{1,0:T(8,128)}) %reduce-scatter.7.cloned.1.call-update) | async-done | bytes 524304 | tf_op jit(solution)/shard_map/reduce_scatter | solution.py:136
  357.7 4.7 all-to-all-start.1
  366.0 5.4 all-to-all-done.1
  376.5 38.1 %all-reduce.20 = (f32[]{:T(128)}, f32[]{:T(128)}) all-reduce(f32[]{:T(128)} %get-tuple-element.1025, f32[]{:T(128)S(6)} %div.160), channel_id=1, replica_groups=mesh['dp'=4,'tensor'=4,'ctx'=2] {'dp','tensor','ctx'}, use_global_device_ids=true, to_apply=%region_28.29 | all-reduce | flops 2 | bytes 16 | tf_op jit(solution)/shard_map/psum | solution.py:295
  419.1 11.9 all_to_all.48
  433.7 27.3 %all-gather.20.cloned.1.call-done = bf16[512,2048]{1,0:T(8,128)(2,1)} async-done(((bf16[512,256]{1,0:T(8,128)(2,1)}), bf16[512,2048]{1,0:T(8,128)(2,1)}) %all-gather.20.cloned.1.call-update) | async-done | bytes 2097168 | tf_op jit(solution)/shard_map/all_gather | solution.py:132
  461.0 6.8 multiply_reduce_fusion.4
  467.9 24.1 %psum.117 = f32[512,4,2]{0,1,2:T(4,128)S(1)} all-reduce(f32[512,4,2]{0,1,2:T(4,128)S(1)} %add_dynamic-update-slice_fusion), channel_id=1, replica_groups=mesh['dp'=4,'tensor'=4,'ctx'=2] {'tensor','ctx'}, use_global_device_ids=true, to_apply=%region_33.34 | all-reduce | flops 4096 | bytes 32768 | tf_op jit(solution)/shard_map/psum | solution.py:128
  502.4 356.1 %while.59 = (s32[]{:T(128)}, f32[2,1024,256]{2,1,0:T(8,128)}, f32[2,1024]{1,0:T(2,128)S(1)}, f32[2]{0:T(128)S(1)}, f32[2,256,2,1024]{1,0,3,2:T(2,128)}, /*index=...) while((s32[]{:T(128)}, f32[2,1024,256]{2,1,0:T(8,128)}, ...), condition=%wide.region_55.56_spmd.clone, body=%wide.region_34.55_spmd.clone.sunk | while | flops 14128893952 | bytes 200716656 | solution.py:117
  542.0 5.5 add_bitcast_fusion.15
  547.4 6.2 copy.664
  567.9 5.5 multiply_add_fusion.6
  581.9 11.5 dynamic_update_slice.129
  593.4 42.9 %dynamic_update_slice.128 = f32[2,256,2,1024]{1,0,3,2:T(2,128)} dynamic-update-slice(f32[2,256,2,1024]{1,0,3,2:T(2,128)} %get-tuple-element.1662, f32[1,256,2,1024]{1,0,3,2:T(1,128)} %copy.665, s32[]{:T(128)S(6)} %sub.758, s32[]{:T(128)} %constant.288.clone.1..sunk.1, s32[]{:T(128)} %constant.288.clone.1..sunk.1, s32[]{:T(128)} %constant.288.clone.1..sunk.1) | dynamic-update-slice | bytes 4194308 | tf_op jit(solution)/shard_map/transpose(jvp())/while/body/jit(dynamic_update_index_in_dim)/dynamic_update_slice | solution.py:117
  636.3 42.6 %dynamic_update_slice.127 = f32[2,256,2,1024]{1,0,3,2:T(2,128)} dynamic-update-slice(f32[2,256,2,1024]{1,0,3,2:T(2,128)} %get-tuple-element.1661, f32[1,256,2,1024]{1,0,3,2:T(1,128)S(1)} %copy-done.9, s32[]{:T(128)S(6)} %sub.758, s32[]{:T(128)} %constant.288.clone.1..sunk.1, s32[]{:T(128)} %constant.288.clone.1..sunk.1, s32[]{:T(128)} %constant.288.clone.1..sunk.1) | dynamic-update-slice | bytes 4194308 | tf_op jit(solution)/shard_map/transpose(jvp())/while/body/jit(dynamic_update_index_in_dim)/dynamic_update_slice | solution.py:117
  718.6 5.5 add_bitcast_fusion.15
  724.1 6.4 copy.664
  744.8 5.2 multiply_add_fusion.6
  758.5 11.5 dynamic_update_slice.129
  770.1 42.9 %dynamic_update_slice.128 = f32[2,256,2,1024]{1,0,3,2:T(2,128)} dynamic-update-slice(f32[2,256,2,1024]{1,0,3,2:T(2,128)} %get-tuple-element.1662, f32[1,256,2,1024]{1,0,3,2:T(1,128)} %copy.665, s32[]{:T(128)S(6)} %sub.758, s32[]{:T(128)} %constant.288.clone.1..sunk.1, s32[]{:T(128)} %constant.288.clone.1..sunk.1, s32[]{:T(128)} %constant.288.clone.1..sunk.1) | dynamic-update-slice | bytes 4194308 | tf_op jit(solution)/shard_map/transpose(jvp())/while/body/jit(dynamic_update_index_in_dim)/dynamic_update_slice | solution.py:117
  813.0 42.6 %dynamic_update_slice.127 = f32[2,256,2,1024]{1,0,3,2:T(2,128)} dynamic-update-slice(f32[2,256,2,1024]{1,0,3,2:T(2,128)} %get-tuple-element.1661, f32[1,256,2,1024]{1,0,3,2:T(1,128)S(1)} %copy-done.9, s32[]{:T(128)S(6)} %sub.758, s32[]{:T(128)} %constant.288.clone.1..sunk.1, s32[]{:T(128)} %constant.288.clone.1..sunk.1, s32[]{:T(128)} %constant.288.clone.1..sunk.1) | dynamic-update-slice | bytes 4194308 | tf_op jit(solution)/shard_map/transpose(jvp())/while/body/jit(dynamic_update_index_in_dim)/dynamic_update_slice | solution.py:117
  858.5 6.4 reshape.868
  865.0 6.4 reshape.867
  873.7 24.2 %psum.118 = f32[512,2,4]{0,2,1:T(4,128)S(1)} all-reduce(f32[512,2,4]{0,2,1:T(4,128)S(1)} %maximum_dynamic-update-slice_fusion.1), channel_id=1, replica_groups=mesh['dp'=4,'tensor'=4,'ctx'=2] {'tensor','ctx'}, use_global_device_ids=true, to_apply=%region_56.57 | all-reduce | flops 4096 | bytes 32768 | tf_op jit(solution)/shard_map/psum | solution.py:128
  897.9 11.8 reduce-scatter.11.cloned.1.call-done
  909.8 47.0 %reduce-scatter.9.cloned.1.call-done = f32[512,2,256]{0,2,1:T(8,128)} async-done(((f32[512,2,1024]{0,2,1:T(8,128)}), f32[512,2,256]{0,2,1:T(8,128)}) %reduce-scatter.9.cloned.1.call-update) | async-done | bytes 1048592 | tf_op jit(solution)/shard_map/reduce_scatter | solution.py:326
  1000.4 4.6 fusion.183
  1011.4 30.5 %reduce-scatter.13.cloned.1.call-done = f32[512,256]{1,0:T(8,128)} async-done(((f32[512,2048]{1,0:T(8,128)}), f32[512,256]{1,0:T(8,128)}) %reduce-scatter.13.cloned.1.call-update) | async-done | bytes 524304 | tf_op jit(solution)/shard_map/reduce_scatter | solution.py:136
  1043.9 7.5 fusion.165
  1056.5 13.8 %psum.119 = f32[512,2]{0,1:T(2,128)S(1)} all-reduce(f32[512,2]{0,1:T(2,128)S(1)} %pad_maximum_fusion.2), channel_id=1, replica_groups=mesh['dp'=4,'tensor'=4,'ctx'=2] {'tensor','ctx'}, use_global_device_ids=true, to_apply=%region_62.63 | all-reduce | flops 1024 | bytes 8192 | tf_op jit(solution)/shard_map/psum | solution.py:128
  1082.2 4.7 all-to-all-done.3
  1089.4 138.3 %reduce-scatter.15.cloned.1.call-done = f32[512,2,2,256]{3,0,2,1:T(8,128)} async-done(((f32[2048,2,2,256]{3,0,2,1:T(8,128)}), f32[512,2,2,256]{3,0,2,1:T(8,128)}) %reduce-scatter.15.cloned.1.call-update) | async-done | bytes 2097168 | tf_op jit(solution)/shard_map/reduce_scatter | solution.py:363
  1227.8 4.5 copy.454
  1232.3 76.0 %reduce-scatter.17.cloned.1.call-done = f32[2,256,512]{2,1,0:T(8,128)} async-done(((f32[2,256,2048]{2,1,0:T(8,128)}), f32[2,256,512]{2,1,0:T(8,128)}) %reduce-scatter.17.cloned.1.call-update) | async-done | bytes 1048592 | tf_op jit(solution)/shard_map/reduce_scatter | solution.py:364
  (675 shorter events, 349.9 us)
Async XLA Ops:
  7.2 92.0 %all-gather.12.cloned.1.call-start = ((), (), s32[]{:S(2)}) async-start(), calls=%async_computation.11 | async-start | bytes 5242880 | tf_op jit(solution)/shard_map/all_gather | solution.py:141
  30.9 42.0 %copy-start.106 = (s32[4,3]{1,0:T(4,128)S(1)}, s32[4,3]{1,0:T(4,128)}, u32[]{:S(2)}) copy-start(s32[4,3]{1,0:T(4,128)} %param.31) | copy-start | bytes 148
  30.9 42.3 %copy-start.105 = (bf16[4,2,256]{2,1,0:T(2,128)(2,1)S(1)}, bf16[4,2,256]{2,1,0:T(2,128)(2,1)}, u32[]{:S(2)}) copy-start(bf16[4,2,256]{2,1,0:T(2,128)(2,1)} %param.23) | copy-start | bytes 12292
  30.9 42.3 %copy-start.89 = (bf16[3,4,2,256]{3,2,1,0:T(2,128)(2,1)S(1)}, bf16[3,4,2,256]{3,2,1,0:T(2,128)(2,1)}, u32[]{:S(2)}) copy-start(bf16[3,4,2,256]{3,2,1,0:T(2,128)(2,1)} %param.25) | copy-start | bytes 36868
  30.9 22.0 %all-to-all-start = ((bf16[4,128,256]{2,1,0:T(8,128)(2,1)}), bf16[4,128,256]{2,1,0:T(8,128)(2,1)S(1)}, u32[]{:S(2)}, u32[]{:S(2)}) async-start(bf16[4,128,256]{2,1,0:T(8,128)(2,1)} %bitcast.2), calls=%async_computation | async-start | bytes 524288 | tf_op jit(solution)/shard_map/all_to_all | solution.py:122
  37.3 91.0 %all-gather.10.cloned.1.call-start = ((), (), s32[]{:S(2)}) async-start(), calls=%async_computation.10 | async-start | bytes 2359296 | tf_op jit(solution)/shard_map/all_gather | solution.py:132
  54.8 50.8 %copy-start.34 = (bf16[512,256]{1,0:T(8,128)(2,1)}, bf16[512,256]{1,0:T(8,128)(2,1)S(1)}, u32[]{:S(2)}) copy-start(bf16[512,256]{1,0:T(8,128)(2,1)S(1)} %gather_fusion.1) | copy-start | bytes 786436
  72.1 126.5 %all-gather.16.cloned.1.call-start = ((), (), s32[]{:S(2)}) async-start(), calls=%async_computation.19 | async-start | bytes 2621440 | tf_op jit(solution)/shard_map/all_gather | solution.py:250
  73.4 86.0 %copy-start.56 = (bf16[1,4,2,256]{1,3,2,0:T(8,128)(2,1)}, bf16[1,4,2,256]{1,3,2,0:T(8,128)(2,1)S(1)}, u32[]{:S(2)}) copy-start(bf16[1,4,2,256]{1,3,2,0:T(8,128)(2,1)S(1)} %copy.398) | copy-start | bytes 12292
  73.6 68.4 %copy-start.58 = (bf16[1,4,2,256]{1,3,2,0:T(8,128)(2,1)}, bf16[1,4,2,256]{1,3,2,0:T(8,128)(2,1)S(1)}, u32[]{:S(2)}) copy-start(bf16[1,4,2,256]{1,3,2,0:T(8,128)(2,1)S(1)} %copy.409) | copy-start | bytes 12292
  73.8 82.6 %copy-start.54 = (bf16[1,4,2,256]{1,3,2,0:T(8,128)(2,1)}, bf16[1,4,2,256]{1,3,2,0:T(8,128)(2,1)S(1)}, u32[]{:S(2)}) copy-start(bf16[1,4,2,256]{1,3,2,0:T(8,128)(2,1)S(1)} %copy.403) | copy-start | bytes 12292
  76.9 75.5 %copy-start.70 = (f32[2,256]{1,0:T(2,128)}, f32[2,256]{1,0:T(2,128)S(1)}, u32[]{:S(2)}) copy-start(f32[2,256]{1,0:T(2,128)S(1)} %get-tuple-element.1198) | copy-start | bytes 6148
  76.9 75.5 %copy-start.72 = (f32[2,256]{1,0:T(2,128)}, f32[2,256]{1,0:T(2,128)S(1)}, u32[]{:S(2)}) copy-start(f32[2,256]{1,0:T(2,128)S(1)} %get-tuple-element.1200) | copy-start | bytes 6148
  165.9 47.4 %all-gather.18.cloned.1.call-start = ((), (), s32[]{:S(2)}) async-start(), calls=%async_computation.20 | async-start | bytes 2621440 | tf_op jit(solution)/shard_map/all_gather | solution.py:249
  166.5 129.9 %all-gather.14.cloned.1.call-start = ((), (), s32[]{:S(2)}) async-start(), calls=%async_computation.12 | async-start | bytes 2621440 | tf_op jit(solution)/shard_map/all_gather | solution.py:142
  167.1 185.6 %reduce-scatter.7.cloned.1.call-start = ((), (), s32[]{:S(2)}) async-start(), calls=%async_computation.13 | async-start | bytes 4718592 | tf_op jit(solution)/shard_map/reduce_scatter | solution.py:136
  167.3 293.8 %copy-start.76 = (f32[2,256]{1,0:T(2,128)}, f32[2,256]{1,0:T(2,128)S(1)}, u32[]{:S(2)}) copy-start(f32[2,256]{1,0:T(2,128)S(1)} %convert_element_type.188) | copy-start | bytes 6148
  301.4 61.1 %copy-start.93 = (s32[512]{0:T(512)S(1)}, s32[512]{0:T(512)}, u32[]{:S(2)}) copy-start(s32[512]{0:T(512)} %get-tuple-element.1210) | copy-start | bytes 6148
  306.6 59.4 %copy-start.82 = (s32[1024]{0:T(1024)}, s32[1024]{0:T(1024)S(1)}, u32[]{:S(2)}) copy-start(s32[1024]{0:T(1024)S(1)} %pad_clamp_fusion.2) | copy-start | bytes 12292
  357.7 13.8 %all-to-all-start.1 = ((bf16[4,128,256]{2,1,0:T(8,128)(2,1)}), bf16[4,128,256]{2,1,0:T(8,128)(2,1)}, u32[]{:S(2)}, u32[]{:S(2)}) async-start(bf16[4,128,256]{2,1,0:T(8,128)(2,1)} %bitcast.811), calls=%async_computation.2 | async-start | bytes 524288 | tf_op jit(solution)/shard_map/all_to_all | solution.py:122
  362.4 98.6 %all-gather.20.cloned.1.call-start = ((), (), s32[]{:S(2)}) async-start(), calls=%async_computation.21 | async-start | bytes 2359296 | tf_op jit(solution)/shard_map/all_gather | solution.py:132
  362.5 54.1 %copy-start.85 = (s32[1024]{0:T(1024)S(1)}, s32[1024]{0:T(1024)}, u32[]{:S(2)}) copy-start(s32[1024]{0:T(1024)} %copy-done.84) | copy-start | bytes 12292
  366.0 53.1 %copy-start.80 = (s32[1024]{0:T(1024)}, s32[1024]{0:T(1024)S(1)}, u32[]{:S(2)}) copy-start(s32[1024]{0:T(1024)S(1)} %pad_clamp_fusion.1) | copy-start | bytes 12292
  374.0 57.0 %copy-start.87 = (s32[1024]{0:T(1024)S(1)}, s32[1024]{0:T(1024)}, u32[]{:S(2)}) copy-start(s32[1024]{0:T(1024)} %copy-done.86) | copy-start | bytes 12292
  433.6 476.1 %reduce-scatter.11.cloned.1.call-start = ((), (), s32[]{:S(2)}) async-start(), calls=%async_computation.15 | async-start | bytes 5242880 | tf_op jit(solution)/shard_map/reduce_scatter | solution.py:327
  593.4 42.9 %copy-start.9 = (f32[1,256,2,1024]{1,0,3,2:T(1,128)S(1)}, f32[1,256,2,1024]{1,0,3,2:T(1,128)}, u32[]{:S(2)}) copy-start(f32[1,256,2,1024]{1,0,3,2:T(1,128)} %copy.664) | copy-start | bytes 6291460 | tf_op jit(solution)/shard_map/transpose(jvp())/while
  636.3 42.6 %copy-start.11 = (f32[2,256,2,256]{3,1,2,0:T(8,128)S(1)}, f32[2,256,2,256]{3,1,2,0:T(8,128)}, u32[]{:S(2)}) copy-start(f32[2,256,2,256]{3,1,2,0:T(8,128)} %copy-done.10) | copy-start | bytes 3145732 | tf_op jit(solution)/shard_map/transpose(jvp())/while
  770.1 42.9 %copy-start.9 = (f32[1,256,2,1024]{1,0,3,2:T(1,128)S(1)}, f32[1,256,2,1024]{1,0,3,2:T(1,128)}, u32[]{:S(2)}) copy-start(f32[1,256,2,1024]{1,0,3,2:T(1,128)} %copy.664) | copy-start | bytes 6291460 | tf_op jit(solution)/shard_map/transpose(jvp())/while
  813.0 42.6 %copy-start.11 = (f32[2,256,2,256]{3,1,2,0:T(8,128)S(1)}, f32[2,256,2,256]{3,1,2,0:T(8,128)}, u32[]{:S(2)}) copy-start(f32[2,256,2,256]{3,1,2,0:T(8,128)} %copy-done.10) | copy-start | bytes 3145732 | tf_op jit(solution)/shard_map/transpose(jvp())/while
  864.9 91.8 %reduce-scatter.9.cloned.1.call-start = ((), (), s32[]{:S(2)}) async-start(), calls=%async_computation.14 | async-start | bytes 5242880 | tf_op jit(solution)/shard_map/reduce_scatter | solution.py:326
  871.4 85.3 %copy-start.68 = (bf16[2,4,3,2,256]{4,3,2,1,0:T(2,128)(2,1)S(1)}, bf16[2,4,3,2,256]{4,3,2,1,0:T(2,128)(2,1)}, u32[]{:S(2)}) copy-start(bf16[2,4,3,2,256]{4,3,2,1,0:T(2,128)(2,1)} %param.26) | copy-start | bytes 73732
  871.5 170.4 %reduce-scatter.13.cloned.1.call-start = ((), (), s32[]{:S(2)}) async-start(), calls=%async_computation.16 | async-start | bytes 4718592 | tf_op jit(solution)/shard_map/reduce_scatter | solution.py:136
  990.4 90.3 %all-reduce.24.cloned.1.call-start = ((), (), s32[]{:S(2)}) async-start(), calls=%async_computation.22 | async-start | bytes 180224 | tf_op jit(solution)/shard_map/psum | solution.py:366
  1000.4 41.5 %copy-start.35 = (bf16[512,256]{1,0:T(8,128)(2,1)S(1)}, bf16[512,256]{1,0:T(8,128)(2,1)}, u32[]{:S(2)}) copy-start(bf16[512,256]{1,0:T(8,128)(2,1)} %copy-done.34) | copy-start | bytes 786436
  1000.4 41.5 %copy-start.64 = (f32[512,1]{0,1:T(1,128)S(1)}, f32[512,1]{0,1:T(1,128)}, u32[]{:S(2)}) copy-start(f32[512,1]{0,1:T(1,128)} %copy-done.63) | copy-start | bytes 6148
  1000.4 41.5 %copy-start.66 = (f32[512,1]{0,1:T(1,128)S(1)}, f32[512,1]{0,1:T(1,128)}, u32[]{:S(2)}) copy-start(f32[512,1]{0,1:T(1,128)} %copy-done.65) | copy-start | bytes 6148
  1000.4 41.5 %copy-start.91 = (f32[256]{0:T(256)S(1)}, f32[256]{0:T(256)}, u32[]{:S(2)}) copy-start(f32[256]{0:T(256)} %copy-done.90) | copy-start | bytes 3076
  1043.9 183.9 %reduce-scatter.15.cloned.1.call-start = ((), (), s32[]{:S(2)}) async-start(), calls=%async_computation.17 | async-start | bytes 10485760 | tf_op jit(solution)/shard_map/reduce_scatter | solution.py:363
  1051.5 256.8 %reduce-scatter.17.cloned.1.call-start = ((), (), s32[]{:S(2)}) async-start(), calls=%async_computation.18 | async-start | bytes 5242880 | tf_op jit(solution)/shard_map/reduce_scatter | solution.py:364
  1073.2 13.6 %all-to-all-start.3 = ((bf16[4,128,256]{2,1,0:T(8,128)(2,1)}), bf16[4,128,256]{2,1,0:T(8,128)(2,1)S(1)}, u32[]{:S(2)}, u32[]{:S(2)}) async-start(bf16[4,128,256]{2,1,0:T(8,128)(2,1)} %bitcast.87), calls=%async_computation.7 | async-start | bytes 524288 | tf_op jit(solution)/shard_map/all_to_all | solution.py:122
  1086.8 225.5 %copy-start.1 = (bf16[512,256]{1,0:T(8,128)(2,1)S(1)}, bf16[512,256]{1,0:T(8,128)(2,1)}, u32[]{:S(2)}) copy-start(bf16[512,256]{1,0:T(8,128)(2,1)} %param.19) | copy-start | bytes 786436
  1089.4 218.9 %copy-start.114 = (f32[256]{0:T(256)S(1)}, f32[256]{0:T(256)}, u32[]{:S(2)}) copy-start(f32[256]{0:T(256)} %get-tuple-element.1706) | copy-start | bytes 3076
  1089.4 219.4 %copy-start.97 = (f32[4,2,256]{2,1,0:T(2,128)S(1)}, f32[4,2,256]{2,1,0:T(2,128)}, u32[]{:S(2)}) copy-start(f32[4,2,256]{2,1,0:T(2,128)} %get-tuple-element.1708) | copy-start | bytes 24580
  1089.4 220.0 %copy-start.109 = (f32[2,256]{1,0:T(2,128)S(1)}, f32[2,256]{1,0:T(2,128)}, u32[]{:S(2)}) copy-start(f32[2,256]{1,0:T(2,128)} %get-tuple-element.1709) | copy-start | bytes 6148
  1089.4 220.6 %copy-start.69 = (f32[3,4,2,256]{3,2,1,0:T(2,128)S(1)}, f32[3,4,2,256]{3,2,1,0:T(2,128)}, u32[]{:S(2)}) copy-start(f32[3,4,2,256]{3,2,1,0:T(2,128)} %get-tuple-element.1710) | copy-start | bytes 73732
  1089.4 221.2 %copy-start.113 = (f32[2,4]{1,0:T(2,128)S(1)}, f32[2,4]{1,0:T(2,128)}, u32[]{:S(2)}) copy-start(f32[2,4]{1,0:T(2,128)} %get-tuple-element.1712) | copy-start | bytes 100
  1089.4 221.8 %copy-start.108 = (f32[2,256]{1,0:T(2,128)S(1)}, f32[2,256]{1,0:T(2,128)}, u32[]{:S(2)}) copy-start(f32[2,256]{1,0:T(2,128)} %get-tuple-element.1713) | copy-start | bytes 6148
  1089.4 222.4 %copy-start.107 = (f32[2,256]{1,0:T(2,128)S(1)}, f32[2,256]{1,0:T(2,128)}, u32[]{:S(2)}) copy-start(f32[2,256]{1,0:T(2,128)} %get-tuple-element.1714) | copy-start | bytes 6148
  (104 other events, 663.9 us)
Sparse Core Ops, SparseCore 0:
  10.2 88.9 all-gather.11
  101.6 26.6 all-gather.9
  166.0 22.9 all-gather.15
  190.4 22.8 all-gather.17
  214.7 45.6 all-gather.13
  301.5 51.1 reduce-scatter.6
  433.8 27.2 all-gather.19
  865.1 44.6 reduce-scatter.10
  912.3 44.4 reduce-scatter.8
  990.5 51.3 reduce-scatter.12
  1045.9 34.7 all-reduce.23
  1083.0 144.7 reduce-scatter.14
  1230.8 77.4 reduce-scatter.16
where the time goes:
time: 1340 us; the launch traced here: 1320 us
  waiting for transfers between devices  459 us (34%)
  local copies, waits for them, and re-layouts  388 us (29%)
  matrix products  180 us (13%)
  blocking collectives  176 us (13%)
  other arithmetic  71.8 us (5%)
  between operations  19.4 us (1%)
  starting transfers between devices  16.2 us (1%)
    dynamic_update_slice x16, local copies, waits for them, and re-layouts, run_cell(): final_state, hidden = lax.scan(jax.checkpoint(cell_block), initial, blocks)  215 us
    reduce_scatter x1, waiting for transfers between devices, shards(): lax.psum_scatter(grad_up, 'dp', scatter_dimension=0, tiled=True)  138 us
    psum x6, blocking collectives, row_sums(): return lax.psum(values_in, ('tensor', 'ctx'))  126 us
    reduce_scatter x2, waiting for transfers between devices, fold_columns(): lax.psum_scatter(values_in, ('tensor', 'ctx'), scatter_dimension=1, tiled...  76.5 us
    reduce_scatter x1, waiting for transfers between devices, shards(): lax.psum_scatter(grad_down, 'dp', scatter_dimension=2, tiled=True)  76 us
    all_gather x2, waiting for transfers between devices, spread_rows(): return lax.all_gather(values_in, ('tensor', 'ctx'), axis=1, tiled=True)  50.1 us
    reduce_scatter x1, waiting for transfers between devices, shards(): lax.psum_scatter(grad_query, 'tensor', scatter_dimension=2, tiled=True)  47 us
    psum x1, blocking collectives, shards(): lax.psum((jnp.sum(keep * 0.5 * jnp.sum(difference * difference, axis=1)),...  38.1 us
  transfers between devices with their start and end apart: 16, of which 14 were waited for; matrix products, arithmetic and copies ran while one was open for 12% of the time, Pallas kernels for 0%

commit v1 on v0

v1 whole, which is shorter than its diff:
```python
import jax
import jax.numpy as jnp
from jax import lax
from jax.sharding import PartitionSpec as P

NEG_FILL = -1e30
EPSILON = 1e-05
PLANE = ("tensor", "ctx")
BF = jnp.bfloat16
F32 = jnp.float32


def mm(a, b):
    return jnp.dot(a, b, preferred_element_type=F32)


def mm_nt(a, b):
    return lax.dot_general(a, b, (((1,), (1,)), ((), ())), preferred_element_type=F32)


def mm_tn(a, b):
    return lax.dot_general(a, b, (((0,), (0,)), ((), ())), preferred_element_type=F32)


def split(v):
    high = lax.reduce_precision(v, 8, 7)
    return high.astype(BF), (v - high).astype(BF)


def two(v, b, product):
    high, rest = split(v)
    return product(high, b) + product(rest, b)


def shift_down(v, offset):
    return jnp.concatenate([jnp.zeros((offset,) + v.shape[1:], v.dtype), v[:-offset]], axis=0)


def shift_up(v, offset):
    return jnp.concatenate([v[offset:], jnp.zeros((offset,) + v.shape[1:], v.dtype)], axis=0)


def shards(
    tokens,
    targets,
    ln_gain,
    up_weight,
    conv_weight,
    conv_bias,
    qkv_weight,
    gate_weight,
    gate_bias,
    group_gain,
    skip_gain,
    down_weight,
    lengths,
    permutation,
    valid,
):
    rows, own_width = tokens.shape
    dp_count = lax.axis_size("dp")
    tensor_count = lax.axis_size("tensor")
    ctx_count = lax.axis_size("ctx")
    spread = tensor_count * ctx_count
    width = own_width * spread
    dp = lax.axis_index("dp")
    ctx = lax.axis_index("ctx")
    plane = lax.axis_index("tensor") * ctx_count + ctx
    heads, chan = up_weight.shape[2], up_weight.shape[3]
    local = heads * chan
    all_heads = gate_weight.shape[1]
    head_width = chan * tensor_count
    all_rows = rows * dp_count
    cap = rows // dp_count
    block = up_weight.shape[0]

    up_cell = lax.all_gather(up_weight[:, 0].reshape(block, local), "dp", axis=0, tiled=True)
    up_gate = lax.all_gather(up_weight[:, 1].reshape(block, local), "dp", axis=0, tiled=True)
    down_all = lax.all_gather(down_weight.reshape(local, -1), "dp", axis=0, tiled=False)

    place = jnp.arange(rows, dtype=jnp.int32)
    own_perm = lax.dynamic_slice_in_dim(permutation, dp * rows, rows)
    dest = own_perm // rows
    earlier = (dest[:, None] == dest[None, :]) & (place[:, None] > place[None, :])
    code = dest * cap + jnp.sum(earlier.astype(jnp.int32), axis=1)
    send_map = (place[:, None] == code[None, :]).astype(BF)
    by_source = permutation.reshape(dp_count, rows)
    mine = by_source // rows == dp
    before = (place[:, None] < place[None, :]).astype(BF)
    rank = mm(mine.astype(BF), before).astype(jnp.int32)
    hit = mine[:, None, :] & (rank[:, None, :] == jnp.arange(cap, dtype=jnp.int32)[None, :, None])
    slot_of = jnp.sum(jnp.where(hit, (by_source - dp * rows)[:, None, :], 0), axis=2).reshape(-1)
    recv_map = (place[:, None] == slot_of[None, :]).astype(BF)

    ends_all = jnp.cumsum(lengths, axis=1)
    ends = lax.dynamic_index_in_dim(ends_all, dp, 0, keepdims=False)
    segment = jnp.sum((place[:, None] >= ends[None, :]).astype(jnp.int32), axis=1)
    seg_col = segment[:, None]
    valid_all = lax.all_gather(valid, "dp", axis=0, tiled=True)
    total_of = jnp.sum(
        jnp.where(
            (permutation // rows)[:, None] == jnp.arange(dp_count, dtype=jnp.int32)[None, :],
            ends_all[:, -1][None, :],
            0,
        ),
        axis=1,
    )
    count = jnp.sum(jnp.where(permutation % rows < total_of, valid_all, 0)).astype(F32)

    payload = jnp.concatenate(
        [tokens, targets, jnp.broadcast_to(valid[:, None], (rows, 128)).astype(BF)], axis=1
    )
    sent = mm(send_map, payload).astype(BF)
    arrived = lax.all_to_all(sent, "dp", split_axis=0, concat_axis=0, tiled=True)
    placed = mm(recv_map, arrived).astype(BF)
    work = placed[:, :own_width]
    goal = placed[:, own_width : 2 * own_width].astype(F32)
    keep = placed[:, 2 * own_width : 2 * own_width + 1].astype(F32) * (
        seg_col < lengths.shape[1]
    ).astype(F32)

    work_full = lax.all_gather(work, PLANE, axis=1, tiled=True).astype(F32)
    gain_full = lax.all_gather(ln_gain, PLANE, axis=0, tiled=True).astype(F32)
    row_mean = jnp.mean(work_full, axis=1, keepdims=True)
    row_var = jnp.mean(work_full * work_full, axis=1, keepdims=True) - row_mean * row_mean
    row_rstd = lax.rsqrt(row_var + EPSILON)
    normed = ((work_full - row_mean) * row_rstd * gain_full[None]).astype(BF)
    own_x = work.astype(F32)
    x_hat = (own_x - row_mean) * row_rstd

    branch_low = mm(normed, up_cell).astype(BF)
    branch = branch_low.astype(F32)
    taps = conv_weight.astype(F32).reshape(-1, local)
    tap_count = taps.shape[0]
    linked = [None] + [
        jnp.concatenate([jnp.full((j,), -1, jnp.int32), segment[:-j]])[:, None] == seg_col
        for j in range(1, tap_count)
    ]
    conv = conv_bias.astype(F32).reshape(1, local) + taps[0][None] * branch
    for j in range(1, tap_count):
        conv = conv + jnp.where(linked[j], taps[j][None] * shift_down(branch, j), 0.0)
    sig = jax.nn.sigmoid(conv)
    act = conv * sig
    width_of_map = qkv_weight.shape[1]
    cin = jnp.arange(chan, dtype=jnp.int32)
    same_map = cin[:, None] // width_of_map == cin[None, :] // width_of_map
    maps = [
        [
            jnp.where(same_map, jnp.tile(qkv_weight[s, :, h], (chan // width_of_map, 1)), 0).astype(BF)
            for h in range(heads)
        ]
        for s in range(3)
    ]

    def head_of(v, h):
        return v[:, h * chan : (h + 1) * chan]

    def per_head(parts):
        return jnp.concatenate(parts, axis=1)

    q = per_head([two(head_of(act, h), maps[0][h], mm) for h in range(heads)]).astype(BF)
    k = per_head([two(head_of(act, h), maps[1][h], mm) for h in range(heads)]).astype(BF)
    v = per_head([mm(head_of(branch_low, h), maps[2][h]) for h in range(heads)]).astype(BF)
    qkv = jnp.concatenate([q, k, v], axis=1)
    gates_w = gate_weight.reshape(2 * all_heads, -1)
    pre_part = mm_nt(gates_w, qkv)
    pre = lax.psum(pre_part, PLANE) + gate_bias.astype(F32).reshape(-1, 1)
    own_pre = lax.dynamic_slice_in_dim(
        pre.reshape(2, all_heads, rows), ctx * heads, heads, 1
    )
    in_gate, forget = own_pre[0], own_pre[1]
    log_forget = jax.nn.log_sigmoid(forget)
    rising = jnp.cumsum(log_forget, axis=1)
    score_part = jnp.stack([mm_nt(head_of(q, h), head_of(k, h)) for h in range(heads)])
    scores = lax.psum(score_part, "tensor")
    allowed = (seg_col == segment[None, :]) & (place[:, None] >= place[None, :])
    scale = head_width**-0.5
    hidden, weights, decays, inv_r, dens, live = [], [], [], [], [], []
    for h in range(heads):
        logit = jnp.where(
            allowed, rising[h][:, None] + (in_gate[h] - rising[h])[None, :], NEG_FILL
        )
        top = jnp.max(logit, axis=1, keepdims=True)
        decay = jnp.where(allowed, jnp.exp(logit - top), 0.0) * scale
        weight = scores[h] * decay
        den = jnp.sum(weight, axis=1, keepdims=True)
        floor = jnp.exp(-top)
        inv = 1.0 / jnp.maximum(jnp.abs(den), floor)
        weight_low = weight.astype(BF)
        hidden.append(mm(weight_low, head_of(v, h)) * inv)
        weights.append(weight)
        decays.append(decay)
        inv_r.append(inv)
        dens.append(den)
        live.append(jnp.abs(den) > floor)
    hidden_all = per_head(hidden)
    moments = lax.psum(
        jnp.stack(
            [jnp.stack([jnp.sum(hh, axis=1), jnp.sum(hh * hh, axis=1)]) for hh in hidden]
        ),
        "tensor",
    ) / head_width
    h_mean = [moments[h, 0][:, None] for h in range(heads)]
    h_rstd = [
        lax.rsqrt(moments[h, 1][:, None] - h_mean[h] * h_mean[h] + EPSILON) for h in range(heads)
    ]
    h_hat = per_head([(hidden[h] - h_mean[h]) * h_rstd[h] for h in range(heads)])

    gate_branch = mm(normed, up_gate).astype(BF).astype(F32)
    group = group_gain.astype(F32).reshape(1, local)
    skip = skip_gain.astype(F32).reshape(1, local)
    gate_sig = jax.nn.sigmoid(gate_branch)
    silu = gate_branch * gate_sig
    inner = h_hat * group + skip * act
    mixed = (inner * silu).astype(BF)
    down_part = jnp.concatenate([mm(mixed, down_all[z]) for z in range(dp_count)], axis=1)
    down_out = lax.psum_scatter(down_part.astype(BF), PLANE, scatter_dimension=1, tiled=True)
    result = (own_x + down_out.astype(F32)).astype(BF)
    difference = result.astype(F32) - goal
    loss_part = jnp.sum(keep * 0.5 * jnp.sum(difference * difference, axis=1, keepdims=True))
    loss = lax.psum(loss_part, ("dp", "tensor", "ctx")) / count
    grad_work = (all_rows / count * keep * difference).astype(BF)
    grad_full = lax.all_gather(grad_work, PLANE, axis=1, tiled=True)

    grad_down = jnp.concatenate(
        [mm_tn(mixed, grad_full[:, z * block : (z + 1) * block]) for z in range(dp_count)], axis=0
    )
    down_owned = lax.psum_scatter(grad_down.astype(BF), "dp", scatter_dimension=0, tiled=True)
    grad_mixed = sum(
        mm_nt(grad_full[:, z * block : (z + 1) * block], down_all[z]) for z in range(dp_count)
    )
    grad_inner = grad_mixed * silu
    grad_gate_branch = grad_mixed * inner * (gate_sig + silu * (1.0 - gate_sig))
    g_gate_low = grad_gate_branch.astype(BF)
    grad_up_gate = mm_tn(normed, g_gate_low)
    up_gate_owned = lax.psum_scatter(grad_up_gate.astype(BF), "dp", scatter_dimension=0, tiled=True)
    grad_skip = jnp.sum(grad_inner * act, axis=0)
    grad_group = jnp.sum(grad_inner * h_hat, axis=0)
    grad_act = grad_inner * skip
    u = grad_inner * group
    u_moments = lax.psum(
        jnp.stack(
            [
                jnp.stack(
                    [
                        jnp.sum(head_of(u, h), axis=1),
                        jnp.sum(head_of(u, h) * head_of(h_hat, h), axis=1),
                    ]
                )
                for h in range(heads)
            ]
        ),
        "tensor",
    )
    d_num, d_den, radial = [], [], []
    for h in range(heads):
        mean_u = u_moments[h, 0][:, None] / head_width
        sum_ux = u_moments[h, 1][:, None]
        d_hidden = h_rstd[h] * (head_of(u, h) - mean_u - head_of(h_hat, h) * (sum_ux / head_width))
        rho = sum_ux * (EPSILON * h_rstd[h] * h_rstd[h])
        d_num.append((d_hidden * inv_r[h]).astype(BF))
        d_den.append(jnp.where(live[h], jnp.where(dens[h] > 0.0, -rho, rho) * inv_r[h], 0.0))
        radial.append(rho)
    dw_part = jnp.stack([mm_nt(d_num[h], head_of(v, h)) for h in range(heads)])
    dw = lax.psum(dw_part, "tensor")
    grad_q, grad_k, grad_v, pre_grads = [], [], [], []
    for h in range(heads):
        full = dw[h] + d_den[h]
        exact = jnp.where(live[h], 0.0, radial[h])
        noisy = jnp.sum(full * weights[h], axis=1, keepdims=True)
        square = jnp.sum(weights[h] * weights[h], axis=1, keepdims=True)
        full = full - weights[h] * ((noisy - exact) / jnp.where(square > 0.0, square, 1.0))
        d_score = (full * decays[h]).astype(BF)
        d_logit = full * weights[h]
        over_rows = jnp.sum(d_logit, axis=1)
        over_cols = jnp.sum(d_logit, axis=0)
        grad_q.append(mm(d_score, head_of(k, h)))
        grad_k.append(mm_tn(d_score, head_of(q, h)))
        grad_v.append(mm_tn(weights[h].astype(BF), d_num[h]))
        delta = over_rows - over_cols
        d_forget = jnp.sum(delta) - jnp.cumsum(delta) + delta
        pre_grads.append(
            jnp.stack([over_cols, d_forget * (1.0 - jax.nn.sigmoid(forget[h]))])
        )
    own_grads = jnp.stack(pre_grads, axis=1)
    pre_grad = (
        lax.all_gather(own_grads, "ctx", axis=1, tiled=True).reshape(2 * all_heads, rows)
    )
    grad_gate_bias = jnp.sum(pre_grad, axis=1).reshape(2, all_heads)
    grad_proj = jnp.concatenate(grad_q + grad_k + grad_v, axis=1) + two(
        pre_grad.T, gates_w, mm
    )
    grad_gate_weight = two(pre_grad, qkv, mm).reshape(gate_weight.shape)
    gq, gk, gv = (grad_proj[:, s * local : (s + 1) * local] for s in range(3))

    grad_maps = []
    act_low = act.astype(BF)
    gq_low, gk_low, gv_low = gq.astype(BF), gk.astype(BF), gv.astype(BF)
    for left, right in ((act_low, gq_low), (act_low, gk_low), (branch_low, gv_low)):
        per = []
        for h in range(heads):
            dense = jnp.where(same_map, mm_tn(head_of(left, h), head_of(right, h)), 0.0)
            per.append(jnp.sum(dense.reshape(chan // width_of_map, width_of_map, chan), axis=0))
        grad_maps.append(jnp.stack(per, axis=1))
    grad_qkv = jnp.stack(grad_maps)
    grad_act = grad_act + per_head(
        [
            mm_nt(head_of(gq_low, h), maps[0][h]) + mm_nt(head_of(gk_low, h), maps[1][h])
            for h in range(heads)
        ]
    )
    grad_conv = grad_act * (sig + act * (1.0 - sig))
    grad_branch = per_head([mm_nt(head_of(gv_low, h), maps[2][h]) for h in range(heads)])
    grad_branch = grad_branch + taps[0][None] * grad_conv
    grad_taps = [jnp.sum(grad_conv * branch, axis=0)]
    for j in range(1, tap_count):
        kept = jnp.where(linked[j], grad_conv, 0.0)
        grad_branch = grad_branch + taps[j][None] * shift_up(kept, j)
        grad_taps.append(jnp.sum(kept * shift_down(branch, j), axis=0))
    g_cell_low = grad_branch.astype(BF)
    grad_up_cell = mm_tn(normed, g_cell_low)
    up_cell_owned = lax.psum_scatter(grad_up_cell.astype(BF), "dp", scatter_dimension=0, tiled=True)
    grad_normed_part = mm_nt(g_cell_low, up_cell) + mm_nt(g_gate_low, up_gate)
    grad_normed = lax.psum_scatter(
        grad_normed_part.astype(BF), PLANE, scatter_dimension=1, tiled=True
    ).astype(F32)
    ln_float = ln_gain.astype(F32)[None]
    grad_scaled = grad_normed * ln_float
    grad_ln = jnp.sum(grad_normed * x_hat, axis=0)
    lines = lax.psum(
        jnp.stack([jnp.sum(grad_scaled, axis=1), jnp.sum(grad_scaled * x_hat, axis=1)]), PLANE
    )
    grad_x = row_rstd * (
        grad_scaled - lines[0][:, None] / width - x_hat * (lines[1][:, None] / width)
    )
    grad_slot = (grad_work.astype(F32) + grad_x).astype(BF)
    back = mm_tn(recv_map, jnp.concatenate([result, grad_slot], axis=1)).astype(BF)
    home = lax.all_to_all(back, "dp", split_axis=0, concat_axis=0, tiled=True)
    out_rows = mm_tn(send_map, home).astype(BF)

    small = [
        grad_ln,
        jnp.stack(grad_taps).reshape(-1),
        jnp.sum(grad_conv, axis=0),
        grad_qkv.reshape(-1),
        grad_gate_weight.reshape(-1),
        grad_gate_bias.reshape(-1),
        grad_group,
        grad_skip,
    ]
    sizes = [s.shape[0] for s in small]
    summed = lax.psum(jnp.concatenate(small), "dp")
    pieces, at = [], 0
    for size in sizes:
        pieces.append(summed[at : at + size])
        at += size
    grad_up = jnp.stack(
        [
            up_cell_owned.astype(F32).reshape(block, heads, chan),
            up_gate_owned.astype(F32).reshape(block, heads, chan),
        ],
        axis=1,
    )
    return (
        out_rows[:, :own_width],
        loss,
        out_rows[:, own_width:],
        pieces[0],
        grad_up,
        pieces[1].reshape(conv_weight.shape),
        pieces[2].reshape(conv_bias.shape),
        pieces[3].reshape(qkv_weight.shape),
        pieces[4].reshape(gate_weight.shape),
        pieces[5].reshape(gate_bias.shape),
        pieces[6].reshape(group_gain.shape),
        pieces[7].reshape(skip_gain.shape),
        down_owned.astype(F32).reshape(down_weight.shape),
    )


def solution(mesh):
    return jax.shard_map(
        shards,
        mesh=mesh,
        in_specs=(
            P("dp", ("tensor", "ctx")),
            P("dp", ("tensor", "ctx")),
            P(("tensor", "ctx")),
            P("dp", None, "ctx", "tensor"),
            P(None, "ctx", "tensor"),
            P("ctx", "tensor"),
            P(None, None, "ctx", "tensor"),
            P(None, None, None, "ctx", "tensor"),
            P(),
            P("ctx", "tensor"),
            P("ctx", "tensor"),
            P("ctx", "tensor", "dp"),
            P(),
            P(),
            P("dp"),
        ),
        out_specs=(
            P("dp", ("tensor", "ctx")),
            P(),
            P("dp", ("tensor", "ctx")),
            P(("tensor", "ctx")),
            P("dp", None, "ctx", "tensor"),
            P(None, "ctx", "tensor"),
            P("ctx", "tensor"),
            P(None, None, "ctx", "tensor"),
            P(None, None, None, "ctx", "tensor"),
            P(),
            P("ctx", "tensor"),
            P("ctx", "tensor"),
            P("ctx", "tensor", "dp"),
        ),
        check_vma=False,
    )
```

time: 1340 us -> 704 us (0.53)
  local copies, waits for them, and re-layouts: 388 us -> 44.6 us
  matrix products: 180 us -> 64.9 us
  waiting for transfers between devices: 459 us -> 375 us
  blocking collectives: 176 us -> 123 us
  other arithmetic: 71.8 us -> 54.9 us
    reduce_scatter x6 -> x5, waiting for transfers between devices: 350 us -> 121 us  [the longest x1 44.4 us: shards(): lax.psum_scatter(grad_up_cell.astype(BF), 'dp', scatter_dimension=0, tile...]
    dynamic_update_slice x16 -> x0, local copies, waits for them, and re-layouts: 215 us -> none  [run_cell(): final_state, hidden = lax.scan(jax.checkpoint(cell_block), initial, blocks)]
    dot_general x58 -> x62, matrix products: 180 us -> 64.9 us  [the longest x27 27.2 us: mm(): return jnp.dot(a, b, preferred_element_type=F32)]
    psum x1 -> x3, waiting for transfers between devices: 1.85 us -> 82.5 us  [the longest x1 51.4 us: shards(): dw = lax.psum(dw_part, 'tensor')]
    all_gather x6 -> x5, waiting for transfers between devices: 83 us -> 154 us  [the longest x1 45.2 us: shards(): lax.all_gather(up_weight[:, 0].reshape(block, local), 'dp', axis=0, tiled...]
    psum x7 -> x5, blocking collectives: 164 us -> 94 us  [the longest x1 42.6 us: shards(): loss = lax.psum(loss_part, ('dp', 'tensor', 'ctx')) / count]
    all_gather x0 -> x3, blocking collectives: none -> 28.8 us  [the longest x1 12.5 us: shards(): gain_full = lax.all_gather(ln_gain, PLANE, axis=0, tiled=True).astype(F32)]
    reshape x19 -> x17, local copies, waits for them, and re-layouts: 32.9 us -> 7.31 us  [the longest x6 2.35 us: shards(): dense.reshape(chan // width_of_map, width_of_map, chan)]
  transfers between devices with their start and end apart: 16 -> 15, of which waited for: 14 -> 13; matrix products, arithmetic and copies ran while one was open for 12% -> 12% of each run, Pallas kernels for 0% -> 0%
where the time goes in v1:
time: 704 us; the launch traced here: 694 us
  waiting for transfers between devices  375 us (53%)
  blocking collectives  123 us (17%)
  matrix products  64.9 us (9%)
  other arithmetic  54.9 us (8%)
  local copies, waits for them, and re-layouts  44.6 us (6%)
  between operations  18.9 us (3%)
  starting transfers between devices  12.8 us (2%)
    psum x1, waiting for transfers between devices, shards(): dw = lax.psum(dw_part, 'tensor')  51.4 us
    all_gather x1, waiting for transfers between devices, shards(): lax.all_gather(up_weight[:, 0].reshape(block, local), 'dp', axis=0, tiled...  45.2 us
    reduce_scatter x1, waiting for transfers between devices, shards(): lax.psum_scatter(grad_up_cell.astype(BF), 'dp', scatter_dimension=0, tile...  44.4 us
    psum x1, blocking collectives, shards(): loss = lax.psum(loss_part, ('dp', 'tensor', 'ctx')) / count  42.6 us
    all_gather x1, waiting for transfers between devices, shards(): lax.all_gather(down_weight.reshape(local, -1), 'dp', axis=0, tiled=False)  40.7 us
    reduce_scatter x1, waiting for transfers between devices, shards(): lax.psum_scatter(grad_up_gate.astype(BF), 'dp', scatter_dimension=0, tile...  36 us
    all_gather x1, waiting for transfers between devices, shards(): lax.all_gather(up_weight[:, 1].reshape(block, local), 'dp', axis=0, tiled...  33.1 us
    all_gather x1, waiting for transfers between devices, shards(): grad_full = lax.all_gather(grad_work, PLANE, axis=1, tiled=True)  28 us
  transfers between devices with their start and end apart: 15, of which 13 were waited for; matrix products, arithmetic and copies ran while one was open for 12% of the time, Pallas kernels for 0%

profile of v1, /device:TPU:0, one launch (start us, length us, event | category | flops | bytes accessed | tf_op | source)
XLA Modules:
  0.0 693.7 jit_solution(16336519967867436091)
XLA Ops:
  9.8 2.5 convolution_convert_fusion.3
  12.3 6.4 all-to-all-start
  19.3 16.8 %all-to-all-done = bf16[4,128,640]{2,1,0:T(8,128)(2,1)S(1)} async-done(((bf16[4,128,640]{2,1,0:T(8,128)(2,1)}), bf16[4,128,640]{2,1,0:T(8,128)(2,1)S(1)}, u32[]{:S(2)}, u32[]{:S(2)}) %all-to-all-start) | async-done | bytes 655392 | tf_op jit(solution)/shard_map/all_to_all | solution.py:114
  40.8 12.5 %all-gather = bf16[8,1,256]{2,1,0:T(2,128)(2,1)S(1)} all-gather(bf16[1,1,256]{2,1,0:T(2,128)(2,1)S(1)} %reshape.784), channel_id=1, replica_groups=mesh['dp'=4,'tensor'=4,'ctx'=2] {'tensor','ctx'}, dimensions={0}, use_global_device_ids=true | all-gather | bytes 4608 | tf_op jit(solution)/shard_map/all_gather | solution.py:123
  58.6 6.7 all-gather.8.cloned.1.call-done
  65.4 2.3 convert_reduce_fusion
  68.3 45.2 %all-gather.10.cloned.1.call-done = bf16[2048,512]{1,0:T(8,128)(2,1)} async-done(((bf16[512,512]{1,0:T(8,128)(2,1)}), bf16[2048,512]{1,0:T(8,128)(2,1)}) %all-gather.10.cloned.1.call-update) | async-done | bytes 2097168 | tf_op jit(solution)/shard_map/all_gather | solution.py:77
  113.5 3.0 convolution_convert_fusion.15
  117.7 2.1 fusion.142
  131.2 24.9 %psum.57 = f32[8,512]{1,0:T(8,128)S(1)} all-reduce(f32[8,512]{1,0:T(8,128)S(1)} %convolution_bitcast_fusion.4), channel_id=1, replica_groups=mesh['dp'=4,'tensor'=4,'ctx'=2] {'tensor','ctx'}, use_global_device_ids=true, to_apply=%region_7.8 | all-reduce | flops 4096 | bytes 32768 | tf_op jit(solution)/shard_map/psum | solution.py:167
  157.9 18.9 %all-reduce.12.cloned.1.call-done = f32[2,512,512]{2,1,0:T(8,128)} async-done(((f32[2,512,512]{2,1,0:T(8,128)}), f32[2,512,512]{2,1,0:T(8,128)}) %all-reduce.12.cloned.1.call-update) | async-done | bytes 2097168 | tf_op jit(solution)/shard_map/psum | solution.py:175
  176.8 2.4 fusion.152
  182.2 5.9 psum.58
  188.2 2.0 subtract_multiply_fusion
  191.3 33.1 %all-gather.12.cloned.1.call-done = bf16[2048,512]{1,0:T(8,128)(2,1)} async-done(((bf16[512,512]{1,0:T(8,128)(2,1)}), bf16[2048,512]{1,0:T(8,128)(2,1)}) %all-gather.12.cloned.1.call-update) | async-done | bytes 2097168 | tf_op jit(solution)/shard_map/all_gather | solution.py:78
  224.4 5.5 multiply_convert_fusion.3
  229.8 40.7 %all-gather.14.cloned.1.call-done = bf16[4,512,512]{2,1,0:T(8,128)(2,1)} async-done(((bf16[1,512,512]{2,1,0:T(8,128)(2,1)}), bf16[4,512,512]{2,1,0:T(8,128)(2,1)}) %all-gather.14.cloned.1.call-update) | async-done | bytes 2097168 | tf_op jit(solution)/shard_map/all_gather | solution.py:79
  270.5 1.8 convolution_convert_fusion.10
  272.4 1.7 convolution_convert_fusion.11
  277.2 11.9 %all-gather.1 = s32[4,1,512]{2,1,0:T(1,128)S(1)} all-gather(s32[1,1,512]{2,1,0:T(1,128)S(1)} %bitcast.297), channel_id=1, replica_groups=mesh['dp'=4,'tensor'=4,'ctx'=2] {'dp'}, dimensions={0}, use_global_device_ids=true | all-gather | bytes 10240 | tf_op jit(solution)/shard_map/all_gather | solution.py:99
  291.4 25.2 %reduce-scatter.6.cloned.1.call-done = bf16[512,256]{0,1:T(8,128)(2,1)} async-done(((bf16[512,2048]{0,1:T(8,128)(2,1)}), bf16[512,256]{0,1:T(8,128)(2,1)}) %reduce-scatter.6.cloned.1.call-update) | async-done | bytes 262160 | tf_op jit(solution)/shard_map/reduce_scatter | solution.py:217
  316.6 2.0 multiply_convert_fusion.6
  318.7 28.0 %all-gather.16.cloned.1.call-done = bf16[512,2048]{0,1:T(8,128)(2,1)} async-done(((bf16[512,256]{0,1:T(8,128)(2,1)}), bf16[512,2048]{0,1:T(8,128)(2,1)}) %all-gather.16.cloned.1.call-update) | async-done | bytes 2097168 | tf_op jit(solution)/shard_map/all_gather | solution.py:223
  346.8 1.8 fusion.58
  348.7 1.7 convolution_add_fusion.4
  351.5 1.6 broadcast_multiply_fusion
  354.1 7.0 %psum.59 = f32[2,2,512]{2,1,0:T(2,128)S(1)} all-reduce(f32[2,2,512]{2,1,0:T(2,128)S(1)} %pad_maximum_fusion.7), channel_id=1, replica_groups=mesh['dp'=4,'tensor'=4,'ctx'=2] {'tensor'}, use_global_device_ids=true, to_apply=%region_26.27 | all-reduce | flops 2048 | bytes 16384 | tf_op jit(solution)/shard_map/psum | solution.py:241
  362.4 2.1 multiply_convert_fusion.5
  368.0 51.4 %all-reduce.14.cloned.1.call-done = f32[2,512,512]{2,1,0:T(8,128)} async-done(((f32[2,512,512]{2,1,0:T(8,128)}), f32[2,512,512]{2,1,0:T(8,128)}) %all-reduce.14.cloned.1.call-update) | async-done | bytes 2097168 | tf_op jit(solution)/shard_map/psum | solution.py:265
  419.4 2.3 multiply_reduce_fusion.7
  430.4 4.4 all_gather.31
  436.0 2.1 convolution_dynamic-update-slice_fusion.5
  446.5 1.9 multiply_reduce_fusion
  448.5 1.6 multiply_reduce_fusion.4
  454.3 2.6 add_convert_fusion
  467.8 2.1 convolution_select_fusion.1
  470.9 1.9 convolution_select_fusion
  483.0 15.4 %reduce-scatter.8.cloned.1.call-done = bf16[512,256]{0,1:T(8,128)(2,1)} async-done(((bf16[512,2048]{0,1:T(8,128)(2,1)}), bf16[512,256]{0,1:T(8,128)(2,1)}) %reduce-scatter.8.cloned.1.call-update) | async-done | bytes 262160 | tf_op jit(solution)/shard_map/reduce_scatter | solution.py:324
  501.2 4.2 convolution_convert_fusion
  506.5 4.3 convolution_convert_fusion.1
  510.9 13.6 %psum.61 = f32[2,512]{1,0:T(2,128)S(1)} all-reduce(f32[2,512]{1,0:T(2,128)S(1)} %pad_maximum_fusion.9), channel_id=1, replica_groups=mesh['dp'=4,'tensor'=4,'ctx'=2] {'tensor','ctx'}, use_global_device_ids=true, to_apply=%region_45.46 | all-reduce | flops 1024 | bytes 8192 | tf_op jit(solution)/shard_map/psum | solution.py:330
  526.1 5.4 all-to-all-start.1
  532.1 42.6 %psum.62 = f32[]{:T(128)} all-reduce(f32[]{:T(128)} %multiply_reduce_fusion.15), channel_id=1, replica_groups=mesh['dp'=4,'tensor'=4,'ctx'=2] {'dp','tensor','ctx'}, use_global_device_ids=true, to_apply=%region_48.49 | all-reduce | flops 1 | bytes 8 | tf_op jit(solution)/shard_map/psum | solution.py:221
  574.7 2.1 convert.53
  577.5 12.3 %all-reduce.16.cloned.1.call-done = f32[22280]{0:T(1024)} async-done(((f32[22280]{0:T(1024)}), f32[22280]{0:T(1024)}) %all-reduce.16.cloned.1.call-update) | async-done | bytes 89136 | tf_op jit(solution)/shard_map/psum | solution.py:352
  600.4 36.0 %reduce-scatter.12.cloned.1.call-done = bf16[512,512]{1,0:T(8,128)(2,1)} async-done(((bf16[2048,512]{1,0:T(8,128)(2,1)}), bf16[512,512]{1,0:T(8,128)(2,1)}) %reduce-scatter.12.cloned.1.call-update) | async-done | bytes 524304 | tf_op jit(solution)/shard_map/reduce_scatter | solution.py:236
  637.6 44.4 %reduce-scatter.10.cloned.1.call-done = bf16[512,512]{1,0:T(8,128)(2,1)} async-done(((bf16[2048,512]{1,0:T(8,128)(2,1)}), bf16[512,512]{1,0:T(8,128)(2,1)}) %reduce-scatter.10.cloned.1.call-update) | async-done | bytes 524304 | tf_op jit(solution)/shard_map/reduce_scatter | solution.py:322
  683.2 2.4 maximum_convert_fusion
  (561 shorter events, 105.9 us)
Async XLA Ops:
  12.3 26.0 %copy-start.45 = (bf16[512,2,2,256]{3,2,1,0:T(2,128)(2,1)S(1)}, bf16[512,2,2,256]{3,2,1,0:T(2,128)(2,1)}, u32[]{:S(2)}) copy-start(bf16[512,2,2,256]{3,2,1,0:T(2,128)(2,1)} %param.18) | copy-start | bytes 3145732
  12.3 23.7 %all-to-all-start = ((bf16[4,128,640]{2,1,0:T(8,128)(2,1)}), bf16[4,128,640]{2,1,0:T(8,128)(2,1)S(1)}, u32[]{:S(2)}, u32[]{:S(2)}) async-start(bf16[4,128,640]{2,1,0:T(8,128)(2,1)} %bitcast.1), calls=%async_computation | async-start | bytes 1310720 | tf_op jit(solution)/shard_map/all_to_all | solution.py:114
  18.7 46.7 %all-gather.8.cloned.1.call-start = ((), (), s32[]{:S(2)}) async-start(), calls=%async_computation.7 | async-start | bytes 2359296 | tf_op jit(solution)/shard_map/all_gather | solution.py:122
  38.2 75.3 %all-gather.10.cloned.1.call-start = ((), (), s32[]{:S(2)}) async-start(), calls=%async_computation.8 | async-start | bytes 2621440 | tf_op jit(solution)/shard_map/all_gather | solution.py:77
  39.9 136.9 %all-reduce.12.cloned.1.call-start = ((), (), s32[]{:S(2)}) async-start(), calls=%async_computation.9 | async-start | bytes 4194304 | tf_op jit(solution)/shard_map/psum | solution.py:175
  40.2 73.3 %copy-start.127 = (s32[4,3]{1,0:T(4,128)}, s32[4,3]{1,0:T(4,128)S(1)}, u32[]{:S(2)}) copy-start(s32[4,3]{1,0:T(4,128)S(1)} %reduce_window_sum.57) | copy-start | bytes 148
  56.9 66.0 %copy-start.31 = (bf16[256,256]{1,0:T(8,128)(2,1)}, bf16[256,256]{1,0:T(8,128)(2,1)S(1)}, u32[]{:S(2)}) copy-start(bf16[256,256]{1,0:T(8,128)(2,1)S(1)} %tile.65) | copy-start | bytes 393220
  57.9 64.8 %copy-start.29 = (bf16[256,256]{1,0:T(8,128)(2,1)}, bf16[256,256]{1,0:T(8,128)(2,1)S(1)}, u32[]{:S(2)}) copy-start(bf16[256,256]{1,0:T(8,128)(2,1)S(1)} %tile.68) | copy-start | bytes 393220
  65.4 48.1 %copy-start.27 = (bf16[512,2048]{0,1:T(8,128)(2,1)S(1)}, bf16[512,2048]{0,1:T(8,128)(2,1)}, u32[]{:S(2)}) copy-start(bf16[512,2048]{0,1:T(8,128)(2,1)} %all-gather.8.cloned.1.call-done) | copy-start | bytes 6291460
  126.3 98.0 %all-gather.12.cloned.1.call-start = ((), (), s32[]{:S(2)}) async-start(), calls=%async_computation.10 | async-start | bytes 2621440 | tf_op jit(solution)/shard_map/all_gather | solution.py:78
  127.3 143.2 %all-gather.14.cloned.1.call-start = ((), (), s32[]{:S(2)}) async-start(), calls=%async_computation.11 | async-start | bytes 2621440 | tf_op jit(solution)/shard_map/all_gather | solution.py:79
  127.9 188.7 %reduce-scatter.6.cloned.1.call-start = ((), (), s32[]{:S(2)}) async-start(), calls=%async_computation.12 | async-start | bytes 2359296 | tf_op jit(solution)/shard_map/reduce_scatter | solution.py:217
  129.4 47.4 %copy-start.37 = (bf16[256,256]{1,0:T(8,128)(2,1)}, bf16[256,256]{1,0:T(8,128)(2,1)S(1)}, u32[]{:S(2)}) copy-start(bf16[256,256]{1,0:T(8,128)(2,1)S(1)} %tile.77) | copy-start | bytes 393220
  129.5 47.3 %copy-start.39 = (bf16[256,256]{1,0:T(8,128)(2,1)}, bf16[256,256]{1,0:T(8,128)(2,1)S(1)}, u32[]{:S(2)}) copy-start(bf16[256,256]{1,0:T(8,128)(2,1)S(1)} %tile.74) | copy-start | bytes 393220
  129.9 50.0 %copy-start.21 = (bf16[512,256]{0,1:T(8,128)(2,1)}, bf16[512,256]{0,1:T(8,128)(2,1)S(1)}, u32[]{:S(2)}) copy-start(bf16[512,256]{0,1:T(8,128)(2,1)S(1)} %get-tuple-element.130) | copy-start | bytes 786436
  130.9 45.9 %copy-start = (bf16[512,1536]{0,1:T(8,128)(2,1)}, bf16[512,1536]{0,1:T(8,128)(2,1)S(1)}, u32[]{:S(2)}) copy-start(bf16[512,1536]{0,1:T(8,128)(2,1)S(1)} %get-tuple-element.131) | copy-start | bytes 4718596
  157.3 21.9 %copy-start.89 = (f32[512]{0:T(512)}, f32[512]{0:T(512)S(1)}, u32[]{:S(2)}) copy-start(f32[512]{0:T(512)S(1)} %get-tuple-element.110) | copy-start | bytes 6148
  157.3 21.9 %copy-start.93 = (f32[512]{0:T(512)}, f32[512]{0:T(512)S(1)}, u32[]{:S(2)}) copy-start(f32[512]{0:T(512)S(1)} %get-tuple-element.109) | copy-start | bytes 6148
  157.4 21.9 %copy-start.91 = (f32[512]{0:T(512)}, f32[512]{0:T(512)S(1)}, u32[]{:S(2)}) copy-start(f32[512]{0:T(512)S(1)} %get-tuple-element.112) | copy-start | bytes 6148
  157.4 21.9 %copy-start.95 = (f32[512]{0:T(512)}, f32[512]{0:T(512)S(1)}, u32[]{:S(2)}) copy-start(f32[512]{0:T(512)S(1)} %get-tuple-element.111) | copy-start | bytes 6148
  157.9 21.3 %copy-start.76 = (f32[512]{0:T(512)}, f32[512]{0:T(512)S(1)}, u32[]{:S(2)}) copy-start(f32[512]{0:T(512)S(1)} %get-tuple-element.39) | copy-start | bytes 6148
  157.9 21.4 %copy-start.78 = (f32[512]{0:T(512)}, f32[512]{0:T(512)S(1)}, u32[]{:S(2)}) copy-start(f32[512]{0:T(512)S(1)} %get-tuple-element.40) | copy-start | bytes 6148
  180.3 44.0 %copy-start.105 = (f32[512]{0:T(512)S(1)}, f32[512]{0:T(512)}, u32[]{:S(2)}) copy-start(f32[512]{0:T(512)} %get-tuple-element.119) | copy-start | bytes 6148
  180.3 44.0 %copy-start.107 = (f32[512]{0:T(512)S(1)}, f32[512]{0:T(512)}, u32[]{:S(2)}) copy-start(f32[512]{0:T(512)} %get-tuple-element.120) | copy-start | bytes 6148
  180.3 44.0 %copy-start.117 = (f32[1,2,2,128]{3,1,2,0:T(2,128)S(1)}, f32[1,2,2,128]{3,1,2,0:T(2,128)}, u32[]{:S(2)}) copy-start(f32[1,2,2,128]{3,1,2,0:T(2,128)} %copy.163) | copy-start | bytes 6148
  180.3 44.0 %copy-start.119 = (f32[1,2,2,128]{3,1,2,0:T(2,128)S(1)}, f32[1,2,2,128]{3,1,2,0:T(2,128)}, u32[]{:S(2)}) copy-start(f32[1,2,2,128]{3,1,2,0:T(2,128)} %copy.164) | copy-start | bytes 6148
  180.3 44.0 %copy-start.129 = (f32[8,1,256]{2,1,0:T(1,128)S(1)}, f32[8,1,256]{2,1,0:T(1,128)}, u32[]{:S(2)}) copy-start(f32[8,1,256]{2,1,0:T(1,128)} %convert_element_type.230) | copy-start | bytes 24580
  188.2 164.9 %copy-start.72 = (f32[1,1,512]{2,1,0:T(1,128)}, f32[1,1,512]{2,1,0:T(1,128)S(1)}, u32[]{:S(2)}) copy-start(f32[1,1,512]{2,1,0:T(1,128)S(1)} %get-tuple-element.95) | copy-start | bytes 6148
  188.2 164.9 %copy-start.73 = (f32[1,1,512]{2,1,0:T(1,128)}, f32[1,1,512]{2,1,0:T(1,128)S(1)}, u32[]{:S(2)}) copy-start(f32[1,1,512]{2,1,0:T(1,128)S(1)} %get-tuple-element.97) | copy-start | bytes 6148
  188.2 173.6 %copy-start.70 = (f32[512]{0:T(512)}, f32[512]{0:T(512)S(1)}, u32[]{:S(2)}) copy-start(f32[512]{0:T(512)S(1)} %add_rsqrt_fusion.1) | copy-start | bytes 6148
  188.2 172.9 %copy-start.68 = (f32[512]{0:T(512)}, f32[512]{0:T(512)S(1)}, u32[]{:S(2)}) copy-start(f32[512]{0:T(512)S(1)} %add_rsqrt_fusion) | copy-start | bytes 6148
  276.6 70.2 %all-gather.16.cloned.1.call-start = ((), (), s32[]{:S(2)}) async-start(), calls=%async_computation.13 | async-start | bytes 2359296 | tf_op jit(solution)/shard_map/all_gather | solution.py:223
  318.7 100.6 %all-reduce.14.cloned.1.call-start = ((), (), s32[]{:S(2)}) async-start(), calls=%async_computation.14 | async-start | bytes 4194304 | tf_op jit(solution)/shard_map/psum | solution.py:265
  367.7 51.7 %copy-start.81 = (f32[512]{0:T(512)S(1)}, f32[512]{0:T(512)}, u32[]{:S(2)}) copy-start(f32[512]{0:T(512)} %get-tuple-element.52) | copy-start | bytes 6148
  367.7 51.7 %copy-start.83 = (f32[512]{0:T(512)S(1)}, f32[512]{0:T(512)}, u32[]{:S(2)}) copy-start(f32[512]{0:T(512)} %get-tuple-element.50) | copy-start | bytes 6148
  367.7 130.7 %reduce-scatter.8.cloned.1.call-start = ((), (), s32[]{:S(2)}) async-start(), calls=%async_computation.15 | async-start | bytes 2359296 | tf_op jit(solution)/shard_map/reduce_scatter | solution.py:324
  456.9 117.8 %reduce-scatter.14.cloned.1.call-start = ((), (), s32[]{:S(2)}) async-start(), calls=%async_computation.19 | async-start | bytes 2621440 | tf_op jit(solution)/shard_map/reduce_scatter | solution.py:228
  464.1 125.7 %all-reduce.16.cloned.1.call-start = ((), (), s32[]{:S(2)}) async-start(), calls=%async_computation.16 | async-start | bytes 180224 | tf_op jit(solution)/shard_map/psum | solution.py:352
  476.0 22.4 %copy-start.17 = (bf16[512,640]{0,1:T(8,128)(2,1)S(1)}, bf16[512,640]{0,1:T(8,128)(2,1)}, u32[]{:S(2)}) copy-start(bf16[512,640]{0,1:T(8,128)(2,1)} %copy-done.16) | copy-start | bytes 1966084
  476.0 22.4 %copy-start.46 = (bf16[512,256]{0,1:T(8,128)(2,1)S(1)}, bf16[512,256]{0,1:T(8,128)(2,1)}, u32[]{:S(2)}) copy-start(bf16[512,256]{0,1:T(8,128)(2,1)} %get-tuple-element.55) | copy-start | bytes 786436
  476.0 22.4 %copy-start.106 = (f32[512]{0:T(512)S(1)}, f32[512]{0:T(512)}, u32[]{:S(2)}) copy-start(f32[512]{0:T(512)} %get-tuple-element.119) | copy-start | bytes 6148
  476.0 22.4 %copy-start.108 = (f32[512]{0:T(512)S(1)}, f32[512]{0:T(512)}, u32[]{:S(2)}) copy-start(f32[512]{0:T(512)} %get-tuple-element.120) | copy-start | bytes 6148
  480.0 21.2 %copy-start.130 = (f32[8,1,256]{2,1,0:T(1,128)S(1)}, f32[8,1,256]{2,1,0:T(1,128)}, u32[]{:S(2)}) copy-start(f32[8,1,256]{2,1,0:T(1,128)} %convert_element_type.230) | copy-start | bytes 24580
  501.1 135.3 %reduce-scatter.12.cloned.1.call-start = ((), (), s32[]{:S(2)}) async-start(), calls=%async_computation.18 | async-start | bytes 2621440 | tf_op jit(solution)/shard_map/reduce_scatter | solution.py:236
  505.5 176.5 %reduce-scatter.10.cloned.1.call-start = ((), (), s32[]{:S(2)}) async-start(), calls=%async_computation.17 | async-start | bytes 2621440 | tf_op jit(solution)/shard_map/reduce_scatter | solution.py:322
  510.8 20.6 %copy-start.138 = (pred[512]{0:T(512)(128)(4,1)S(1)}, pred[512]{0:T(512)(128)(4,1)}, u32[]{:S(2)}) copy-start(pred[512]{0:T(512)(128)(4,1)} %get-tuple-element.115) | copy-start | bytes 1540
  524.8 74.3 %copy-start.145 = (s32[512]{0:T(512)S(1)}, s32[512]{0:T(512)}, u32[]{:S(2)}) copy-start(s32[512]{0:T(512)} %copy-done.144) | copy-start | bytes 6148
  526.1 73.0 %all-to-all-start.1 = ((bf16[4,128,512]{2,1,0:T(8,128)(2,1)}), bf16[4,128,512]{2,1,0:T(8,128)(2,1)S(1)}, u32[]{:S(2)}, u32[]{:S(2)}) async-start(bf16[4,128,512]{2,1,0:T(8,128)(2,1)} %bitcast.63), calls=%async_computation.3 | async-start | bytes 1048576 | tf_op jit(solution)/shard_map/all_to_all | solution.py:338
  (123 other events, 417.9 us)
Sparse Core Ops, SparseCore 0:
  38.3 27.0 all-gather.7
  67.5 45.9 all-gather.9
  126.5 50.3 all-reduce.11
  178.3 45.9 all-gather.11
  225.8 44.6 all-gather.13
  276.7 39.9 reduce-scatter.5
  318.8 27.8 all-gather.15
  367.8 51.4 all-reduce.13
  457.0 41.3 reduce-scatter.7
  500.6 50.8 reduce-scatter.13
  554.5 35.2 all-reduce.15
  592.5 43.8 reduce-scatter.11
  638.8 43.1 reduce-scatter.9

commit v2 on v1

v2 whole, which is shorter than its diff:
```python
import itertools
import types

import jax
import jax.numpy as jnp
from jax import lax
from jax.experimental import pallas as pl
from jax.experimental.pallas import tpu as pltpu
from jax.sharding import PartitionSpec as P

NEG_FILL = -1e30
EPSILON = 1e-05
BF = jnp.bfloat16
F32 = jnp.float32
MESH = pl.DeviceIdType.MESH
VMEM_LIMIT = 60 * 1024 * 1024
LINE = 128
BAND = 2


def mm(a, b):
    return jnp.dot(a, b, preferred_element_type=F32)


def mm_nt(a, b):
    return lax.dot_general(a, b, (((1,), (1,)), ((), ())), preferred_element_type=F32)


def mm_tn(a, b):
    return lax.dot_general(a, b, (((0,), (0,)), ((), ())), preferred_element_type=F32)


def split(v):
    high = v.astype(BF)
    return high, (v - high.astype(F32)).astype(BF)


def sigmoid(v):
    return 1.0 / (1.0 + jnp.exp(-v))


class Links:
    def __init__(self, send, recv, limit):
        self.send, self.recv, self.limit, self.all = send, recv, limit, []
        self.closed = 0

    def go(self, src, dst, peer):
        k = len(self.all)
        assert k < self.limit
        copy = pltpu.make_async_remote_copy(
            src_ref=src,
            dst_ref=dst,
            send_sem=self.send.at[k],
            recv_sem=self.recv.at[k],
            device_id=peer,
            device_id_type=MESH,
        )
        copy.start()
        self.all.append(copy)
        return copy

    def close(self):
        for copy in self.all[self.closed :]:
            copy.wait_send()
        self.closed = len(self.all)


class Ring:
    def __init__(self, links, own, hold, next_peer, owners):
        self.links, self.own, self.hold = links, own, hold
        self.peer, self.owners = next_peer, owners
        self.flying, self.at = None, 0

    def start(self):
        source = self.own if self.at == 0 else self.hold.at[self.owners[self.at]]
        self.flying = self.links.go(source, self.hold.at[self.owners[self.at]], self.peer)

    def step(self):
        if self.at >= len(self.owners) - 1:
            return False
        if self.flying is None:
            self.start()
        self.flying.wait_recv()
        self.at += 1
        self.flying = None
        if self.at < len(self.owners) - 1:
            self.start()
            return True
        return False

    def finish(self):
        while self.step():
            pass


def coordinates(dp_count):
    z, t, c = lax.axis_index("dp"), lax.axis_index("tensor"), lax.axis_index("ctx")
    core = lax.rem(t, 2)
    m = types.SimpleNamespace(z=z, t=t, c=c, core=core, y=lax.div(t, 2))
    m.sib_t, m.far_t, m.other_c = t + 1 - 2 * core, lax.rem(t + 2, 4), 1 - c
    m.sib, m.yn, m.xn = (z, m.sib_t, c), (z, m.far_t, c), (z, t, m.other_c)
    m.slot = t * 2 + c
    m.slot_x, m.slot_y, m.slot_d = t * 2 + m.other_c, m.far_t * 2 + c, m.far_t * 2 + m.other_c
    m.to_sib = 2 - 4 * core
    if dp_count == 4:
        def after(v):
            return lax.rem(2 * v + 1, 5)

        def before(v):
            return lax.rem(3 * v + 2, 5)
    else:
        def after(v):
            return lax.rem(v + 1, dp_count)

        def before(v):
            return lax.rem(v + dp_count - 1, dp_count)

    m.ring_next = (after(z), t, c)
    m.owners = [z]
    for _ in range(dp_count - 1):
        m.owners.append(before(m.owners[-1]))
    m.dp_peers = [(lax.rem(z + d, dp_count), t, c) for d in range(1, dp_count)]
    m.plane_peers = [
        (z, lax.rem(t + dt, 4), lax.rem(c + dc, 2))
        for dt in range(4)
        for dc in range(2)
        if dt or dc
    ]
    m.tensor_peers = [(z, lax.rem(t + dt, 4), c) for dt in range(1, 4)]
    return m


def plane_gather(links, m, full, rows):
    half = rows // 2
    first, second = pl.ds(0, half), pl.ds(half, half)

    def send(slot, part, peer):
        return links.go(full.at[slot, part], full.at[slot, part], peer)

    x_first = send(m.slot, first, m.xn)
    y_second = send(m.slot, second, m.yn)
    to_sib = links.go(full.at[m.slot], full.at[m.slot], m.sib)
    x_second = send(m.slot, second, m.xn)
    y_first = send(m.slot, first, m.yn)
    yield m.slot
    to_sib.wait_recv()
    yield m.slot + m.to_sib
    x_first.wait_recv()
    d_first = send(m.slot_x, first, m.yn)
    y_second.wait_recv()
    d_second = send(m.slot_y, second, m.xn)
    x_second.wait_recv()
    sib_x = links.go(full.at[m.slot_x], full.at[m.slot_x], m.sib)
    yield m.slot_x
    y_first.wait_recv()
    sib_y = links.go(full.at[m.slot_y], full.at[m.slot_y], m.sib)
    yield m.slot_y
    sib_x.wait_recv()
    yield m.slot_x + m.to_sib
    d_first.wait_recv()
    d_second.wait_recv()
    sib_d = links.go(full.at[m.slot_d], full.at[m.slot_d], m.sib)
    yield m.slot_d
    sib_y.wait_recv()
    yield m.slot_y + m.to_sib
    sib_d.wait_recv()
    yield m.slot_d + m.to_sib


def to_lanes(columns, rows):
    lane = lax.broadcasted_iota(jnp.int32, (rows, 128), 1)
    out = jnp.zeros((rows, 128), F32)
    for j, column in enumerate(columns):
        out = jnp.where(lane == j, column, out)
    return out.T[:8]


def to_columns(lines):
    rows = lines.shape[1]
    return jnp.concatenate([lines, jnp.zeros((120, rows), F32)], axis=0).T


def push_sum(links, m, lines, box, peers, own_place, count):
    box[own_place] = lines
    copies = [links.go(box.at[own_place], box.at[own_place], peer) for peer in peers]

    def finish():
        for copy in copies:
            copy.wait_recv()
        total = box[0]
        for k in range(1, count):
            total = total + box[k]
        return total

    return finish


def prefix_lanes(v):
    width = v.shape[1]
    lane = lax.broadcasted_iota(jnp.int32, v.shape, 1)
    step = 1
    while step < width:
        v = v + jnp.where(lane >= step, pltpu.roll(v, step, 1), 0.0)
        step *= 2
    return v


def band(rows):
    out, at = [], 0
    for i in range(rows // LINE):
        low = max(0, i - BAND)
        out.append((i, low, at, i - low + 1))
        at += i - low + 1
    return out, at


def wide(ref, h, at, width):
    return jnp.concatenate([ref[h, at + k] for k in range(width)], axis=1)


def plane_scatter(links, m, part, b, rows):
    half = rows // 2
    first, second = pl.ds(0, half), pl.ds(half, half)
    own_k = m.y * 2 + m.c
    far_y = 1 - m.y
    copies = []
    for k in range(4):
        b.out[k] = part(k // 2, 1 - m.core, k % 2).astype(BF)
        copies.append(links.go(b.out.at[k], b.into.at[k], m.sib))
    for k in range(4):
        b.acc[k] = part(k // 2, m.core, k % 2)
    for k in range(4):
        copies[k].wait_recv()
        b.acc[k] += b.into[k].astype(F32)
    copies = []
    for y in range(2):
        b.small_out[y] = b.acc[y * 2 + m.other_c, first].astype(BF)
        copies.append(links.go(b.small_out.at[y], b.small_in.at[y], m.xn))
    for x in range(2):
        b.small_out[2 + x] = b.acc[far_y * 2 + x, second].astype(BF)
        copies.append(links.go(b.small_out.at[2 + x], b.small_in.at[2 + x], m.yn))
    for k in range(4):
        copies[k].wait_recv()
    for y in range(2):
        b.acc[y * 2 + m.c, first] += b.small_in[y].astype(F32)
    for x in range(2):
        b.acc[m.y * 2 + x, second] += b.small_in[2 + x].astype(F32)
    b.small_out[4] = b.acc[far_y * 2 + m.c, first].astype(BF)
    to_y = links.go(b.small_out.at[4], b.small_in.at[4], m.yn)
    b.small_out[5] = b.acc[m.y * 2 + m.other_c, second].astype(BF)
    to_x = links.go(b.small_out.at[5], b.small_in.at[5], m.xn)
    to_y.wait_recv()
    to_x.wait_recv()
    b.acc[own_k, first] += b.small_in[4].astype(F32)
    b.acc[own_k, second] += b.small_in[5].astype(F32)
    return own_k


def forward(b, m, links, shape):
    rows, local, chan, n_dp, block, wide_d = shape
    cap, heads = rows // n_dp, local // chan
    width = 8 * wide_d
    scale = (4 * chan) ** -0.5
    blocks, n_blocks = band(rows)
    low_rows = pl.ds(0, rows)

    partners = m.plane_peers + m.dp_peers
    barrier = pltpu.get_barrier_semaphore()
    for peer in partners:
        pl.semaphore_signal(barrier, inc=1, device_id=peer, device_id_type=MESH)
    sent = mm(b.send_map[...], b.payload[...]).astype(BF)
    b.sent_tokens[...] = sent[:, :wide_d]
    b.sent_rest[...] = sent[:, wide_d:]
    own_place = pl.ds(pl.multiple_of(m.z * cap, 16), cap)
    b.full[m.slot, own_place] = b.sent_tokens[own_place]
    b.rest[own_place] = b.sent_rest[own_place]
    b.gains[m.slot] = b.ln8[...]
    b.up_cell[m.z] = b.own_cell[...]
    b.up_gate[m.z] = b.own_gate[...]
    b.down[m.z] = b.own_down[...]
    pl.semaphore_wait(barrier, len(partners))

    cell = Ring(links, b.own_cell, b.up_cell, m.ring_next, m.owners)
    gate = Ring(links, b.own_gate, b.up_gate, m.ring_next, m.owners)
    down = Ring(links, b.own_down, b.down, m.ring_next, m.owners)
    a2a, a2a_rest = [], []
    for d, peer in enumerate(m.dp_peers):
        place = pl.ds(pl.multiple_of(lax.rem(m.z + d + 1, n_dp) * cap, 16), cap)
        a2a.append(links.go(b.sent_tokens.at[place], b.full.at[m.slot, own_place], peer))
    cell.start()
    gain_copies = [
        links.go(b.gains.at[m.slot], b.gains.at[m.slot], peer) for peer in m.plane_peers
    ]
    for d, peer in enumerate(m.dp_peers):
        place = pl.ds(pl.multiple_of(lax.rem(m.z + d + 1, n_dp) * cap, 16), cap)
        a2a_rest.append(links.go(b.sent_rest.at[place], b.rest.at[own_place], peer))
    for copy in a2a:
        copy.wait_recv()

    b.sums[...] = jnp.zeros((rows, 128), F32)
    b.squares[...] = jnp.zeros((rows, 128), F32)
    arrivals = 0
    for slot in plane_gather(links, m, b.full, rows):
        columns = pl.ds(pl.multiple_of(slot * wide_d, 128), wide_d)

        def place_rows(r, carry, slot=slot, columns=columns):
            at = pl.ds(pl.multiple_of(r * LINE, LINE), LINE)
            x = mm(b.recv_map[at], b.full[slot])
            b.x_full[at, columns] = x.astype(BF)
            b.sums[at] += jnp.sum(x, axis=1, keepdims=True)
            b.squares[at] += jnp.sum(x * x, axis=1, keepdims=True)
            return carry

        lax.fori_loop(0, rows // LINE, place_rows, 0)
        arrivals += 1
        if arrivals in (3, 6):
            cell.step()
    for copy in gain_copies:
        copy.wait_recv()

    def normalise(r, carry):
        at = pl.ds(pl.multiple_of(r * 64, 64), 64)
        mean = b.sums[at][:, :1] / width
        var = b.squares[at][:, :1] / width - mean * mean
        rstd = lax.rsqrt(var + EPSILON)
        b.mean[at] = jnp.broadcast_to(mean, (64, 128))
        b.rstd[at] = jnp.broadcast_to(rstd, (64, 128))
        for i in range(8):
            x = b.x_full[at, i * wide_d : (i + 1) * wide_d].astype(F32)
            x = (x - mean) * rstd * b.gains[i, :1]
            b.normed[at, i * wide_d : (i + 1) * wide_d] = x.astype(BF)
        return carry

    lax.fori_loop(0, rows // 64, normalise, 0)

    def project(hold, ring, target):
        for s in range(n_dp):
            if s:
                while ring.at < s:
                    ring.step()
            owner = m.owners[s]
            columns = pl.ds(pl.multiple_of(owner * block, 128), block)
            product = mm(b.normed[:, columns], hold[owner])
            target[...] = product if s == 0 else target[...] + product

    project(b.up_cell, cell, b.wide_f)
    links.close()
    gate.start()
    down.start()

    place = lax.broadcasted_iota(jnp.int32, (rows, 1), 0)
    ends, total = [], 0
    for k in range(b.lengths.shape[1]):
        total = total + b.lengths[m.z, k]
        ends.append(total)
    begin = jnp.zeros((rows, 1), jnp.int32)
    for end in ends:
        begin = jnp.where(place >= end, end, begin)
    b.begin[...] = jnp.broadcast_to(begin, (rows, 128))

    def convolve(i, carry):
        at = pl.ds(pl.multiple_of(i * 128, 128), 128)
        low = b.wide_f[:, at].astype(BF)
        b.branch[:, at] = low
        x = low.astype(F32)
        since = lax.broadcasted_iota(jnp.int32, (rows, 128), 0) - b.begin[...]
        conv = b.chan_params[4:5, at] + b.chan_params[0:1, at] * x
        for j in range(1, 4):
            back = b.chan_params[j : j + 1, at] * pltpu.roll(x, j, 0)
            conv = conv + jnp.where(since >= j, back, 0.0)
        sig = sigmoid(conv)
        act = conv * sig
        b.act[:, at] = act
        b.slope[:, at] = sig + act * (1.0 - sig)
        return carry

    lax.fori_loop(0, local // 128, convolve, 0)
    r_map = lax.broadcasted_iota(jnp.int32, (chan, chan), 0) // 4
    c_map = lax.broadcasted_iota(jnp.int32, (chan, chan), 1) // 4
    same = r_map == c_map
    for s in range(3):
        for h in range(heads):
            base = b.maps8[s, h]
            dense = jnp.broadcast_to(base[None], (chan // 8, 8, chan)).reshape(chan, chan)
            b.maps[s, h] = jnp.where(same, dense, 0.0).astype(BF)
    for h in range(heads):
        at = slice(h * chan, (h + 1) * chan)
        high, rest = split(b.act[:, at])
        for s in range(2):
            b.qkv[:, s * local + h * chan : s * local + (h + 1) * chan] = (
                mm(high, b.maps[s, h]) + mm(rest, b.maps[s, h])
            ).astype(BF)
        b.qkv[:, 2 * local + h * chan : 2 * local + (h + 1) * chan] = mm(
            b.branch[:, at], b.maps[2, h]
        ).astype(BF)

    pre_part = mm_nt(b.gates_w[...], b.qkv[...])[:8]
    pre_sum = push_sum(links, m, pre_part, b.pre_box, m.plane_peers, m.slot, 8)

    def q_of(h, i):
        return b.qkv[i * LINE : (i + 1) * LINE, h * chan : (h + 1) * chan]

    def k_of(h, low, n):
        return b.qkv[
            low * LINE : (low + n) * LINE, local + h * chan : local + (h + 1) * chan
        ]

    def v_of(h, low, n):
        return b.qkv[
            low * LINE : (low + n) * LINE, 2 * local + h * chan : 2 * local + (h + 1) * chan
        ]

    b.of = (q_of, k_of, v_of)
    for h in range(heads):
        for i, low, at, n in blocks:
            tile = mm_nt(q_of(h, i), k_of(h, low, n))
            for k in range(n):
                b.score_part[h, at + k] = tile[:, k * LINE : (k + 1) * LINE]
    other = links.go(b.score_part.at[1 - m.core], b.score_in.at[0], m.sib)
    other.wait_recv()
    b.score_sum[0] = b.score_part[m.core] + b.score_in[0]
    far = links.go(b.score_sum.at[0], b.score_in.at[1], m.yn)

    pre = pre_sum() + b.gate_bias[:, :1]
    b.pre[...] = pre
    line8 = lax.broadcasted_iota(jnp.int32, (8, rows), 0)
    head = m.c * heads + m.core
    in_gate = jnp.sum(jnp.where(line8 == head, pre, 0.0), axis=0, keepdims=True)
    forget = jnp.sum(jnp.where(line8 == head + 4, pre, 0.0), axis=0, keepdims=True)
    log_forget = jnp.minimum(forget, 0.0) - jnp.log(1.0 + jnp.exp(-jnp.abs(forget)))
    rising = prefix_lanes(jnp.broadcast_to(log_forget, (8, rows)))
    rise_col = to_columns(rising)
    gate_line = in_gate - rising[:1]
    gate.step()
    far.wait_recv()
    b.score_sum[1] = b.score_sum[0] + b.score_in[1]
    for i, low, at, n in blocks:
        lines = slice(i * LINE, (i + 1) * LINE)
        t_at = i * LINE + lax.broadcasted_iota(jnp.int32, (LINE, n * LINE), 0)
        s_at = low * LINE + lax.broadcasted_iota(jnp.int32, (LINE, n * LINE), 1)
        allowed = (s_at <= t_at) & (s_at >= b.begin[lines][:, :1])
        logit = jnp.where(
            allowed, rise_col[lines][:, :1] + gate_line[:, low * LINE : (low + n) * LINE], NEG_FILL
        )
        top = jnp.max(logit, axis=1, keepdims=True)
        decay = jnp.where(allowed, jnp.exp(logit - top), 0.0) * scale
        weight = wide(b.score_sum, 1, at, n) * decay
        den = jnp.sum(weight, axis=1, keepdims=True)
        floor = jnp.exp(-top)
        inv = 1.0 / jnp.maximum(jnp.abs(den), floor)
        shares = (weight * inv).astype(BF)
        b.inv[lines] = jnp.broadcast_to(inv, (LINE, 128))
        sign = jnp.where(jnp.abs(den) > floor, jnp.where(den > 0.0, 1.0, -1.0), 0.0)
        b.sign[lines] = jnp.broadcast_to(sign, (LINE, 128))
        for k in range(n):
            b.decay[at + k] = decay[:, k * LINE : (k + 1) * LINE]
            b.weight[at + k] = weight[:, k * LINE : (k + 1) * LINE]
            b.share[m.core, at + k] = shares[:, k * LINE : (k + 1) * LINE]
    shared = links.go(b.share.at[m.core], b.share.at[m.core], m.sib)
    gate.step()
    shared.wait_recv()
    columns = []
    for h in range(heads):
        for i, low, at, n in blocks:
            lines = slice(i * LINE, (i + 1) * LINE)
            b.hidden[lines, h * chan : (h + 1) * chan] = mm(
                wide(b.share, h, at, n), v_of(h, low, n)
            )
        hid = b.hidden[:, h * chan : (h + 1) * chan]
        columns.append(jnp.sum(hid, axis=1, keepdims=True))
        columns.append(jnp.sum(hid * hid, axis=1, keepdims=True))
    moment_sum = push_sum(
        links, m, to_lanes(columns, rows), b.moment_box, m.tensor_peers, m.t, 4
    )
    gate.finish()
    down.step()
    project(b.up_gate, gate, b.wide_f)
    moments = to_columns(moment_sum()) / (4 * chan)
    for h in range(heads):
        mean = moments[:, 2 * h : 2 * h + 1]
        rstd = lax.rsqrt(moments[:, 2 * h + 1 : 2 * h + 2] - mean * mean + EPSILON)
        b.head_rstd[h] = jnp.broadcast_to(rstd, (rows, 128))
        b.head_mean[h] = jnp.broadcast_to(mean, (rows, 128))
    down.step()

    def mix(i, carry):
        at = pl.ds(pl.multiple_of(i * 128, 128), 128)
        h = lax.div(i, chan // 128)
        hat = (b.hidden[:, at] - b.head_mean[h]) * b.head_rstd[h]
        b.hidden[:, at] = hat
        low = b.wide_f[:, at].astype(BF)
        b.gate_low[:, at] = low
        g = low.astype(F32)
        inner = hat * b.chan_params[5:6, at] + b.chan_params[6:7, at] * b.act[:, at]
        b.mixed[:, at] = (inner * (g * sigmoid(g))).astype(BF)
        return carry

    lax.fori_loop(0, local // 128, mix, 0)
    down.finish()
    piece = min(block, wide_d)

    def down_part(y, core, x):
        slot = (y * 2 + core) * 2 + x
        parts = []
        for k in range(wide_d // piece):
            if block >= 2 * wide_d:
                owner = lax.div((y * 2 + core) * 2 * wide_d, block)
                parts.append(mm(b.mixed[...], b.down[owner, :, x * wide_d : (x + 1) * wide_d]))
            else:
                owner = lax.div(slot * wide_d, block) + k
                parts.append(mm(b.mixed[...], b.down[owner]))
        return jnp.concatenate(parts, axis=1)

    for copy in a2a_rest:
        copy.wait_recv()
    placed = mm(b.recv_map[...], b.rest[...])
    b.goal[...] = placed[:, :wide_d].astype(BF)
    keep = placed[:, wide_d : wide_d + 1] * (place < ends[-1]).astype(F32)
    count_part = jnp.broadcast_to(jnp.sum(keep, axis=0, keepdims=True), (8, 128))
    count_sum = push_sum(links, m, count_part, b.count_box, m.dp_peers, m.z, n_dp)
    own_k = plane_scatter(links, m, down_part, b, rows)
    count = count_sum()[:1, :1]
    own_columns = pl.ds(pl.multiple_of(m.slot * wide_d, 128), wide_d)
    result = (b.x_full[:, own_columns].astype(F32) + b.acc[own_k]).astype(BF)
    difference = result.astype(F32) - b.goal[...].astype(F32)
    per_row = jnp.sum(difference * difference, axis=1, keepdims=True)
    loss_part = jnp.sum(keep * 0.5 * per_row, axis=0, keepdims=True) / count
    b.loss_part[...] = jnp.broadcast_to(loss_part, (8, 128))
    own_gradient = ((rows * n_dp) / count * keep * difference).astype(BF)
    b.own_gradient[...] = own_gradient
    links.close()
    b.full[m.slot] = own_gradient
    b.arriving = plane_gather(links, m, b.full, rows)
    next_slot = next(b.arriving)

    b.sent_out[...] = mm_tn(b.recv_map[...], result).astype(BF)
    b.home_out[own_place] = b.sent_out[own_place]
    b.home_copies = []
    for d, peer in enumerate(m.dp_peers):
        place = pl.ds(pl.multiple_of(lax.rem(m.z + d + 1, n_dp) * cap, 16), cap)
        b.home_copies.append(links.go(b.sent_out.at[place], b.home_out.at[own_place], peer))
    b.arriving = itertools.chain([next_slot], b.arriving)


class RingSum:
    def __init__(self, links, part, hold, target, peer, owners):
        self.links, self.part, self.hold, self.target = links, part, hold, target
        self.peer, self.owners, self.at = peer, owners, 0
        self.flying = None

    def start(self):
        self.hold[0] = self.part(self.owners[1]).astype(BF)
        self.flying = self.links.go(self.hold.at[0], self.hold.at[1], self.peer)

    def step(self):
        if self.at >= len(self.owners) - 1:
            return False
        if self.flying is None:
            self.start()
        own = self.part(self.owners[(self.at + 2) % len(self.owners)])
        self.flying.wait_recv()
        self.at += 1
        total = own + self.hold[self.at].astype(F32)
        if self.at == len(self.owners) - 1:
            self.target(total)
            return False
        self.hold[self.at] = total.astype(BF)
        self.flying = self.links.go(
            self.hold.at[self.at], self.hold.at[self.at + 1], self.peer
        )
        return True

    def finish(self):
        while self.step():
            pass


def backward(b, m, links, shape):
    rows, local, chan, n_dp, block, wide_d = shape
    cap, heads = rows // n_dp, local // chan
    all_heads = 2 * heads
    width, head_width = 8 * wide_d, 4 * chan
    blocks, n_blocks = band(rows)
    q_of, k_of, v_of = b.of
    line8 = lax.broadcasted_iota(jnp.int32, (8, rows), 0)
    head = m.c * heads + m.core

    seen = 0
    for slot in b.arriving:
        g = b.full[slot]
        if block >= wide_d:
            ratio = block // wide_d
            at = pl.ds(pl.multiple_of(lax.rem(slot, ratio) * wide_d, 128), wide_d)
            product = mm_nt(g, b.down[lax.div(slot, ratio), :, at])
        else:
            ratio = wide_d // block
            product = sum(
                mm_nt(g[:, k * block : (k + 1) * block], b.down[slot * ratio + k])
                for k in range(ratio)
            )
        b.wide_f[...] = product if seen == 0 else b.wide_f[...] + product
        seen += 1

    def down_grad(owner):
        if block >= wide_d:
            ratio = block // wide_d
            return jnp.concatenate(
                [mm_tn(b.mixed[...], b.full[owner * ratio + k]) for k in range(ratio)], axis=1
            )
        ratio = wide_d // block
        at = pl.ds(pl.multiple_of(lax.rem(owner, ratio) * block, 128), block)
        return mm_tn(b.mixed[...], b.full[lax.div(owner, ratio), :, at])

    def up_grad(grads):
        def part(owner):
            at = pl.ds(pl.multiple_of(owner * block, 128), block)
            return mm_tn(b.normed[:, at], grads[...])

        return part

    def keep_down(total):
        b.grad_down[...] = total

    def keep_gate(total):
        b.grad_up[:, local:] = total

    def keep_cell(total):
        b.grad_up[:, :local] = total

    ring_down = RingSum(links, down_grad, b.ring_down, keep_down, m.ring_next, m.owners)
    ring_gate = RingSum(links, up_grad(b.g_gate), b.ring_gate, keep_gate, m.ring_next, m.owners)
    ring_cell = RingSum(links, up_grad(b.g_cell), b.ring_cell, keep_cell, m.ring_next, m.owners)
    ring_down.start()

    def unmix(i, carry):
        at = pl.ds(pl.multiple_of(i * 128, 128), 128)
        gm = b.wide_f[:, at]
        g = b.gate_low[:, at].astype(F32)
        sig = sigmoid(g)
        silu = g * sig
        hat, act = b.hidden[:, at], b.act[:, at]
        group, skip = b.chan_params[5:6, at], b.chan_params[6:7, at]
        inner = hat * group + skip * act
        b.g_gate[:, at] = (gm * inner * (sig + silu * (1.0 - sig))).astype(BF)
        gi = gm * silu
        b.small[5:6, at] = jnp.sum(gi * hat, axis=0, keepdims=True)
        b.small[6:7, at] = jnp.sum(gi * act, axis=0, keepdims=True)
        b.g_act[:, at] = gi * skip
        b.wide_f[:, at] = gi * group
        return carry

    lax.fori_loop(0, local // 128, unmix, 0)
    columns = []
    for h in range(heads):
        u = b.wide_f[:, h * chan : (h + 1) * chan]
        columns.append(jnp.sum(u, axis=1, keepdims=True))
        columns.append(
            jnp.sum(u * b.hidden[:, h * chan : (h + 1) * chan], axis=1, keepdims=True)
        )
    u_sum = push_sum(links, m, to_lanes(columns, rows), b.u_box, m.tensor_peers, m.t, 4)
    u_moments = to_columns(u_sum())
    rhos = []
    for h in range(heads):
        at = slice(h * chan, (h + 1) * chan)
        rstd = b.head_rstd[h][:, :1]
        mean_u = u_moments[:, 2 * h : 2 * h + 1] / head_width
        sum_ux = u_moments[:, 2 * h + 1 : 2 * h + 2]
        d_hidden = rstd * (b.wide_f[:, at] - mean_u - b.hidden[:, at] * (sum_ux / head_width))
        b.d_hidden[:, at] = d_hidden.astype(BF)
        rhos.append(sum_ux * (EPSILON * rstd * rstd))
    rho = jnp.where(m.core == 0, rhos[0], rhos[1])
    for h in range(heads):
        for i, low, at, n in blocks:
            tile = mm_nt(
                b.d_hidden[i * LINE : (i + 1) * LINE, h * chan : (h + 1) * chan], v_of(h, low, n)
            )
            for k in range(n):
                b.score_part[h, at + k] = tile[:, k * LINE : (k + 1) * LINE]
    other = links.go(b.score_part.at[1 - m.core], b.score_in.at[0], m.sib)
    other.wait_recv()
    b.share_out[...] = (b.score_part[m.core] + b.score_in[0]).astype(BF)
    far = links.go(b.share_out, b.share_in, m.yn)
    ring_down.step()
    ring_gate.start()
    far.wait_recv()
    b.lines[...] = jnp.zeros((8, rows), F32)
    for i, low, at, n in blocks:
        lines = slice(i * LINE, (i + 1) * LINE)
        across = slice(low * LINE, (low + n) * LINE)

        def spread(ref):
            return jnp.concatenate([ref[at + k].astype(F32) for k in range(n)], axis=1)

        inv, sign, radial = b.inv[lines][:, :1], b.sign[lines][:, :1], rho[lines]
        weight = spread(b.weight)
        full = (spread(b.share_out) + spread(b.share_in)) * inv - sign * radial * inv
        exact = jnp.where(sign == 0.0, radial, 0.0)
        noisy = jnp.sum(full * weight, axis=1, keepdims=True)
        square = jnp.sum(weight * weight, axis=1, keepdims=True)
        full = full - weight * ((noisy - exact) / jnp.where(square > 0.0, square, 1.0))
        d_score = (full * spread(b.decay)).astype(BF)
        for k in range(n):
            b.d_score[m.core, at + k] = d_score[:, k * LINE : (k + 1) * LINE]
        b.lines[0:1, across] += jnp.sum(full * weight, axis=0, keepdims=True)
        b.exact[lines] = jnp.broadcast_to(exact, (LINE, 128))
    scored = links.go(b.d_score.at[m.core], b.d_score.at[m.core], m.sib)
    over_cols = b.lines[0:1]
    over_rows = b.exact[...].T[0:1]
    delta = jnp.broadcast_to(over_rows - over_cols, (8, rows))
    after = jnp.sum(delta, axis=1, keepdims=True) - prefix_lanes(delta) + delta
    forget = jnp.sum(jnp.where(line8 == head + all_heads, b.pre[...], 0.0), axis=0, keepdims=True)
    d_forget = after[:1] / (1.0 + jnp.exp(forget))
    own_lines = jnp.where(line8 == head, over_cols, 0.0) + jnp.where(
        line8 == head + all_heads, d_forget, 0.0
    )
    head_peers = [
        m.sib,
        m.xn,
        (m.z, m.sib_t, m.other_c),
    ]
    pre_sum = push_sum(links, m, own_lines, b.grad_box, head_peers, m.c * 2 + m.core, 4)

    for h in range(heads):
        at = slice(2 * local + h * chan, 2 * local + (h + 1) * chan)
        b.g_proj[:, at] = jnp.zeros((rows, chan), F32)
        for i, low, place, n in blocks:
            d_hid = b.d_hidden[i * LINE : (i + 1) * LINE, h * chan : (h + 1) * chan]
            b.g_proj[low * LINE : (low + n) * LINE, at] += mm_tn(wide(b.share, h, place, n), d_hid)
    ring_down.step()
    scored.wait_recv()
    for h in range(heads):
        at = slice(h * chan, (h + 1) * chan)
        k_at = slice(local + h * chan, local + (h + 1) * chan)
        b.g_proj[:, k_at] = jnp.zeros((rows, chan), F32)
        for i, low, place, n in blocks:
            tile = wide(b.d_score, h, place, n)
            b.g_proj[i * LINE : (i + 1) * LINE, at] = mm(tile, k_of(h, low, n))
            b.g_proj[low * LINE : (low + n) * LINE, k_at] += mm_tn(tile, q_of(h, i))
    pre_grad = pre_sum()
    pre16 = jnp.concatenate([pre_grad, jnp.zeros((8, rows), F32)], axis=0)
    high, rest = split(pre16)
    b.g_proj[...] += mm_tn(high, b.gates_w[...]) + mm_tn(rest, b.gates_w[...])
    gate_grad = (mm(high, b.qkv[...]) + mm(rest, b.qkv[...]))[:8]
    for s in range(3):
        b.small[8 * (s + 1) : 8 * (s + 2)] = gate_grad[:, s * local : (s + 1) * local]
    b.small[32:40] = jnp.broadcast_to(jnp.sum(pre_grad, axis=1, keepdims=True), (8, local))
    ring_down.finish()
    ring_gate.step()

    r_map = lax.broadcasted_iota(jnp.int32, (chan, chan), 0) // 4
    c_map = lax.broadcasted_iota(jnp.int32, (chan, chan), 1) // 4
    same = r_map == c_map
    for h in range(heads):
        at = slice(h * chan, (h + 1) * chan)
        act_low = b.act[:, at].astype(BF)
        extra = None
        for s in range(3):
            low = b.g_proj[:, s * local + h * chan : s * local + (h + 1) * chan].astype(BF)
            left = act_low if s < 2 else b.branch[:, at]
            dense = jnp.where(same, mm_tn(left, low), 0.0)
            folded = jnp.sum(dense.reshape(chan // 8, 8, chan), axis=0)
            b.small[40 + 8 * s : 48 + 8 * s, at] = folded
            back = mm_nt(low, b.maps[s, h])
            if s == 0:
                extra = back
            elif s == 1:
                b.g_act[:, at] += extra + back
            else:
                b.wide_f[:, at] = back

    def unconvolve(i, carry):
        at = pl.ds(pl.multiple_of(i * 128, 128), 128)
        since = lax.broadcasted_iota(jnp.int32, (rows, 128), 0) - b.begin[...]
        x = b.branch[:, at].astype(F32)
        gc = b.g_act[:, at] * b.slope[:, at]
        gb = b.wide_f[:, at] + b.chan_params[0:1, at] * gc
        b.small[0:1, at] = jnp.sum(gc * x, axis=0, keepdims=True)
        b.small[4:5, at] = jnp.sum(gc, axis=0, keepdims=True)
        for j in range(1, 4):
            kept = jnp.where(since >= j, gc, 0.0)
            gb = gb + b.chan_params[j : j + 1, at] * pltpu.roll(kept, rows - j, 0)
            b.small[j : j + 1, at] = jnp.sum(kept * pltpu.roll(x, j, 0), axis=0, keepdims=True)
        b.g_cell[:, at] = gb.astype(BF)
        return carry

    lax.fori_loop(0, local // 128, unconvolve, 0)
    ring_gate.step()
    ring_cell.start()

    def up_part(y, core, x):
        slot = (y * 2 + core) * 2 + x
        if block >= wide_d:
            ratio = block // wide_d
            at = pl.ds(pl.multiple_of(lax.rem(slot, ratio) * wide_d, 16), wide_d)
            owner = lax.div(slot, ratio)
            return mm_nt(b.g_cell[...], b.up_cell[owner, at]) + mm_nt(
                b.g_gate[...], b.up_gate[owner, at]
            )
        ratio = wide_d // block
        return jnp.concatenate(
            [
                mm_nt(b.g_cell[...], b.up_cell[slot * ratio + k])
                + mm_nt(b.g_gate[...], b.up_gate[slot * ratio + k])
                for k in range(ratio)
            ],
            axis=1,
        )

    own_k = plane_scatter(links, m, up_part, b, rows)
    ring_gate.finish()
    grad_normed = b.acc[own_k]
    own_columns = pl.ds(pl.multiple_of(m.slot * wide_d, 128), wide_d)
    x_hat = (b.x_full[:, own_columns].astype(F32) - b.mean[:, :1]) * b.rstd[:, :1]
    grad_scaled = grad_normed * b.ln8[:1]
    line_sum = push_sum(
        links,
        m,
        to_lanes(
            [
                jnp.sum(grad_scaled, axis=1, keepdims=True),
                jnp.sum(grad_scaled * x_hat, axis=1, keepdims=True),
            ],
            rows,
        ),
        b.line_box,
        m.plane_peers,
        m.slot,
        8,
    )
    loss_sum = push_sum(links, m, b.loss_part[...], b.loss_box, m.plane_peers, m.slot, 8)
    b.small[7:8] = jnp.zeros((1, local), F32)
    b.small[64:72] = jnp.zeros((8, local), F32)
    b.small[7:8, :wide_d] = jnp.sum(grad_normed * x_hat, axis=0, keepdims=True)
    b.small[64:65, :128] = loss_sum()[:1]
    b.small_box[m.z] = b.small[...]
    small_copies = [
        links.go(b.small_box.at[m.z], b.small_box.at[m.z], peer) for peer in m.dp_peers
    ]
    ring_cell.step()
    lines = to_columns(line_sum()) / width
    grad_x = b.rstd[:, :1] * (grad_scaled - lines[:, :1] - x_hat * lines[:, 1:2])
    own_grad = b.own_gradient[...].astype(F32)
    grad_slot = (own_grad + grad_x).astype(BF)
    b.sent_tokens[...] = mm_tn(b.recv_map[...], grad_slot).astype(BF)
    own_place = pl.ds(pl.multiple_of(m.z * cap, 16), cap)
    b.home_grad[own_place] = b.sent_tokens[own_place]
    copies = []
    for d, peer in enumerate(m.dp_peers):
        place = pl.ds(pl.multiple_of(lax.rem(m.z + d + 1, n_dp) * cap, 16), cap)
        copies.append(links.go(b.sent_tokens.at[place], b.home_grad.at[own_place], peer))
    for copy in b.home_copies:
        copy.wait_recv()
    b.output[...] = mm_tn(b.send_map[...], b.home_out[...]).astype(BF)
    for copy in small_copies:
        copy.wait_recv()
    total = b.small_box[0]
    for k in range(1, n_dp):
        total = total + b.small_box[k]
    b.small_sum[...] = total
    for copy in copies:
        copy.wait_recv()
    b.grad_input[...] = mm_tn(b.send_map[...], b.home_grad[...]).astype(BF)
    ring_cell.finish()


def kernel(names, shape, limit, *refs):
    b = types.SimpleNamespace(**dict(zip(names, refs)))
    m = coordinates(shape[3])
    links = Links(b.send_sem, b.recv_sem, limit)
    forward(b, m, links, shape)
    backward(b, m, links, shape)
    links.close()


def shards(
    tokens,
    targets,
    ln_gain,
    up_weight,
    conv_weight,
    conv_bias,
    qkv_weight,
    gate_weight,
    gate_bias,
    group_gain,
    skip_gain,
    down_weight,
    lengths,
    permutation,
    valid,
):
    rows, wide_d = tokens.shape
    n_dp = lax.axis_size("dp")
    dp = lax.axis_index("dp")
    heads, chan = up_weight.shape[2], up_weight.shape[3]
    local = heads * chan
    cap = rows // n_dp
    block = up_weight.shape[0]
    width = 8 * wide_d

    place = jnp.arange(rows, dtype=jnp.int32)
    own_perm = lax.dynamic_slice_in_dim(permutation, dp * rows, rows)
    dest = own_perm // rows
    earlier = (dest[:, None] == dest[None, :]) & (place[:, None] > place[None, :])
    code = dest * cap + jnp.sum(earlier.astype(jnp.int32), axis=1)
    send_map = (place[:, None] == code[None, :]).astype(BF)
    by_source = permutation.reshape(n_dp, rows)
    mine = by_source // rows == dp
    before = (place[:, None] < place[None, :]).astype(BF)
    rank = mm(mine.astype(BF), before).astype(jnp.int32)
    hit = mine[:, None, :] & (rank[:, None, :] == jnp.arange(cap, dtype=jnp.int32)[None, :, None])
    slot_of = jnp.sum(jnp.where(hit, (by_source - dp * rows)[:, None, :], 0), axis=2).reshape(-1)
    recv_map = (place[:, None] == slot_of[None, :]).astype(BF)
    payload = jnp.concatenate(
        [tokens, targets, jnp.broadcast_to(valid[:, None], (rows, 128)).astype(BF)], axis=1
    )
    chan_params = jnp.concatenate(
        [
            conv_weight.reshape(4, local),
            conv_bias.reshape(1, local),
            group_gain.reshape(1, local),
            skip_gain.reshape(1, local),
            jnp.zeros((1, local), BF),
        ],
        axis=0,
    ).astype(F32)
    inputs = {
        "send_map": send_map,
        "recv_map": recv_map,
        "payload": payload,
        "ln8": jnp.broadcast_to(ln_gain[None], (8, wide_d)).astype(F32),
        "own_cell": up_weight[:, 0].reshape(block, local),
        "own_gate": up_weight[:, 1].reshape(block, local),
        "own_down": down_weight.reshape(local, block),
        "chan_params": chan_params,
        "maps8": jnp.tile(qkv_weight.transpose(0, 2, 1, 3), (1, 1, 2, 1)).astype(F32),
        "gates_w": jnp.pad(gate_weight.reshape(8, 3 * local), ((0, 8), (0, 0))),
        "gate_bias": jnp.broadcast_to(gate_bias.reshape(8, 1), (8, 128)).astype(F32),
        "lengths": lengths,
    }
    outputs = {
        "output": ((rows, wide_d), BF),
        "grad_input": ((rows, wide_d), BF),
        "small_sum": ((72, local), F32),
        "grad_up": ((block, 2 * local), F32),
        "grad_down": ((local, block), F32),
    }
    n_blocks = band(rows)[1]
    half = rows // 2
    limit = 120 + 12 * n_dp
    scratch = {
        "sent_tokens": ((rows, wide_d), BF),
        "sent_rest": ((rows, wide_d + 128), BF),
        "rest": ((rows, wide_d + 128), BF),
        "full": ((8, rows, wide_d), BF),
        "gains": ((8, 8, wide_d), F32),
        "up_cell": ((n_dp, block, local), BF),
        "up_gate": ((n_dp, block, local), BF),
        "down": ((n_dp, local, block), BF),
        "sums": ((rows, 128), F32),
        "squares": ((rows, 128), F32),
        "mean": ((rows, 128), F32),
        "rstd": ((rows, 128), F32),
        "x_full": ((rows, width), BF),
        "normed": ((rows, width), BF),
        "wide_f": ((rows, local), F32),
        "begin": ((rows, 128), jnp.int32),
        "branch": ((rows, local), BF),
        "act": ((rows, local), F32),
        "slope": ((rows, local), F32),
        "maps": ((3, heads, chan, chan), BF),
        "qkv": ((rows, 3 * local), BF),
        "pre_box": ((8, 8, rows), F32),
        "pre": ((8, rows), F32),
        "score_part": ((heads, n_blocks, LINE, LINE), F32),
        "score_in": ((2, n_blocks, LINE, LINE), F32),
        "score_sum": ((2, n_blocks, LINE, LINE), F32),
        "decay": ((n_blocks, LINE, LINE), F32),
        "weight": ((n_blocks, LINE, LINE), F32),
        "share": ((heads, n_blocks, LINE, LINE), BF),
        "inv": ((rows, 128), F32),
        "sign": ((rows, 128), F32),
        "hidden": ((rows, local), F32),
        "moment_box": ((4, 8, rows), F32),
        "head_rstd": ((heads, rows, 128), F32),
        "head_mean": ((heads, rows, 128), F32),
        "gate_low": ((rows, local), BF),
        "mixed": ((rows, local), BF),
        "goal": ((rows, wide_d), BF),
        "count_box": ((n_dp, 8, 128), F32),
        "out": ((4, rows, wide_d), BF),
        "into": ((4, rows, wide_d), BF),
        "acc": ((4, rows, wide_d), F32),
        "small_out": ((6, half, wide_d), BF),
        "small_in": ((6, half, wide_d), BF),
        "loss_part": ((8, 128), F32),
        "own_gradient": ((rows, wide_d), BF),
        "sent_out": ((rows, wide_d), BF),
        "home_out": ((rows, wide_d), BF),
        "home_grad": ((rows, wide_d), BF),
        "ring_down": ((n_dp, local, block), BF),
        "ring_gate": ((n_dp, block, local), BF),
        "ring_cell": ((n_dp, block, local), BF),
        "g_gate": ((rows, local), BF),
        "g_cell": ((rows, local), BF),
        "small": ((72, local), F32),
        "small_box": ((n_dp, 72, local), F32),
        "g_act": ((rows, local), F32),
        "u_box": ((4, 8, rows), F32),
        "d_hidden": ((rows, local), BF),
        "share_out": ((n_blocks, LINE, LINE), BF),
        "share_in": ((n_blocks, LINE, LINE), BF),
        "lines": ((8, rows), F32),
        "d_score": ((heads, n_blocks, LINE, LINE), BF),
        "exact": ((rows, 128), F32),
        "grad_box": ((4, 8, rows), F32),
        "g_proj": ((rows, 3 * local), F32),
        "line_box": ((8, 8, rows), F32),
        "loss_box": ((8, 8, 128), F32),
    }
    vmem = pl.BlockSpec(memory_space=pltpu.VMEM)
    smem = pl.BlockSpec(memory_space=pltpu.SMEM)
    names = list(inputs) + list(outputs) + list(scratch) + ["send_sem", "recv_sem"]
    results = pl.pallas_call(
        lambda *refs: kernel(names, (rows, local, chan, n_dp, block, wide_d), limit, *refs),
        out_shape=[jax.ShapeDtypeStruct(*spec) for spec in outputs.values()],
        in_specs=[smem if name == "lengths" else vmem for name in inputs],
        out_specs=[vmem] * len(outputs),
        scratch_shapes=[pltpu.VMEM(*spec) for spec in scratch.values()]
        + [pltpu.SemaphoreType.DMA((limit,)), pltpu.SemaphoreType.DMA((limit,))],
        compiler_params=pltpu.CompilerParams(
            collective_id=0, has_side_effects=True, vmem_limit_bytes=VMEM_LIMIT
        ),
    )(*inputs.values())
    o = types.SimpleNamespace(**dict(zip(outputs, results)))
    small = o.small_sum
    maps = small[40:64].reshape(3, 2, 4, heads, chan).sum(axis=1)
    return (
        o.output,
        small[64, 0],
        o.grad_input,
        small[7, :wide_d],
        o.grad_up.reshape(up_weight.shape),
        small[0:4].reshape(conv_weight.shape),
        small[4].reshape(conv_bias.shape),
        maps,
        small[8:32].reshape(3, 8, local).transpose(1, 0, 2).reshape(gate_weight.shape),
        small[32:40, 0].reshape(gate_bias.shape),
        small[5].reshape(group_gain.shape),
        small[6].reshape(skip_gain.shape),
        o.grad_down.reshape(down_weight.shape),
    )


def solution(mesh):
    return jax.shard_map(
        shards,
        mesh=mesh,
        in_specs=(
            P("dp", ("tensor", "ctx")),
            P("dp", ("tensor", "ctx")),
            P(("tensor", "ctx")),
            P("dp", None, "ctx", "tensor"),
            P(None, "ctx", "tensor"),
            P("ctx", "tensor"),
            P(None, None, "ctx", "tensor"),
            P(None, None, None, "ctx", "tensor"),
            P(),
            P("ctx", "tensor"),
            P("ctx", "tensor"),
            P("ctx", "tensor", "dp"),
            P(),
            P(),
            P("dp"),
        ),
        out_specs=(
            P("dp", ("tensor", "ctx")),
            P(),
            P("dp", ("tensor", "ctx")),
            P(("tensor", "ctx")),
            P("dp", None, "ctx", "tensor"),
            P(None, "ctx", "tensor"),
            P("ctx", "tensor"),
            P(None, None, "ctx", "tensor"),
            P(None, None, None, "ctx", "tensor"),
            P(),
            P("ctx", "tensor"),
            P("ctx", "tensor"),
            P("ctx", "tensor", "dp"),
        ),
        check_vma=False,
    )
```

time: 704 us -> 327 us (0.46); the launches traced: 694 us -> 326 us
  waiting for transfers between devices: 375 us -> 0 us
  Pallas kernels: 0 us -> 291 us
  blocking collectives: 123 us -> 0 us
  matrix products: 64.9 us -> 0.18 us
  other arithmetic: 54.9 us -> 7.99 us
  between operations: 18.9 us -> 0.73 us
  local copies, waits for them, and re-layouts: 44.6 us -> 26.7 us
  starting transfers between devices: 12.8 us -> 0 us
    pallas_call x0 -> x1, Pallas kernels: none -> 291 us  [shards(): pl.pallas_call(lambda *refs: kernel(names, (rows, local, chan, n_dp, bloc...]
    all_gather x5 -> x0, waiting for transfers between devices: 154 us -> none  [the longest x1 45.2 us: shards(): lax.all_gather(up_weight[:, 0].reshape(block, local), 'dp', axis=0, tiled...]
    reduce_scatter x5 -> x0, waiting for transfers between devices: 121 us -> none  [the longest x1 44.4 us: shards(): lax.psum_scatter(grad_up_cell.astype(BF), 'dp', scatter_dimension=0, tile...]
    psum x5 -> x0, blocking collectives: 94 us -> none  [the longest x1 42.6 us: shards(): loss = lax.psum(loss_part, ('dp', 'tensor', 'ctx')) / count]
    psum x3 -> x0, waiting for transfers between devices: 82.5 us -> none  [the longest x1 51.4 us: shards(): dw = lax.psum(dw_part, 'tensor')]
    dot_general x35 -> x0, matrix products: 37.7 us -> none  [the longest x18 23.5 us: mm_tn(): lax.dot_general(a, b, (((0,), (0,)), ((), ())), preferred_element_type=F32)]
    all_gather x3 -> x0, blocking collectives: 28.8 us -> none  [the longest x1 12.5 us: shards(): gain_full = lax.all_gather(ln_gain, PLANE, axis=0, tiled=True).astype(F32)]
    dot_general x27 -> x1, matrix products: 27.2 us -> 0.18 us  [mm(): return jnp.dot(a, b, preferred_element_type=F32)]
  transfers between devices with their start and end apart: 15 -> 0, of which waited for: 13 -> 0; matrix products, arithmetic and copies ran while one was open for 12% -> 0% of each run, Pallas kernels for 0% -> 0%
where the time goes in v2:
time: 327 us; the launch traced here: 326 us
  Pallas kernels  291 us (89%)
  local copies, waits for them, and re-layouts  26.7 us (8%)
  other arithmetic  7.99 us (2%)
    pallas_call x1, Pallas kernels, shards(): pl.pallas_call(lambda *refs: kernel(names, (rows, local, chan, n_dp, bloc...  291 us
    unnamed x18, local copies, waits for them, and re-layouts  7.54 us

profile of v2, /device:TPU:0, one launch (start us, length us, event | category | flops | bytes accessed | tf_op | source)
XLA Modules:
  0.0 326.2 jit_solution(15327216324347073500)
XLA Ops:
  0.6 0.7 reshape.128
  1.4 0.7 convert_element_type.42
  2.1 0.7 copy.37
  2.8 0.7 copy.38
  3.4 0.7 copy.39
  4.1 0.8 add_select_fusion.1
  4.9 0.3 convert_reduce_fusion
  5.1 0.8 multiply_add_fusion
  5.9 0.7 broadcast_in_dim.25.refs_10_
  6.6 0.7 copy.36
  7.3 0.7 reshape.115
  8.0 0.2 convolution_convert_fusion
  8.2 0.3 select_reduce_fusion
  8.5 0.6 convert_element_type.44.refs_7_
  9.1 1.3 broadcast_in_dim.23.refs_3_
  10.4 0.7 convert_bitcast_fusion
  11.1 0.6 convert_element_type.47.refs_8_
  11.8 0.0 copy-start
  11.8 0.8 reshape.121
  12.6 0.6 pad.4.refs_9_
  13.3 0.1 broadcast_in_dim.22
  13.4 1.9 pad_maximum_fusion.refs_2_
  15.3 1.3 fusion
  16.6 0.0 copy-done
  16.6 0.7 fusion.9
  17.3 0.9 copy.35
  18.2 0.9 copy.34
  19.1 290.5 %shard_map.246 = (bf16[512,256]{1,0:T(8,128)(2,1)}, bf16[512,256]{1,0:T(8,128)(2,1)}, f32[72,512]{1,0:T(8,128)}, f32[512,1024]{1,0:T(8,128)}, f32[512,512]{1,0:T(8,128)}) custom-call(bf16[512,512]{1,0:T(8,128)(2,1)} %get-tuple-element.56.refs_0_, bf16[512,512]{1,0:T(8,128)(2,1)} %get-tuple-element.57.refs_1_, bf16[512,640]{1,0:T(8,128)(2,1)} %pad_maximum_fusion.refs_2_, ...), custom_call_target="tpu_custom_call" | custom-call | tf_op jit(solution)/shard_map/pallas_call | solution.py:1024
  309.7 1.2 slice.35
  310.9 0.8 slice_reduce_fusion
  311.6 0.6 reshape_squeeze.21
  312.3 1.3 slice.36
  313.5 0.9 slice_reduce_fusion.1
  314.4 0.6 reshape_squeeze.23
  315.0 0.6 reshape_squeeze.22
  315.6 0.6 reshape_squeeze.20
  316.2 0.7 slice.37
  316.9 0.8 slice_bitcast_fusion
  317.8 0.6 copy.33
  318.4 0.6 reshape.123
  319.0 0.6 reduce_sum.29
  319.7 4.1 %reshape.122 = f32[512,2,2,256]{3,2,1,0:T(2,128)} reshape(f32[512,1024]{1,0:T(8,128)} %get-tuple-element.21) | data formatting | bytes 4194304 | tf_op jit(solution)/shard_map/reshape | solution.py:1043
  323.8 0.0 copy-done.3
  323.8 0.7 copy.43
  324.5 0.0 copy-done.2
  324.5 0.7 copy.44
  325.2 0.0 copy-done.1
  325.2 1.0 copy.45
  (11 shorter events, 0.1 us)
Async XLA Ops:
  11.8 4.8 %copy-start = (bf16[512,2,2,256]{3,2,1,0:T(2,128)(2,1)S(1)}, bf16[512,2,2,256]{3,2,1,0:T(2,128)(2,1)}, u32[]{:S(2)}) copy-start(bf16[512,2,2,256]{3,2,1,0:T(2,128)(2,1)} %param.18) | copy-start | bytes 3145732
  319.7 4.1 %copy-start.3 = (bf16[512,256]{1,0:T(8,128)(2,1)S(1)}, bf16[512,256]{1,0:T(8,128)(2,1)}, u32[]{:S(2)}) copy-start(bf16[512,256]{1,0:T(8,128)(2,1)} %get-tuple-element.71) | copy-start | bytes 786436
  319.7 4.8 %copy-start.2 = (bf16[512,256]{1,0:T(8,128)(2,1)S(1)}, bf16[512,256]{1,0:T(8,128)(2,1)}, u32[]{:S(2)}) copy-start(bf16[512,256]{1,0:T(8,128)(2,1)} %get-tuple-element.73) | copy-start | bytes 786436
  319.7 5.5 %copy-start.1 = (f32[512,512]{1,0:T(8,128)S(1)}, f32[512,512]{1,0:T(8,128)}, u32[]{:S(2)}) copy-start(f32[512,512]{1,0:T(8,128)} %get-tuple-element.22) | copy-start | bytes 3145732

commit v3 on v2

v3 whole, which is shorter than its diff:
```python
import itertools
import types

import jax
import jax.numpy as jnp
from jax import lax
from jax.experimental import pallas as pl
from jax.experimental.pallas import tpu as pltpu
from jax.sharding import PartitionSpec as P

NEG_FILL = -1e30
EPSILON = 1e-05
BF = jnp.bfloat16
F32 = jnp.float32
MESH = pl.DeviceIdType.MESH
VMEM_LIMIT = 62 * 1024 * 1024
LINE = 128
BAND = 2


def mm(a, b):
    return jnp.dot(a, b, preferred_element_type=F32)


def mm_nt(a, b):
    return lax.dot_general(a, b, (((1,), (1,)), ((), ())), preferred_element_type=F32)


def mm_tn(a, b):
    return lax.dot_general(a, b, (((0,), (0,)), ((), ())), preferred_element_type=F32)


def split(v):
    high = v.astype(BF)
    return high, (v - high.astype(F32)).astype(BF)


def sigmoid(v):
    return 1.0 / (1.0 + jnp.exp(-v))


class Links:
    def __init__(self, send, recv, limit):
        self.send, self.recv, self.limit = send, recv, limit
        self.used, self.open = 0, []

    def make(self, src, dst, peer):
        k = self.used
        self.used += 1
        assert k < self.limit
        copy = pltpu.make_async_remote_copy(
            src_ref=src,
            dst_ref=dst,
            send_sem=self.send.at[k],
            recv_sem=self.recv.at[k],
            device_id=peer,
            device_id_type=MESH,
        )
        return copy

    def go(self, src, dst, peer):
        copy = self.make(src, dst, peer)
        copy.start()
        self.open.append(copy)
        return copy

    def settle(self, copies):
        for copy in copies:
            copy.wait_send()
        self.open = [c for c in self.open if all(c is not done for done in copies)]

    def close(self):
        self.settle(list(self.open))


class Ring:
    def __init__(self, links, hold, part, next_peer, owners):
        self.links, self.hold, self.part = links, hold, part
        self.peer, self.owners = next_peer, owners
        self.flying, self.at = None, 0

    def start(self):
        block = self.hold.at[self.owners[self.at], self.part]
        self.flying = self.links.go(block, block, self.peer)

    def step(self):
        if self.at >= len(self.owners) - 1:
            return False
        if self.flying is None:
            self.start()
        self.flying.wait_recv()
        self.at += 1
        self.flying = None
        if self.at < len(self.owners) - 1:
            self.start()
            return True
        return False

    def last_leg(self):
        while self.at < len(self.owners) - 2:
            self.step()

    def finish(self):
        while self.step():
            pass

    def settle(self):
        self.links.close()


def when(condition, *actions):
    @pl.when(condition)
    def _():
        for action in actions:
            action()


class LineGather:
    def __init__(self, links, hold, m, count):
        self.z, self.count, self.at = m.z, count, 0
        z, last = m.z, count - 1
        self.ways = []
        for d in range(1, count):
            to_right = jnp.maximum(z - (d - 1), 0)
            to_left = jnp.minimum(z + (d - 1), last)
            self.ways.append(
                (
                    (
                        links.make(hold.at[to_right], hold.at[to_right], m.right),
                        (z < last) & (z >= d - 1),
                        z >= d,
                    ),
                    (
                        links.make(hold.at[to_left], hold.at[to_left], m.left),
                        (z > 0) & (z + d - 1 <= last),
                        z + d <= last,
                    ),
                )
            )

    def start(self):
        for copy, sends, _ in self.ways[self.at]:
            when(sends, copy.start)

    def step(self):
        if self.at >= self.count - 1:
            return
        for copy, _, receives in self.ways[self.at]:
            when(receives, copy.wait_recv)
        self.at += 1
        if self.at < self.count - 1:
            self.start()

    def last_leg(self):
        while self.at < self.count - 2:
            self.step()

    def finish(self):
        while self.at < self.count - 1:
            self.step()

    def settle(self):
        for pair in self.ways:
            for copy, sends, _ in pair:
                when(sends, copy.wait_send)


class LineSum:
    def __init__(self, links, part, hold, target, m, count):
        self.part, self.hold, self.target = part, hold, target
        self.z, self.count, self.at = m.z, count, 0
        places = (m.z, count - 1 - m.z)
        self.ways = [
            (
                places[way],
                [
                    links.make(hold.at[way, t], hold.at[way, t + 1], peer)
                    for t in range(count - 1)
                ],
            )
            for way, peer in enumerate((m.right, m.left))
        ]

    def step(self):
        t, count = self.at, self.count
        if t > count - 1:
            return
        self.at += 1
        if t == count - 1:
            total = self.part(self.z)
        for way, (place, copies) in enumerate(self.ways):
            behind = place > 0
            if t:
                when(behind & (place <= t), copies[t - 1].wait_recv)
            if t == count - 1:
                total = total + jnp.where(behind, self.hold[way, t].astype(F32), 0.0)
                continue

            def send(way=way, place=place, copies=copies, behind=behind):
                ahead = count - 1 - t
                own = self.part(self.z + ahead if way == 0 else self.z - ahead)
                if t:
                    own = own + jnp.where(behind, self.hold[way, t].astype(F32), 0.0)
                self.hold[way, t] = own.astype(BF)
                copies[t].start()

            when(place <= t, send)
        if t == count - 1:
            self.target(total)

    def settle(self):
        for place, copies in self.ways:
            for t, copy in enumerate(copies):
                when(place <= t, copy.wait_send)


class RingSum:
    def __init__(self, links, part, hold, target, m, count):
        self.links, self.part, self.hold, self.target = links, part, hold, target
        self.m, self.count, self.at = m, count, -1
        self.sent = []

    def step(self):
        if self.at >= self.count - 1:
            return
        self.at += 1
        own = self.part(self.m.owners[(self.at + 1) % self.count])
        if self.at:
            self.sent[-1].wait_recv()
            own = own + self.hold[0, self.at].astype(F32)
        if self.at == self.count - 1:
            self.target(own)
            return
        self.hold[0, self.at] = own.astype(BF)
        self.sent.append(
            self.links.go(
                self.hold.at[0, self.at], self.hold.at[0, self.at + 1], self.m.ring_next
            )
        )

    def settle(self):
        self.links.settle(self.sent)


def coordinates(dp_count):
    z, t, c = lax.axis_index("dp"), lax.axis_index("tensor"), lax.axis_index("ctx")
    core = lax.rem(t, 2)
    m = types.SimpleNamespace(z=z, t=t, c=c, core=core, y=lax.div(t, 2))
    m.sib_t, m.far_t, m.other_c = t + 1 - 2 * core, lax.rem(t + 2, 4), 1 - c
    m.sib, m.yn, m.xn = (z, m.sib_t, c), (z, m.far_t, c), (z, t, m.other_c)
    m.slot = t * 2 + c
    m.slot_x, m.slot_y, m.slot_d = t * 2 + m.other_c, m.far_t * 2 + c, m.far_t * 2 + m.other_c
    m.to_sib = 2 - 4 * core
    if dp_count == 4:
        def after(v):
            return lax.rem(2 * v + 1, 5)

        def before(v):
            return lax.rem(3 * v + 2, 5)
    else:
        def after(v):
            return lax.rem(v + 1, dp_count)

        def before(v):
            return lax.rem(v + dp_count - 1, dp_count)

    m.ring_next = (after(z), t, c)
    m.owners = [z]
    for _ in range(dp_count - 1):
        m.owners.append(before(m.owners[-1]))
    m.right = (lax.rem(z + 1, dp_count), t, c)
    m.left = (lax.rem(z + dp_count - 1, dp_count), t, c)
    m.dp_peers = [(lax.rem(z + d, dp_count), t, c) for d in range(1, dp_count)]
    m.plane_peers = [
        (z, lax.rem(t + dt, 4), lax.rem(c + dc, 2))
        for dt in range(4)
        for dc in range(2)
        if dt or dc
    ]
    m.tensor_peers = [(z, lax.rem(t + dt, 4), c) for dt in range(1, 4)]
    return m


def plane_gather(links, m, full, rows):
    half = rows // 2
    first, second = pl.ds(0, half), pl.ds(half, half)

    sent = []

    def send(slot, part, peer):
        sent.append(links.go(full.at[slot, part], full.at[slot, part], peer))
        return sent[-1]

    x_first = send(m.slot, first, m.xn)
    y_second = send(m.slot, second, m.yn)
    to_sib = send(m.slot, pl.ds(0, rows), m.sib)
    x_second = send(m.slot, second, m.xn)
    y_first = send(m.slot, first, m.yn)
    yield m.slot
    to_sib.wait_recv()
    yield m.slot + m.to_sib
    x_first.wait_recv()
    d_first = send(m.slot_x, first, m.yn)
    y_second.wait_recv()
    d_second = send(m.slot_y, second, m.xn)
    x_second.wait_recv()
    sib_x = send(m.slot_x, pl.ds(0, rows), m.sib)
    yield m.slot_x
    y_first.wait_recv()
    sib_y = send(m.slot_y, pl.ds(0, rows), m.sib)
    yield m.slot_y
    sib_x.wait_recv()
    yield m.slot_x + m.to_sib
    d_first.wait_recv()
    d_second.wait_recv()
    sib_d = send(m.slot_d, pl.ds(0, rows), m.sib)
    yield m.slot_d
    sib_y.wait_recv()
    yield m.slot_y + m.to_sib
    sib_d.wait_recv()
    yield m.slot_d + m.to_sib
    links.settle(sent)


def idle():
    pass


def to_lanes(columns, rows):
    lane = lax.broadcasted_iota(jnp.int32, (rows, 128), 1)
    out = jnp.zeros((rows, 128), F32)
    for j, column in enumerate(columns):
        out = jnp.where(lane == j, column, out)
    return out.T[:8]


def to_lanes_one(column):
    line = lax.broadcasted_iota(jnp.int32, (8, 128), 0)
    lane = lax.broadcasted_iota(jnp.int32, (8, 128), 1)
    return jnp.sum(jnp.where(line == lane, column, 0.0), axis=0, keepdims=True)


def to_columns(lines):
    rows = lines.shape[1]
    return jnp.concatenate([lines, jnp.zeros((120, rows), F32)], axis=0).T


def push_sum(links, m, lines, box, peers, own_place, count):
    box[own_place] = lines
    copies = [links.go(box.at[own_place], box.at[own_place], peer) for peer in peers]

    def finish():
        for copy in copies:
            copy.wait_recv()
        total = box[0]
        for k in range(1, count):
            total = total + box[k]
        return total

    return finish


def prefix_lanes(v):
    width = v.shape[1]
    lane = lax.broadcasted_iota(jnp.int32, v.shape, 1)
    step = 1
    while step < width:
        v = v + jnp.where(lane >= step, pltpu.roll(v, step, 1), 0.0)
        step *= 2
    return v


def band(rows):
    out, at = [], 0
    for i in range(rows // LINE):
        low = max(0, i - BAND)
        out.append((i, low, at, i - low + 1))
        at += i - low + 1
    return out, at


def wide(ref, h, at, width):
    return jnp.concatenate([ref[h, at + k] for k in range(width)], axis=1)


def plane_scatter(links, m, part, b, rows, services):
    half = rows // 2
    first, second = pl.ds(0, half), pl.ds(half, half)
    own_k = m.y * 2 + m.c
    far_y = 1 - m.y
    links.settle(b.scatter_copies)
    copies = []
    for k in range(4):
        b.out[k] = part(k // 2, 1 - m.core, k % 2).astype(BF)
        copies.append(links.go(b.out.at[k], b.into.at[k], m.sib))
    for k in range(4):
        b.acc[k] = part(k // 2, m.core, k % 2)
    b.scatter_copies = copies
    services[0]()
    for k in range(4):
        copies[k].wait_recv()
        b.acc[k] += b.into[k].astype(F32)
    copies = []
    for y in range(2):
        b.small_out[y] = b.acc[y * 2 + m.other_c, first].astype(BF)
        copies.append(links.go(b.small_out.at[y], b.small_in.at[y], m.xn))
    for x in range(2):
        b.small_out[2 + x] = b.acc[far_y * 2 + x, second].astype(BF)
        copies.append(links.go(b.small_out.at[2 + x], b.small_in.at[2 + x], m.yn))
    b.scatter_copies += copies
    services[1]()
    for k in range(4):
        copies[k].wait_recv()
    for y in range(2):
        b.acc[y * 2 + m.c, first] += b.small_in[y].astype(F32)
    for x in range(2):
        b.acc[m.y * 2 + x, second] += b.small_in[2 + x].astype(F32)
    b.small_out[4] = b.acc[far_y * 2 + m.c, first].astype(BF)
    to_y = links.go(b.small_out.at[4], b.small_in.at[4], m.yn)
    b.small_out[5] = b.acc[m.y * 2 + m.other_c, second].astype(BF)
    to_x = links.go(b.small_out.at[5], b.small_in.at[5], m.xn)
    b.scatter_copies += [to_y, to_x]
    services[2]()
    to_y.wait_recv()
    to_x.wait_recv()
    b.acc[own_k, first] += b.small_in[4].astype(F32)
    b.acc[own_k, second] += b.small_in[5].astype(F32)
    return own_k


def forward(b, m, links, shape):
    rows, local, chan, n_dp, block, wide_d = shape
    cap, heads = rows // n_dp, local // chan
    width, all_heads = 8 * wide_d, 2 * heads
    scale = (4 * chan) ** -0.5
    blocks, n_blocks = band(rows)
    low_rows = pl.ds(0, rows)

    b.scatter_copies = []
    partners = m.plane_peers + m.dp_peers
    barrier = pltpu.get_barrier_semaphore()
    for peer in partners:
        pl.semaphore_signal(barrier, inc=1, device_id=peer, device_id_type=MESH)
    own_copies = [
        pltpu.make_async_copy(own, hold.at[m.z], b.local_sem.at[k])
        for k, (own, hold) in enumerate(
            ((b.own_cell, b.up_cell), (b.own_gate, b.up_gate), (b.own_down, b.down))
        )
    ]
    for copy in own_copies:
        copy.start()
    own_place = pl.ds(pl.multiple_of(m.z * cap, 16), cap)
    b.gains[m.slot] = jnp.broadcast_to(b.ln_gain[...].astype(F32), (8, wide_d))
    b.valids[m.z] = jnp.broadcast_to(b.index[n_dp : n_dp + 1].astype(F32), (8, rows))
    count = block // 2 if block % 256 == 0 else block
    cells = [
        Ring(links, b.up_cell, pl.ds(at, count), m.ring_next, m.owners)
        for at in range(0, block, count)
    ]
    gate = Ring(links, b.up_gate, pl.ds(0, block), m.ring_next, m.owners)
    down = Ring(links, b.down, pl.ds(0, local), m.ring_next, m.owners)
    if n_dp <= 4:
        mixed_ring = LineGather(links, b.mixed_all, m, n_dp)
    else:
        mixed_ring = Ring(links, b.mixed_all, pl.ds(0, rows), m.ring_next, m.owners)
    own_copies[0].wait()
    pl.semaphore_wait(barrier, len(partners))
    cells[0].start()

    digits = rows.bit_length() - 1
    packs = max(8, n_dp)
    own = b.index[pl.ds(m.z, 1)]
    dest = lax.shift_right_logical(own, digits)
    to_pack = lax.broadcasted_iota(jnp.int32, (packs, rows), 0) == dest
    ahead = prefix_lanes(jnp.where(to_pack, 1.0, 0.0))
    rank = jnp.sum(jnp.where(to_pack, ahead, 0.0), axis=0, keepdims=True).astype(jnp.int32) - 1
    line = lax.broadcasted_iota(jnp.int32, (rows, rows), 0)
    b.send_map[...] = jnp.where(line == dest * cap + rank, 1.0, 0.0).astype(BF)
    b.sent_tokens[...] = mm(b.send_map[...], b.tokens[...]).astype(BF)
    b.full[m.slot, own_place] = b.sent_tokens[own_place]

    def exchange(out, into):
        copies = []
        for d, peer in enumerate(m.dp_peers):
            place = pl.ds(pl.multiple_of(lax.rem(m.z + d + 1, n_dp) * cap, 16), cap)
            copies.append(links.go(out.at[place], into.at[own_place], peer))
        return copies

    b.exchange = exchange
    a2a = exchange(b.sent_tokens, b.full.at[m.slot])
    b.token_copies = a2a
    for ring in cells[1:]:
        ring.start()
    one = pl.ds(0, 1)
    gain_copies = [
        links.go(b.gains.at[m.slot], b.gains.at[m.slot], peer) for peer in m.plane_peers
    ]
    valid_copies = [
        links.go(b.valids.at[m.z, one], b.valids.at[m.z, one], peer) for peer in m.dp_peers
    ]
    for copy in own_copies[1:]:
        copy.wait()

    b.wide_f[...] = jnp.zeros((rows, rows), F32)

    def place_source(s, carry):
        perm = b.index[pl.ds(s, 1)]
        mine = lax.shift_right_logical(perm, digits) == m.z
        ahead = prefix_lanes(jnp.broadcast_to(jnp.where(mine, 1.0, 0.0), (8, rows)))[:1]
        at = jnp.where(mine, s * cap + ahead.astype(jnp.int32) - 1, -1)
        slot = perm - m.z * rows
        slots = jnp.where(line == slot, 1.0, 0.0).astype(BF)
        places = jnp.where(line == at, 1.0, 0.0).astype(BF)
        b.wide_f[...] += mm_nt(slots, places)
        return carry

    lax.fori_loop(0, n_dp, place_source, 0)
    b.recv_map[...] = b.wide_f[...].astype(BF)
    for copy in a2a:
        copy.wait_recv()
    cells[0].step()

    b.sums[...] = jnp.zeros((rows, 128), F32)
    b.squares[...] = jnp.zeros((rows, 128), F32)
    arrivals = 0
    for slot in plane_gather(links, m, b.full, rows):
        columns = pl.ds(pl.multiple_of(slot * wide_d, 128), wide_d)

        def place_rows(r, carry, slot=slot, columns=columns):
            at = pl.ds(pl.multiple_of(r * LINE, LINE), LINE)
            x = mm(b.recv_map[at], b.full[slot])
            b.normed[at, columns] = x.astype(BF)
            b.sums[at] += jnp.sum(x, axis=1, keepdims=True)
            b.squares[at] += jnp.sum(x * x, axis=1, keepdims=True)
            return carry

        lax.fori_loop(0, rows // LINE, place_rows, 0)
        arrivals += 1
        if arrivals in (3, 8):
            cells[-1].step()
        if arrivals == 6:
            cells[0].step()
    own_columns = pl.ds(pl.multiple_of(m.slot * wide_d, 128), wide_d)
    b.x_own[...] = b.normed[:, own_columns]
    b.sent_goal[...] = mm(b.send_map[...], b.targets[...]).astype(BF)
    b.goal_places[own_place] = b.sent_goal[own_place]
    for copy in gain_copies:
        copy.wait_recv()

    def normalise(r, carry):
        at = pl.ds(pl.multiple_of(r * 64, 64), 64)
        mean = b.sums[at][:, :1] / width
        var = b.squares[at][:, :1] / width - mean * mean
        rstd = lax.rsqrt(var + EPSILON)
        b.sums[at] = jnp.broadcast_to(mean, (64, 128))
        b.squares[at] = jnp.broadcast_to(rstd, (64, 128))
        for i in range(8):
            x = b.normed[at, i * wide_d : (i + 1) * wide_d].astype(F32)
            x = (x - mean) * rstd * b.gains[i, :1]
            b.normed[at, i * wide_d : (i + 1) * wide_d] = x.astype(BF)
        return carry

    lax.fori_loop(0, rows // 64, normalise, 0)

    def project(hold, rings, target):
        count = block // len(rings)
        for s in range(n_dp):
            owner = m.owners[s]
            for r, ring in enumerate(rings):
                while ring.at < s:
                    ring.step()
                columns = pl.ds(pl.multiple_of(owner * block + r * count, 128), count)
                product = mm(b.normed[:, columns], hold[owner, r * count : (r + 1) * count])
                target[...] = product if s + r == 0 else target[...] + product

    for ring in cells:
        ring.last_leg()
    gate.start()
    down.start()
    project(b.up_cell, cells, b.wide_f)

    for h in range(heads):
        at = slice(h * chan, (h + 1) * chan)
        for j in range(4):
            b.chan_params[j : j + 1, at] = b.conv_weight[j].astype(F32)[h : h + 1]
        for j, ref in ((4, b.conv_bias), (5, b.group_gain), (6, b.skip_gain)):
            b.chan_params[j : j + 1, at] = ref[...].astype(F32)[h : h + 1]
        for s in range(3):
            for i in range(4):
                tap = b.qkv_weight[s, i].astype(F32)[h : h + 1]
                b.maps8[s, h, i : i + 1] = tap
                b.maps8[s, h, i + 4 : i + 5] = tap
            for g in range(2 * all_heads):
                row = b.gate_weight[g // all_heads, g % all_heads, s].astype(F32)[h : h + 1]
                b.gates_f[g : g + 1, s * local + h * chan : s * local + (h + 1) * chan] = row
    b.gates_f[8:] = jnp.zeros((8, 3 * local), F32)
    b.gates_w[...] = b.gates_f[...].astype(BF)
    place = lax.broadcasted_iota(jnp.int32, (rows, 1), 0)
    ends, total = [], 0
    for k in range(b.lengths.shape[1]):
        total = total + b.lengths[m.z, k]
        ends.append(total)
    begin = jnp.zeros((rows, 1), jnp.int32)
    for end in ends:
        begin = jnp.where(place >= end, end, begin)
    b.begin[...] = jnp.broadcast_to(begin, (rows, 128))

    def convolve(i, carry):
        at = pl.ds(pl.multiple_of(i * 128, 128), 128)
        low = b.wide_f[:, at].astype(BF)
        b.branch[:, at] = low
        x = low.astype(F32)
        since = lax.broadcasted_iota(jnp.int32, (rows, 128), 0) - b.begin[...]
        conv = b.chan_params[4:5, at] + b.chan_params[0:1, at] * x
        for j in range(1, 4):
            back = b.chan_params[j : j + 1, at] * pltpu.roll(x, j, 0)
            conv = conv + jnp.where(since >= j, back, 0.0)
        sig = sigmoid(conv)
        act = conv * sig
        b.act[:, at] = act
        b.slope[:, at] = sig + act * (1.0 - sig)
        return carry

    lax.fori_loop(0, local // 128, convolve, 0)
    r_map = lax.broadcasted_iota(jnp.int32, (chan, chan), 0) // 4
    c_map = lax.broadcasted_iota(jnp.int32, (chan, chan), 1) // 4
    same = r_map == c_map
    for s in range(3):
        for h in range(heads):
            base = b.maps8[s, h]
            dense = jnp.broadcast_to(base[None], (chan // 8, 8, chan)).reshape(chan, chan)
            b.maps[s, h] = jnp.where(same, dense, 0.0).astype(BF)
    for h in range(heads):
        at = slice(h * chan, (h + 1) * chan)
        high, rest = split(b.act[:, at])
        for s in range(2):
            b.qkv[:, s * local + h * chan : s * local + (h + 1) * chan] = (
                mm(high, b.maps[s, h]) + mm(rest, b.maps[s, h])
            ).astype(BF)
        b.qkv[:, 2 * local + h * chan : 2 * local + (h + 1) * chan] = mm(
            b.branch[:, at], b.maps[2, h]
        ).astype(BF)

    pre_part = mm_nt(b.gates_w[...], b.qkv[...])[:8]
    pre_sum = push_sum(links, m, pre_part, b.pre_box, m.plane_peers, m.slot, 8)

    def q_of(h, i):
        return b.qkv[i * LINE : (i + 1) * LINE, h * chan : (h + 1) * chan]

    def k_of(h, low, n):
        return b.qkv[
            low * LINE : (low + n) * LINE, local + h * chan : local + (h + 1) * chan
        ]

    def v_of(h, low, n):
        return b.qkv[
            low * LINE : (low + n) * LINE, 2 * local + h * chan : 2 * local + (h + 1) * chan
        ]

    b.of = (q_of, k_of, v_of)
    for h in range(heads):
        for i, low, at, n in blocks:
            tile = mm_nt(q_of(h, i), k_of(h, low, n))
            for k in range(n):
                b.score_part[h, at + k] = tile[:, k * LINE : (k + 1) * LINE]
    other = links.go(b.score_part.at[1 - m.core], b.score_in.at[0], m.sib)
    b.score_copy = other
    other.wait_recv()
    b.score_sum[...] = b.score_part[m.core] + b.score_in[0]
    far = links.go(b.score_sum, b.score_in.at[1], m.yn)

    line81 = lax.broadcasted_iota(jnp.int32, (8, 1), 0)
    given = b.gate_bias[...].astype(F32)
    bias = jnp.zeros((8, 1), F32)
    for g in range(2):
        for o in range(all_heads):
            bias = jnp.where(line81 == g * all_heads + o, given[g : g + 1, o : o + 1], bias)
    pre = pre_sum() + bias
    b.pre[...] = pre
    line8 = lax.broadcasted_iota(jnp.int32, (8, rows), 0)
    head = m.c * heads + m.core
    in_gate = jnp.sum(jnp.where(line8 == head, pre, 0.0), axis=0, keepdims=True)
    forget = jnp.sum(jnp.where(line8 == head + all_heads, pre, 0.0), axis=0, keepdims=True)
    log_forget = jnp.minimum(forget, 0.0) - jnp.log(1.0 + jnp.exp(-jnp.abs(forget)))
    rising = prefix_lanes(jnp.broadcast_to(log_forget, (8, rows)))
    rise_col = to_columns(rising)
    gate_line = in_gate - rising[:1]
    gate.step()
    for copy in valid_copies:
        copy.wait_recv()
    b.keep[...] = jnp.zeros((rows, 128), F32)

    def take_source(s, carry):
        perm = b.index[pl.ds(s, 1)]
        valid = b.valids[s][:1]
        pack = lax.shift_right_logical(perm, digits)
        lasts = jnp.zeros((1, rows), jnp.int32)
        for p in range(n_dp):
            last = sum(b.lengths[p, k] for k in range(b.lengths.shape[1]))
            lasts = jnp.where(pack == p, last, lasts)
        counted = jnp.where(perm - pack * rows < lasts, valid, 0.0)
        hits = jnp.where(line == perm - m.z * rows, counted, 0.0)
        b.keep[...] += jnp.sum(hits, axis=1, keepdims=True)
        return carry + jnp.sum(counted, axis=1, keepdims=True)

    valid_count = lax.fori_loop(0, n_dp, take_source, jnp.zeros((1, 1), F32))
    keep = b.keep[:, :1]
    far.wait_recv()
    b.score_part[m.core] = b.score_sum[...] + b.score_in[1]
    for i, low, at, n in blocks:
        lines = slice(i * LINE, (i + 1) * LINE)
        t_at = i * LINE + lax.broadcasted_iota(jnp.int32, (LINE, n * LINE), 0)
        s_at = low * LINE + lax.broadcasted_iota(jnp.int32, (LINE, n * LINE), 1)
        allowed = (s_at <= t_at) & (s_at >= b.begin[lines][:, :1])
        logit = jnp.where(
            allowed, rise_col[lines][:, :1] + gate_line[:, low * LINE : (low + n) * LINE], NEG_FILL
        )
        top = jnp.max(logit, axis=1, keepdims=True)
        decay = jnp.where(allowed, jnp.exp(logit - top), 0.0) * scale
        weight = wide(b.score_part, m.core, at, n) * decay
        den = jnp.sum(weight, axis=1, keepdims=True)
        floor = jnp.exp(-top)
        inv = 1.0 / jnp.maximum(jnp.abs(den), floor)
        shares = (weight * inv).astype(BF)
        b.inv[lines] = jnp.broadcast_to(inv, (LINE, 128))
        sign = jnp.where(jnp.abs(den) > floor, jnp.where(den > 0.0, 1.0, -1.0), 0.0)
        b.sign[lines] = jnp.broadcast_to(sign, (LINE, 128))
        for k in range(n):
            b.decay[at + k] = decay[:, k * LINE : (k + 1) * LINE]
            b.weight[at + k] = weight[:, k * LINE : (k + 1) * LINE]
            b.share[m.core, at + k] = shares[:, k * LINE : (k + 1) * LINE]
    shared = links.go(b.share.at[m.core], b.share.at[m.core], m.sib)
    gate.step()
    shared.wait_recv()
    columns = []
    for h in range(heads):
        for i, low, at, n in blocks:
            lines = slice(i * LINE, (i + 1) * LINE)
            b.hidden[lines, h * chan : (h + 1) * chan] = mm(
                wide(b.share, h, at, n), v_of(h, low, n)
            )
        hid = b.hidden[:, h * chan : (h + 1) * chan]
        columns.append(jnp.sum(hid, axis=1, keepdims=True))
        columns.append(jnp.sum(hid * hid, axis=1, keepdims=True))
    moment_sum = push_sum(
        links, m, to_lanes(columns, rows), b.moment_box, m.tensor_peers, m.t, 4
    )
    gate.finish()
    down.step()
    project(b.up_gate, (gate,), b.wide_f)
    moments = to_columns(moment_sum()) / (4 * chan)
    for h in range(heads):
        mean = moments[:, 2 * h : 2 * h + 1]
        rstd = lax.rsqrt(moments[:, 2 * h + 1 : 2 * h + 2] - mean * mean + EPSILON)
        b.head_rstd[h] = jnp.broadcast_to(rstd, (rows, 128))
        b.head_mean[h] = jnp.broadcast_to(mean, (rows, 128))
    down.step()

    def mix(i, carry):
        at = pl.ds(pl.multiple_of(i * 128, 128), 128)
        h = lax.div(i, chan // 128)
        hat = (b.hidden[:, at] - b.head_mean[h]) * b.head_rstd[h]
        b.hidden[:, at] = hat
        low = b.wide_f[:, at].astype(BF)
        b.gate_low[:, at] = low
        g = low.astype(F32)
        inner = hat * b.chan_params[5:6, at] + b.chan_params[6:7, at] * b.act[:, at]
        b.mixed_all[m.z, :, at] = (inner * (g * sigmoid(g))).astype(BF)
        return carry

    lax.fori_loop(0, local // 128, mix, 0)
    down.last_leg()
    goal_copies = exchange(b.sent_goal, b.goal_places)
    mixed_ring.start()
    down.finish()
    piece = min(block, wide_d)

    def down_part(y, core, x):
        slot = (y * 2 + core) * 2 + x
        parts = []
        for k in range(wide_d // piece):
            if block >= 2 * wide_d:
                owner = lax.div((y * 2 + core) * 2 * wide_d, block)
                parts.append(mm(b.mixed_all[m.z], b.down[owner, :, x * wide_d : (x + 1) * wide_d]))
            else:
                owner = lax.div(slot * wide_d, block) + k
                parts.append(mm(b.mixed_all[m.z], b.down[owner]))
        return jnp.concatenate(parts, axis=1)

    own_k = plane_scatter(links, m, down_part, b, rows, (idle, mixed_ring.step, idle))
    for copy in goal_copies:
        copy.wait_recv()
    goal = mm(b.recv_map[...], b.goal_places[...])
    result = (b.x_own[...].astype(F32) + b.acc[own_k]).astype(BF)
    difference = result.astype(F32) - goal
    per_row = jnp.sum(difference * difference, axis=1, keepdims=True)
    loss_part = jnp.sum(keep * 0.5 * per_row, axis=0, keepdims=True) / valid_count
    b.loss_part[...] = jnp.broadcast_to(loss_part, (8, 128))
    own_gradient = ((rows * n_dp) / valid_count * keep * difference).astype(BF)
    b.own_gradient[...] = own_gradient
    b.mixed_ring = mixed_ring
    b.full[m.slot] = own_gradient
    b.arriving = plane_gather(links, m, b.full, rows)
    next_slot = next(b.arriving)

    b.sent_out[...] = mm_tn(b.recv_map[...], result).astype(BF)
    b.home_out[own_place] = b.sent_out[own_place]
    b.home_copies = exchange(b.sent_out, b.home_out)
    b.arriving = itertools.chain([next_slot], b.arriving)


def backward(b, m, links, shape):
    rows, local, chan, n_dp, block, wide_d = shape
    cap, heads = rows // n_dp, local // chan
    all_heads = 2 * heads
    width, head_width = 8 * wide_d, 4 * chan
    blocks, n_blocks = band(rows)
    q_of, k_of, v_of = b.of
    line8 = lax.broadcasted_iota(jnp.int32, (8, rows), 0)
    head = m.c * heads + m.core

    seen = 0
    for slot in b.arriving:
        g = b.full[slot]
        if block >= wide_d:
            ratio = block // wide_d
            at = pl.ds(pl.multiple_of(lax.rem(slot, ratio) * wide_d, 128), wide_d)
            product = mm_nt(g, b.down[lax.div(slot, ratio), :, at])
        else:
            ratio = wide_d // block
            product = sum(
                mm_nt(g[:, k * block : (k + 1) * block], b.down[slot * ratio + k])
                for k in range(ratio)
            )
        b.wide_f[...] = product if seen == 0 else b.wide_f[...] + product
        seen += 1
        if seen == 6:
            b.mixed_ring.step()

    per = rows // 8
    own_rows = pl.ds(pl.multiple_of(m.slot * per, 16), per)
    for d in range(n_dp):
        to = m.z if d == 0 else m.dp_peers[d - 1][0]
        if block >= wide_d:
            ratio = block // wide_d
            for k in range(ratio):
                b.cols_out[to, :, k * wide_d : (k + 1) * wide_d] = b.full[to * ratio + k, own_rows]
        else:
            ratio = wide_d // block
            at = pl.ds(pl.multiple_of(lax.rem(to, ratio) * block, 128), block)
            b.cols_out[to] = b.full[lax.div(to, ratio), own_rows, at]
    from_here = pl.ds(pl.multiple_of(m.z * per, 16), per)
    b.cols[m.slot, from_here] = b.cols_out[m.z]
    cols_copies = [
        links.go(b.cols_out.at[peer[0]], b.cols.at[m.slot, from_here], peer)
        for peer in m.dp_peers
    ]

    def sum_down():
        for copy in cols_copies:
            copy.wait_recv()
        b.mixed_ring.finish()
        b.grad_down[...] = jnp.zeros((local, block), F32)
        for slot in plane_gather(links, m, b.cols, n_dp * per):
            at = pl.ds(pl.multiple_of(slot * per, 16), per)
            for p in range(0, n_dp, 4):
                left = jnp.concatenate([b.mixed_all[p + k, at] for k in range(4)], axis=0)
                b.grad_down[...] += mm_tn(left, b.cols[slot, p * per : (p + 4) * per])
            yield

    down_sum = sum_down()

    def advance(steps):
        for _ in range(steps):
            next(down_sum, None)

    def up_ring(grads, hold, g, h):
        at_h = slice(h * chan, (h + 1) * chan)

        def part(owner):
            at = pl.ds(pl.multiple_of(owner * block, 128), block)
            return mm_tn(b.normed[:, at], grads[:, at_h])

        def keep(total):
            b.grad_up[:, g, h] = total

        return (LineSum if n_dp <= 4 else RingSum)(links, part, hold.at[h], keep, m, n_dp)

    gates = [up_ring(b.g_gate, b.ring_gate, 1, h) for h in range(heads)]
    cells = [up_ring(b.g_cell, b.ring_cell, 0, h) for h in range(heads)]

    def ticks(rings):
        for _ in range(n_dp):
            for ring in rings:
                yield ring.step()

    gate_ticks, cell_ticks = ticks(gates), ticks(cells)

    def tick(source):
        return lambda: next(source, None)

    def unmix(i, carry):
        at = pl.ds(pl.multiple_of(i * 128, 128), 128)
        gm = b.wide_f[:, at]
        g = b.gate_low[:, at].astype(F32)
        sig = sigmoid(g)
        silu = g * sig
        hat, act = b.hidden[:, at], b.act[:, at]
        group, skip = b.chan_params[5:6, at], b.chan_params[6:7, at]
        inner = hat * group + skip * act
        b.g_gate[:, at] = (gm * inner * (sig + silu * (1.0 - sig))).astype(BF)
        gi = gm * silu
        b.small[5:6, at] = jnp.sum(gi * hat, axis=0, keepdims=True)
        b.small[6:7, at] = jnp.sum(gi * act, axis=0, keepdims=True)
        b.g_act[:, at] = gi * skip
        b.wide_f[:, at] = gi * group
        return carry

    lax.fori_loop(0, local // 128, unmix, 0)
    b.mixed_ring.last_leg()
    next(gate_ticks)
    next(gate_ticks)
    columns = []
    for h in range(heads):
        u = b.wide_f[:, h * chan : (h + 1) * chan]
        columns.append(jnp.sum(u, axis=1, keepdims=True))
        columns.append(
            jnp.sum(u * b.hidden[:, h * chan : (h + 1) * chan], axis=1, keepdims=True)
        )
    u_sum = push_sum(links, m, to_lanes(columns, rows), b.u_box, m.tensor_peers, m.t, 4)
    u_moments = to_columns(u_sum())
    rhos = []
    for h in range(heads):
        at = slice(h * chan, (h + 1) * chan)
        rstd = b.head_rstd[h][:, :1]
        mean_u = u_moments[:, 2 * h : 2 * h + 1] / head_width
        sum_ux = u_moments[:, 2 * h + 1 : 2 * h + 2]
        d_hidden = rstd * (b.wide_f[:, at] - mean_u - b.hidden[:, at] * (sum_ux / head_width))
        b.d_hidden[:, at] = d_hidden.astype(BF)
        rhos.append(sum_ux * (EPSILON * rstd * rstd))
    rho = jnp.where(m.core == 0, rhos[0], rhos[1])
    links.settle([b.score_copy])
    for h in range(heads):
        for i, low, at, n in blocks:
            tile = mm_nt(
                b.d_hidden[i * LINE : (i + 1) * LINE, h * chan : (h + 1) * chan], v_of(h, low, n)
            )
            for k in range(n):
                b.score_part[h, at + k] = tile[:, k * LINE : (k + 1) * LINE]
    other = links.go(b.score_part.at[1 - m.core], b.score_in.at[0], m.sib)
    other.wait_recv()
    b.share_out[...] = (b.score_part[m.core] + b.score_in[0]).astype(BF)
    far = links.go(b.share_out, b.share_in, m.yn)
    far.wait_recv()
    b.lines[...] = jnp.zeros((8, rows), F32)
    for i, low, at, n in blocks:
        lines = slice(i * LINE, (i + 1) * LINE)
        across = slice(low * LINE, (low + n) * LINE)

        def spread(ref):
            return jnp.concatenate([ref[at + k].astype(F32) for k in range(n)], axis=1)

        inv, sign, radial = b.inv[lines][:, :1], b.sign[lines][:, :1], rho[lines]
        weight = spread(b.weight)
        full = (spread(b.share_out) + spread(b.share_in)) * inv - sign * radial * inv
        exact = jnp.where(sign == 0.0, radial, 0.0)
        noisy = jnp.sum(full * weight, axis=1, keepdims=True)
        square = jnp.sum(weight * weight, axis=1, keepdims=True)
        full = full - weight * ((noisy - exact) / jnp.where(square > 0.0, square, 1.0))
        d_score = (full * spread(b.decay)).astype(BF)
        for k in range(n):
            b.d_score[m.core, at + k] = d_score[:, k * LINE : (k + 1) * LINE]
        b.lines[0:1, across] += jnp.sum(full * weight, axis=0, keepdims=True)
        b.keep[lines] = jnp.broadcast_to(exact, (LINE, 128))
    next(gate_ticks)
    scored = links.go(b.d_score.at[m.core], b.d_score.at[m.core], m.sib)
    over_cols = b.lines[0:1]
    over_rows = b.keep[...].T[0:1]
    delta = jnp.broadcast_to(over_rows - over_cols, (8, rows))
    after = jnp.sum(delta, axis=1, keepdims=True) - prefix_lanes(delta) + delta
    forget = jnp.sum(jnp.where(line8 == head + all_heads, b.pre[...], 0.0), axis=0, keepdims=True)
    d_forget = after[:1] / (1.0 + jnp.exp(forget))
    own_lines = jnp.where(line8 == head, over_cols, 0.0) + jnp.where(
        line8 == head + all_heads, d_forget, 0.0
    )
    head_peers = [
        m.sib,
        m.xn,
        (m.z, m.sib_t, m.other_c),
    ]
    pre_sum = push_sum(links, m, own_lines, b.grad_box, head_peers, m.c * 2 + m.core, 4)

    for h in range(heads):
        at = slice(2 * local + h * chan, 2 * local + (h + 1) * chan)
        b.g_proj[:, at] = jnp.zeros((rows, chan), F32)
        for i, low, place, n in blocks:
            d_hid = b.d_hidden[i * LINE : (i + 1) * LINE, h * chan : (h + 1) * chan]
            b.g_proj[low * LINE : (low + n) * LINE, at] += mm_tn(wide(b.share, h, place, n), d_hid)
    next(gate_ticks)
    scored.wait_recv()
    for h in range(heads):
        at = slice(h * chan, (h + 1) * chan)
        k_at = slice(local + h * chan, local + (h + 1) * chan)
        b.g_proj[:, k_at] = jnp.zeros((rows, chan), F32)
        for i, low, place, n in blocks:
            tile = wide(b.d_score, h, place, n)
            b.g_proj[i * LINE : (i + 1) * LINE, at] = mm(tile, k_of(h, low, n))
            b.g_proj[low * LINE : (low + n) * LINE, k_at] += mm_tn(tile, q_of(h, i))
    pre_grad = pre_sum()
    next(gate_ticks)
    advance(1)
    pre16 = jnp.concatenate([pre_grad, jnp.zeros((8, rows), F32)], axis=0)
    high, rest = split(pre16)
    b.g_proj[...] += mm_tn(high, b.gates_w[...]) + mm_tn(rest, b.gates_w[...])
    gate_grad = (mm(high, b.qkv[...]) + mm(rest, b.qkv[...]))[:8]
    for s in range(3):
        b.low_sum[8 * s : 8 * (s + 1)] = gate_grad[:, s * local : (s + 1) * local]
    bias_grad = jnp.sum(pre_grad, axis=1, keepdims=True)
    b.small[8:16] = jnp.zeros((8, local), F32)
    b.small[8:9, :128] = to_lanes_one(bias_grad)
    advance(2)

    r_map = lax.broadcasted_iota(jnp.int32, (chan, chan), 0) // 4
    c_map = lax.broadcasted_iota(jnp.int32, (chan, chan), 1) // 4
    same = r_map == c_map
    for h in range(heads):
        at = slice(h * chan, (h + 1) * chan)
        act_low = b.act[:, at].astype(BF)
        extra = None
        for s in range(3):
            low = b.g_proj[:, s * local + h * chan : s * local + (h + 1) * chan].astype(BF)
            left = act_low if s < 2 else b.branch[:, at]
            dense = jnp.where(same, mm_tn(left, low), 0.0)
            folded = jnp.sum(dense.reshape(chan // 8, 8, chan), axis=0)
            b.low_sum[24 + 4 * s : 28 + 4 * s, at] = folded[:4] + folded[4:]
            back = mm_nt(low, b.maps[s, h])
            if s == 0:
                extra = back
            elif s == 1:
                b.g_act[:, at] += extra + back
            else:
                b.wide_f[:, at] = back

    def unconvolve(i, carry):
        at = pl.ds(pl.multiple_of(i * 128, 128), 128)
        since = lax.broadcasted_iota(jnp.int32, (rows, 128), 0) - b.begin[...]
        x = b.branch[:, at].astype(F32)
        gc = b.g_act[:, at] * b.slope[:, at]
        gb = b.wide_f[:, at] + b.chan_params[0:1, at] * gc
        b.small[0:1, at] = jnp.sum(gc * x, axis=0, keepdims=True)
        b.small[4:5, at] = jnp.sum(gc, axis=0, keepdims=True)
        for j in range(1, 4):
            kept = jnp.where(since >= j, gc, 0.0)
            gb = gb + b.chan_params[j : j + 1, at] * pltpu.roll(kept, rows - j, 0)
            b.small[j : j + 1, at] = jnp.sum(kept * pltpu.roll(x, j, 0), axis=0, keepdims=True)
        b.g_cell[:, at] = gb.astype(BF)
        return carry

    lax.fori_loop(0, local // 128, unconvolve, 0)
    next(gate_ticks)
    next(cell_ticks)
    next(cell_ticks)
    b.low_sum[36:] = jnp.zeros((12, local), F32)
    b.low_box[m.z] = b.low_sum[...].astype(BF)
    low_copies = [links.go(b.low_box.at[m.z], b.low_box.at[m.z], peer) for peer in m.dp_peers]
    advance(4)

    def up_part(y, core, x):
        slot = (y * 2 + core) * 2 + x
        if block >= wide_d:
            ratio = block // wide_d
            at = pl.ds(pl.multiple_of(lax.rem(slot, ratio) * wide_d, 16), wide_d)
            owner = lax.div(slot, ratio)
            return mm_nt(b.g_cell[...], b.up_cell[owner, at]) + mm_nt(
                b.g_gate[...], b.up_gate[owner, at]
            )
        ratio = wide_d // block
        return jnp.concatenate(
            [
                mm_nt(b.g_cell[...], b.up_cell[slot * ratio + k])
                + mm_nt(b.g_gate[...], b.up_gate[slot * ratio + k])
                for k in range(ratio)
            ],
            axis=1,
        )

    own_k = plane_scatter(
        links, m, up_part, b, rows, (lambda: advance(2), tick(gate_ticks), tick(gate_ticks))
    )
    for _ in gate_ticks:
        pass
    grad_normed = b.acc[own_k]
    x_hat = (b.x_own[...].astype(F32) - b.sums[:, :1]) * b.squares[:, :1]
    grad_scaled = grad_normed * b.gains[m.slot, :1]
    line_sum = push_sum(
        links,
        m,
        to_lanes(
            [
                jnp.sum(grad_scaled, axis=1, keepdims=True),
                jnp.sum(grad_scaled * x_hat, axis=1, keepdims=True),
            ],
            rows,
        ),
        b.line_box,
        m.plane_peers,
        m.slot,
        8,
    )
    loss_sum = push_sum(links, m, b.loss_part[...], b.loss_box, m.plane_peers, m.slot, 8)
    b.small[7:8] = jnp.zeros((1, local), F32)
    b.small[7:8, :wide_d] = jnp.sum(grad_normed * x_hat, axis=0, keepdims=True)
    b.small[9:10, :128] = loss_sum()[:1]
    b.small_box[m.z] = b.small[...]
    small_copies = [
        links.go(b.small_box.at[m.z], b.small_box.at[m.z], peer) for peer in m.dp_peers
    ]
    next(cell_ticks)
    lines = to_columns(line_sum()) / width
    grad_x = b.squares[:, :1] * (grad_scaled - lines[:, :1] - x_hat * lines[:, 1:2])
    own_grad = b.own_gradient[...].astype(F32)
    grad_slot = (own_grad + grad_x).astype(BF)
    links.settle(b.token_copies)
    b.sent_tokens[...] = mm_tn(b.recv_map[...], grad_slot).astype(BF)
    own_place = pl.ds(pl.multiple_of(m.z * cap, 16), cap)
    b.home_grad[own_place] = b.sent_tokens[own_place]
    copies = b.exchange(b.sent_tokens, b.home_grad)
    next(cell_ticks)
    for copy in b.home_copies:
        copy.wait_recv()
    b.output[...] = mm_tn(b.send_map[...], b.home_out[...]).astype(BF)
    next(cell_ticks)
    advance(3)
    for copy in small_copies + low_copies:
        copy.wait_recv()
    lows = b.low_box[0].astype(F32)
    for k in range(1, n_dp):
        lows = lows + b.low_box[k].astype(F32)
    b.low_sum[...] = lows
    total = b.small_box[0]
    for k in range(1, n_dp):
        total = total + b.small_box[k]
    b.small[...] = total
    b.loss[...] = total[9:10, :1]
    b.grad_ln[...] = total[7:8, :wide_d]
    for h in range(heads):
        at = slice(h * chan, (h + 1) * chan)
        for j in range(4):
            b.grad_conv_weight[j, h : h + 1] = b.small[j : j + 1, at]
        for j, ref in ((4, b.grad_conv_bias), (5, b.grad_group), (6, b.grad_skip)):
            ref[h : h + 1] = b.small[j : j + 1, at]
        for s in range(3):
            for i in range(4):
                k = 24 + 4 * s + i
                b.grad_qkv[s, i, h : h + 1] = b.low_sum[k : k + 1, at]
            for g in range(2 * all_heads):
                k = 8 * s + g
                b.grad_gate_weight[g // all_heads, g % all_heads, s, h : h + 1] = b.low_sum[
                    k : k + 1, at
                ]
    for g in range(2):
        b.grad_gate_bias[g : g + 1] = total[8:9, g * all_heads : (g + 1) * all_heads]
    for _ in cell_ticks:
        pass
    for copy in copies:
        copy.wait_recv()
    b.grad_input[...] = mm_tn(b.send_map[...], b.home_grad[...]).astype(BF)
    for line in [b.mixed_ring] + gates + cells:
        line.settle()


def kernel(names, shape, limit, *refs):
    b = types.SimpleNamespace(**dict(zip(names, refs)))
    m = coordinates(shape[3])
    links = Links(b.send_sem, b.recv_sem, limit)
    forward(b, m, links, shape)
    backward(b, m, links, shape)
    links.close()


def carry_out(*refs):
    *ends, sems = refs
    half = len(ends) // 2
    copies = [
        pltpu.make_async_copy(ends[k], ends[half + k], sems.at[k]) for k in range(half)
    ]
    for copy in copies:
        copy.start()
    for copy in copies:
        copy.wait()


def shards(
    tokens,
    targets,
    ln_gain,
    up_weight,
    conv_weight,
    conv_bias,
    qkv_weight,
    gate_weight,
    gate_bias,
    group_gain,
    skip_gain,
    down_weight,
    lengths,
    permutation,
    valid,
):
    rows, wide_d = tokens.shape
    n_dp = lax.axis_size("dp")
    heads, chan = up_weight.shape[2], up_weight.shape[3]
    local = heads * chan
    block = up_weight.shape[0]
    width = 8 * wide_d
    up_halves = up_weight.transpose(1, 0, 2, 3).reshape(2, block, local)
    inputs = dict(
        tokens=tokens,
        targets=targets,
        index=jnp.concatenate([permutation.reshape(n_dp, rows), valid.reshape(1, rows)]),
        own_cell=up_halves[0],
        own_gate=up_halves[1],
        own_down=down_weight.reshape(local, block),
        ln_gain=ln_gain.reshape(1, wide_d),
        conv_weight=conv_weight,
        conv_bias=conv_bias,
        qkv_weight=qkv_weight,
        gate_weight=gate_weight,
        gate_bias=gate_bias,
        group_gain=group_gain,
        skip_gain=skip_gain,
        lengths=lengths,
    )
    outputs = dict(
        output=((rows, wide_d), BF),
        loss=((1, 1), F32),
        grad_input=((rows, wide_d), BF),
        grad_ln=((1, wide_d), F32),
        grad_up=(up_weight.shape, F32),
        grad_conv_weight=(conv_weight.shape, F32),
        grad_conv_bias=(conv_bias.shape, F32),
        grad_qkv=(qkv_weight.shape, F32),
        grad_gate_weight=(gate_weight.shape, F32),
        grad_gate_bias=(gate_bias.shape, F32),
        grad_group=(group_gain.shape, F32),
        grad_skip=(skip_gain.shape, F32),
        grad_down=((local, block), F32),
    )
    n_blocks = band(rows)[1]
    half = rows // 2
    limit = 130 + 18 * n_dp
    turns = (2 if n_dp <= 4 else 1, n_dp)
    scratch = dict(
        send_map=((rows, rows), BF),
        recv_map=((rows, rows), BF),
        chan_params=((8, local), F32),
        maps8=((3, heads, 8, chan), F32),
        gates_f=((16, 3 * local), F32),
        gates_w=((16, 3 * local), BF),
        sent_tokens=((rows, wide_d), BF),
        sent_goal=((rows, wide_d), BF),
        goal_places=((rows, wide_d), BF),
        valids=((n_dp, 8, rows), F32),
        keep=((rows, 128), F32),
        full=((8, rows, wide_d), BF),
        gains=((8, 8, wide_d), F32),
        up_cell=((n_dp, block, local), BF),
        up_gate=((n_dp, block, local), BF),
        down=((n_dp, local, block), BF),
        sums=((rows, 128), F32),
        squares=((rows, 128), F32),
        x_own=((rows, wide_d), BF),
        normed=((rows, width), BF),
        wide_f=((rows, local), F32),
        begin=((rows, 128), jnp.int32),
        branch=((rows, local), BF),
        act=((rows, local), F32),
        slope=((rows, local), F32),
        maps=((3, heads, chan, chan), BF),
        qkv=((rows, 3 * local), BF),
        pre_box=((8, 8, rows), F32),
        pre=((8, rows), F32),
        score_part=((heads, n_blocks, LINE, LINE), F32),
        score_in=((2, n_blocks, LINE, LINE), F32),
        score_sum=((n_blocks, LINE, LINE), F32),
        decay=((n_blocks, LINE, LINE), F32),
        weight=((n_blocks, LINE, LINE), F32),
        share=((heads, n_blocks, LINE, LINE), BF),
        inv=((rows, 128), F32),
        sign=((rows, 128), F32),
        hidden=((rows, local), F32),
        moment_box=((4, 8, rows), F32),
        head_rstd=((heads, rows, 128), F32),
        head_mean=((heads, rows, 128), F32),
        gate_low=((rows, local), BF),
        out=((4, rows, wide_d), BF),
        into=((4, rows, wide_d), BF),
        acc=((4, rows, wide_d), F32),
        small_out=((6, half, wide_d), BF),
        small_in=((6, half, wide_d), BF),
        loss_part=((8, 128), F32),
        own_gradient=((rows, wide_d), BF),
        sent_out=((rows, wide_d), BF),
        home_out=((rows, wide_d), BF),
        home_grad=((rows, wide_d), BF),
        mixed_all=((n_dp, rows, local), BF),
        cols_out=((n_dp, rows // 8, block), BF),
        cols=((8, n_dp * rows // 8, block), BF),
        low_sum=((48, local), F32),
        low_box=((n_dp, 48, local), BF),
        ring_gate=((heads,) + turns + (block, chan), BF),
        ring_cell=((heads,) + turns + (block, chan), BF),
        g_gate=((rows, local), BF),
        g_cell=((rows, local), BF),
        small=((16, local), F32),
        small_box=((n_dp, 16, local), F32),
        g_act=((rows, local), F32),
        u_box=((4, 8, rows), F32),
        d_hidden=((rows, local), BF),
        share_out=((n_blocks, LINE, LINE), BF),
        share_in=((n_blocks, LINE, LINE), BF),
        lines=((8, rows), F32),
        d_score=((heads, n_blocks, LINE, LINE), BF),
        grad_box=((4, 8, rows), F32),
        g_proj=((rows, 3 * local), F32),
        line_box=((8, 8, rows), F32),
        loss_box=((8, 8, 128), F32),
    )
    vmem = pl.BlockSpec(memory_space=pltpu.VMEM)
    spaces = {name: pl.BlockSpec(memory_space=pl.ANY) for name in inputs if name[:4] == "own_"}
    spaces["lengths"] = pl.BlockSpec(memory_space=pltpu.SMEM)
    names = list(inputs) + list(outputs) + list(scratch) + ["send_sem", "recv_sem", "local_sem"]
    results = pl.pallas_call(
        lambda *refs: kernel(names, (rows, local, chan, n_dp, block, wide_d), limit, *refs),
        out_shape=[jax.ShapeDtypeStruct(*spec) for spec in outputs.values()],
        in_specs=[spaces.get(name, vmem) for name in inputs],
        out_specs=[vmem] * len(outputs),
        scratch_shapes=[pltpu.VMEM(*spec) for spec in scratch.values()]
        + [pltpu.SemaphoreType.DMA((limit,)), pltpu.SemaphoreType.DMA((limit,))]
        + [pltpu.SemaphoreType.DMA((3,))],
        compiler_params=pltpu.CompilerParams(
            collective_id=0, has_side_effects=True, vmem_limit_bytes=VMEM_LIMIT
        ),
    )(*inputs.values())
    results = pl.pallas_call(
        carry_out,
        out_shape=[jax.ShapeDtypeStruct(*spec) for spec in outputs.values()],
        in_specs=[pl.BlockSpec(memory_space=pl.ANY)] * len(outputs),
        out_specs=[vmem] * len(outputs),
        scratch_shapes=[pltpu.SemaphoreType.DMA((len(outputs),))],
    )(*results)
    o = types.SimpleNamespace(**dict(zip(outputs, results)))
    return (
        o.output,
        o.loss.reshape(()),
        o.grad_input,
        o.grad_ln.reshape(-1),
        o.grad_up,
        o.grad_conv_weight,
        o.grad_conv_bias,
        o.grad_qkv,
        o.grad_gate_weight,
        o.grad_gate_bias,
        o.grad_group,
        o.grad_skip,
        o.grad_down.reshape(down_weight.shape),
    )


def solution(mesh):
    return jax.shard_map(
        shards,
        mesh=mesh,
        in_specs=(
            P("dp", ("tensor", "ctx")),
            P("dp", ("tensor", "ctx")),
            P(("tensor", "ctx")),
            P("dp", None, "ctx", "tensor"),
            P(None, "ctx", "tensor"),
            P("ctx", "tensor"),
            P(None, None, "ctx", "tensor"),
            P(None, None, None, "ctx", "tensor"),
            P(),
            P("ctx", "tensor"),
            P("ctx", "tensor"),
            P("ctx", "tensor", "dp"),
            P(),
            P(),
            P("dp"),
        ),
        out_specs=(
            P("dp", ("tensor", "ctx")),
            P(),
            P("dp", ("tensor", "ctx")),
            P(("tensor", "ctx")),
            P("dp", None, "ctx", "tensor"),
            P(None, "ctx", "tensor"),
            P("ctx", "tensor"),
            P(None, None, "ctx", "tensor"),
            P(None, None, None, "ctx", "tensor"),
            P(),
            P("ctx", "tensor"),
            P("ctx", "tensor"),
            P("ctx", "tensor", "dp"),
        ),
        check_vma=False,
    )
```

time: 327 us -> 262 us (0.80)
  Pallas kernels: 291 us -> 253 us
  local copies, waits for them, and re-layouts: 26.7 us -> 5.61 us
  other arithmetic: 7.99 us -> 1.29 us
    pallas_call x1, Pallas kernels: 291 us -> 248 us  [shards(): pl.pallas_call(lambda *refs: kernel(names, (rows, local, chan, n_dp, bloc...]
    unnamed x18 -> x2, local copies, waits for them, and re-layouts: 7.54 us -> 1.76 us
    pallas_call x0 -> x1, Pallas kernels: none -> 4.72 us  [shards(): pl.pallas_call(carry_out, out_shape=[jax.ShapeDtypeStruct(*spec) for spec...]
    reshape x6 -> x2, local copies, waits for them, and re-layouts: 6.33 us -> 1.92 us  [the longest x1 1.22 us: shards(): ln_gain.reshape(1, wide_d)]
    slice x6 -> x1, local copies, waits for them, and re-layouts: 5.52 us -> 1.92 us  [shards(): up_halves[1]]
    convert_element_type x4 -> x0, other arithmetic: 3.31 us -> none  [the longest x1 1.3 us: shards(): send_map = (place[:, None] == code[None, :]).astype(BF)]
where the time goes in v3:
time: 262 us; the launch traced here: 260 us
  Pallas kernels  253 us (97%)
  local copies, waits for them, and re-layouts  5.61 us (2%)
    pallas_call x1, Pallas kernels, shards(): pl.pallas_call(lambda *refs: kernel(names, (rows, local, chan, n_dp, bloc...  248 us

profile of v3, /device:TPU:0, one launch (start us, length us, event | category | flops | bytes accessed | tf_op | source)
XLA Modules:
  0.0 260.4 jit_solution(15889401043349706898)
XLA Ops:
  0.6 1.2 reshape.55.refs_6_
  1.9 0.7 reshape.52
  2.6 1.3 pad_add_fusion.refs_2_
  3.9 1.9 fusion
  5.8 0.9 copy.29
  6.7 0.9 copy.28
  7.6 247.9 %shard_map.246 = (bf16[512,256]{1,0:T(8,128)(2,1)}, f32[1,1]{1,0:T(1,128)}, bf16[512,256]{1,0:T(8,128)(2,1)}, f32[1,256]{1,0:T(1,128)}, f32[512,2,2,256]{3,2,1,0...) custom-call(bf16[512,256]{1,0:T(8,128)(2,1)} %refs_0_.1, ...), custom_call_target="tpu_custom_call" | custom-call | tf_op jit(solution)/shard_map/pallas_call | solution.py:1333
  255.5 4.7 %shard_map.247 = (bf16[512,256]{1,0:T(8,128)(2,1)}, f32[1,1]{1,0:T(1,128)}, bf16[512,256]{1,0:T(8,128)(2,1)}, f32[1,256]{1,0:T(1,128)}, f32[512,2,2,256]{3,2,1,0...) custom-call(bf16[512,256]{1,0:T(8,128)(2,1)} %get-tuple-element.39.r, ...), custom_call_target="tpu_custom_call" | custom-call | tf_op jit(solution)/shard_map/pallas_call | solution.py:1345
